TPU v7x, 512 devices: a whole 4x4x16 slice. The times are simulated.
512 devices in a mesh: dp: 64 (over x, z_hi, y), tensor: 8 (over z_lo, core).
Axes of the slice: x: 4, y: 4, z: 16 (z_hi: 4, z_lo: 4; z = z_hi * 4 + z_lo), core: 2. Of those that a mesh axis runs over, the one named last changes fastest.
Arguments:
- trainer_token_input: bfloat16 [16384, 8192], P('dp', 'tensor'), may hold values from -6 to 6
- cotangent: bfloat16 [16384, 1024], P('dp', 'tensor'), may hold values from -6 to 6
- adapter_a: float32 [8192, 64], P('tensor'), may hold values from -0.0625 to 0.0625
- adapter_b: float32 [64, 1024], P(None, 'tensor'), may hold values from -0.75 to 0.75
- moment_a: float32 [8192, 64], P('tensor'), may hold values from -0.06 to 0.06
- second_a: float32 [8192, 64], P('tensor'), may hold values from 1e-06 to 0.0001
- moment_b: float32 [64, 1024], P(None, 'tensor'), may hold values from -0.06 to 0.06
- second_b: float32 [64, 1024], P(None, 'tensor'), may hold values from 1e-06 to 0.0001
- value_matrix: bfloat16 [8192, 1024], P(None, 'tensor'), may hold values from -0.0625 to 0.0625
- decode_states: bfloat16 [2048, 4, 8192], P('dp', None, 'tensor'), may hold values from -6 to 6
- new_keys: bfloat16 [2048, 4, 1024], P('dp', None, 'tensor'), may hold values from -6 to 6
- queries: bfloat16 [2048, 4, 8192], P('dp', None, 'tensor')
- cache_keys: bfloat16 [2048, 32, 1024], P('dp', None, 'tensor')
- cache_values: bfloat16 [2048, 32, 1024], P('dp', None, 'tensor'), may hold values from -6 to 6
- lengths: int32 [2048], P('dp'), may hold values from 1 to 32, as said below
Outputs:
- step_a: float32 [8192, 64], P('tensor')
- step_b: float32 [64, 1024], P(None, 'tensor')
- attended: bfloat16 [2048, 4, 8192], P('dp', None, 'tensor')
Inputs may be any that keep to these rules, and one draw needn't show every extreme that they name: `lengths`: the number of valid cache slots of each rollout; some rollout has all 32.
All inputs are finite; a program needn't handle non-finite values.
Results may differ from a plain program's by a relative error of at most 0.0067.
Values may be sent and summed in bfloat16 or wider, within the bound.
No kernel may reach another device: no remote copies, remote signals or barrier semaphores. Data moves between devices by JAX's collectives and lax.ppermute only.
A program may use at most 64 MiB of HBM per device.

v0:
```python
import math

import jax
import jax.numpy as jnp
from jax import lax
from jax.sharding import PartitionSpec as P

HD = 128


adapter_scale = 2.0
learn_rate = 0.001
beta_one = 0.9
beta_two = 0.999
adam_eps = 1e-08
first_fix = 1.0 - 0.9**10
second_fix = 1.0 - 0.999**10


def adam_step(grad, moment, second):
    moment_new = beta_one * moment + (1.0 - beta_one) * grad
    second_new = beta_two * second + (1.0 - beta_two) * grad * grad
    return moment_new / first_fix / (jnp.sqrt(second_new / second_fix) + adam_eps)


def attend(queries, cache_keys, cache_values, new_keys, new_values, lengths):
    rows, steps, width = queries.shape
    slots = cache_keys.shape[1]
    groups = cache_keys.shape[2] // HD
    heads = width // HD // groups
    keys = jnp.concatenate([cache_keys, new_keys], axis=1).reshape(rows, slots + steps, groups, HD)
    values = jnp.concatenate([cache_values, new_values], axis=1).reshape(
        rows, slots + steps, groups, HD
    )
    query = queries.reshape(rows, steps, groups, heads, HD)
    scores = jnp.einsum("sjgqd,skgd->sgqjk", query, keys, preferred_element_type=jnp.float32) * (
        1.0 / math.sqrt(HD)
    )
    position = jnp.arange(slots + steps, dtype=jnp.int32)
    current = jnp.arange(steps, dtype=jnp.int32)
    cache_ok = (position[None, None, :] < lengths[:, None, None]) & (
        position[None, None, :] < slots
    )
    new_ok = (position[None, None, :] >= slots) & (
        position[None, None, :] - slots <= current[None, :, None]
    )
    visible = (cache_ok | new_ok)[:, None, None, :, :]
    scores = jnp.where(visible, scores, -1e30)
    largest = jnp.max(scores, axis=-1, keepdims=True)
    expo = jnp.exp(scores - largest)
    weights = (expo / jnp.sum(expo, axis=-1, keepdims=True)).astype(jnp.bfloat16)
    out = jnp.einsum("sgqjk,skgd->sjgqd", weights, values, preferred_element_type=jnp.float32)
    return out.reshape(rows, steps, width).astype(jnp.bfloat16)


def local(
    trainer_token_input,
    cotangent,
    adapter_a,
    adapter_b,
    moment_a,
    second_a,
    moment_b,
    second_b,
    value_matrix,
    decode_states,
    new_keys,
    queries,
    cache_keys,
    cache_values,
    lengths,
):
    token_count_total = trainer_token_input.shape[0] * lax.axis_size("dp")
    a_low = adapter_a.astype(jnp.bfloat16)
    b_low = adapter_b.astype(jnp.bfloat16)
    acts_part = jnp.dot(trainer_token_input, a_low, preferred_element_type=jnp.float32)
    grads_part = jnp.dot(cotangent, b_low.T, preferred_element_type=jnp.float32)
    acts_sum, grads_sum = lax.psum((acts_part, grads_part), "tensor")
    low_rank_activations = acts_sum.astype(jnp.bfloat16)
    low_rank_gradients = grads_sum.astype(jnp.bfloat16)
    scale_factor = adapter_scale / token_count_total
    grad_b_part = (
        jnp.dot(low_rank_activations.T, cotangent, preferred_element_type=jnp.float32)
        * scale_factor
    )
    grad_a_part = (
        jnp.dot(trainer_token_input.T, low_rank_gradients, preferred_element_type=jnp.float32)
        * scale_factor
    )
    gradient_down_matrix, gradient_up_matrix = lax.psum((grad_a_part, grad_b_part), "dp")
    step_a = adam_step(gradient_down_matrix, moment_a, second_a)
    step_b = adam_step(gradient_up_matrix, moment_b, second_b)
    updated_down_matrix = (adapter_a - learn_rate * step_a).astype(jnp.bfloat16)
    updated_up_matrix = (adapter_b - learn_rate * step_b).astype(jnp.bfloat16)
    weight_change = jnp.dot(
        lax.all_gather(updated_down_matrix, "tensor", axis=0, tiled=True),
        updated_up_matrix,
        preferred_element_type=jnp.float32,
    )
    merged_weight = (value_matrix.astype(jnp.float32) + adapter_scale * weight_change).astype(
        jnp.bfloat16
    )
    rows, steps, _ = decode_states.shape
    kv_width = merged_weight.shape[1]
    piece = lax.all_gather(decode_states, "tensor", axis=2, tiled=True)
    flat = piece.reshape(rows * steps, piece.shape[2])
    projected = jnp.dot(flat, merged_weight, preferred_element_type=jnp.float32)
    new_values = projected.astype(jnp.bfloat16).reshape(rows, steps, kv_width)
    attended = attend(queries, cache_keys, cache_values, new_keys, new_values, lengths)
    return (step_a, step_b, attended)


def solution(mesh):
    return jax.shard_map(
        local,
        mesh=mesh,
        in_specs=(
            P("dp", "tensor"),
            P("dp", "tensor"),
            P("tensor", None),
            P(None, "tensor"),
            P("tensor", None),
            P("tensor", None),
            P(None, "tensor"),
            P(None, "tensor"),
            P(None, "tensor"),
            P("dp", None, "tensor"),
            P("dp", None, "tensor"),
            P("dp", None, "tensor"),
            P("dp", None, "tensor"),
            P("dp", None, "tensor"),
            P("dp"),
        ),
        out_specs=(P("tensor", None), P(None, "tensor"), P("dp", None, "tensor")),
        check_vma=False,
    )
```

profile of v0, /device:TPU:32, one launch (start us, length us, event | category | flops | bytes accessed | tf_op | source)
XLA Modules:
  0.0 1287.0 jit_solution(13756518199647896445)
XLA Ops:
  8.0 0.0 copy-start
  8.0 0.0 copy-start.1
  8.0 0.0 copy-start.3
  8.0 0.0 copy-start.4
  8.0 0.0 copy-start.5
  8.1 0.0 all-reduce.4.cloned.1.call-start
  8.1 1.0 copy-done
  9.1 1.2 fusion.20
  10.4 0.0 copy-start.2
  10.4 0.0 copy-start.10
  10.4 0.0 copy-start.11
  10.4 0.0 copy-start.12
  10.4 1.0 fusion.31
  11.4 30.2 %all-reduce.5 = (bf16[256,64]{1,0:T(8,128)(2,1)S(1)}, bf16[256,64]{1,0:T(8,128)(2,1)S(1)}) all-reduce(f32[256,64]{1,0:T(8,128)S(1)} %fusion.31, f32[256,64]{1,0:T(8,128)S(1)} %fusion.20), channel_id=1, replica_groups=mesh['dp'=64,'tensor'=8] {'tensor'}, use_global_device_ids=true, to_apply=%region_0.0 | all-reduce | flops 32768 | bytes 196608 | tf_op jit(solution)/shard_map/psum | solution.py:78
  41.6 0.9 fusion.6
  42.5 0.0 all-reduce.4.cloned.1.call-update
  42.6 0.0 all-gather.5.cloned.1.call-start
  42.6 0.5 all-gather.5.cloned.1.call-update
  43.2 0.0 copy-start.7
  43.2 0.0 copy-start.8
  43.2 0.0 all-gather.3.cloned.1.call-start
  43.2 0.0 copy-done.3
  43.2 0.1 reshape.142
  43.3 791.1 %all-reduce.4.cloned.1.call-done = f32[1024,64]{0,1:T(8,128)} async-done(((f32[1024,64]{0,1:T(8,128)}), f32[1024,64]{0,1:T(8,128)}) %all-reduce.4.cloned.1.call-update) | async-done | bytes 262160 | tf_op jit(solution)/shard_map/psum | solution.py:90
  834.5 0.0 copy-done.1
  834.5 0.0 copy-done.4
  834.5 0.0 copy-done.5
  834.5 1.9 subtract_convert_fusion
  836.4 0.0 all-gather.3.cloned.1.call-update
  836.4 0.0 copy-done.2
  836.4 0.2 convolution_multiply_fusion.3
  836.6 433.7 %psum.31 = f32[64,128]{1,0:T(8,128)S(1)} all-reduce(f32[64,128]{1,0:T(8,128)S(1)} %convolution_multiply_fusion.3), channel_id=1, replica_groups=mesh['dp'=64,'tensor'=8] {'dp'}, use_global_device_ids=true, to_apply=%region_3.0 | all-reduce | flops 8192 | bytes 65536 | tf_op jit(solution)/shard_map/psum | solution.py:90
  1270.3 0.0 copy-done.10
  1270.3 0.1 fusion.33
  1270.4 0.0 copy-done.11
  1270.4 0.0 copy-done.12
  1270.4 0.4 fusion.41
  1270.8 0.4 fusion.8
  1271.3 0.0 copy-done.7
  1271.3 0.0 copy-done.8
  1271.3 0.0 copy-start.9
  1271.3 0.0 copy-start.6
  1271.4 0.0 all-gather.5.cloned.1.call-done
  1271.4 2.5 reshape.140
  1273.9 0.0 all-gather.3.cloned.1.call-done
  1274.0 0.0 copy-done.6
  1274.0 3.4 fusion.7
  1277.4 0.0 copy-done.9
  1277.4 1.4 fusion.5
  1278.8 0.8 convert_element_type.59
  (6 shorter events, 0.1 us)
Async XLA Ops:
  8.0 1.1 copy-start
  8.0 826.4 %copy-start.1 = (f32[1024,64]{0,1:T(8,128)S(1)}, f32[1024,64]{0,1:T(8,128)}, u32[]{:S(2)}) copy-start(f32[1024,64]{0,1:T(8,128)} %param.17) | copy-start | bytes 786436
  8.0 35.2 %copy-start.3 = (bf16[32,4,1024]{2,1,0:T(4,128)(2,1)S(1)}, bf16[32,4,1024]{2,1,0:T(4,128)(2,1)}, u32[]{:S(2)}) copy-start(bf16[32,4,1024]{2,1,0:T(4,128)(2,1)} %param.26) | copy-start | bytes 786436
  8.0 826.4 %copy-start.4 = (f32[1024,64]{0,1:T(8,128)S(1)}, f32[1024,64]{0,1:T(8,128)}, u32[]{:S(2)}) copy-start(f32[1024,64]{0,1:T(8,128)} %param.20) | copy-start | bytes 786436
  8.0 826.4 %copy-start.5 = (f32[1024,64]{0,1:T(8,128)S(1)}, f32[1024,64]{0,1:T(8,128)}, u32[]{:S(2)}) copy-start(f32[1024,64]{0,1:T(8,128)} %param.19) | copy-start | bytes 786436
  8.1 826.4 %all-reduce.4.cloned.1.call-start = ((), (), s32[]{:S(2)}) async-start(), calls=%async_computation | async-start | bytes 524288 | tf_op jit(solution)/shard_map/psum | solution.py:90
  10.4 826.0 %copy-start.2 = (bf16[256,128]{1,0:T(8,128)(2,1)S(1)}, bf16[256,128]{1,0:T(8,128)(2,1)}, u32[]{:S(2)}) copy-start(bf16[256,128]{1,0:T(8,128)(2,1)} %param.16) | copy-start | bytes 196612
  10.4 1259.9 %copy-start.10 = (s32[32]{0:T(128)S(1)}, s32[32]{0:T(128)}, u32[]{:S(2)}) copy-start(s32[32]{0:T(128)} %param.29) | copy-start | bytes 388
  10.4 1260.0 %copy-start.11 = (bf16[32,32,128]{2,1,0:T(8,128)(2,1)S(1)}, bf16[32,32,128]{2,1,0:T(8,128)(2,1)}, u32[]{:S(2)}) copy-start(bf16[32,32,128]{2,1,0:T(8,128)(2,1)} %param.27) | copy-start | bytes 786436
  10.4 1260.0 %copy-start.12 = (bf16[32,4,128]{2,1,0:T(4,128)(2,1)S(1)}, bf16[32,4,128]{2,1,0:T(4,128)(2,1)}, u32[]{:S(2)}) copy-start(bf16[32,4,128]{2,1,0:T(4,128)(2,1)} %param.25) | copy-start | bytes 98308
  42.6 1228.8 %all-gather.5.cloned.1.call-start = ((), (), s32[]{:S(2)}) async-start(), calls=%async_computation.2 | async-start | bytes 2359296 | tf_op jit(solution)/shard_map/all_gather | solution.py:105
  43.2 1228.1 %copy-start.7 = (f32[64,128]{1,0:T(8,128)S(1)}, f32[64,128]{1,0:T(8,128)}, u32[]{:S(2)}) copy-start(f32[64,128]{1,0:T(8,128)} %param.22) | copy-start | bytes 98308
  43.2 1228.1 %copy-start.8 = (f32[64,128]{1,0:T(8,128)S(1)}, f32[64,128]{1,0:T(8,128)}, u32[]{:S(2)}) copy-start(f32[64,128]{1,0:T(8,128)} %param.21) | copy-start | bytes 98308
  43.2 1230.8 %all-gather.3.cloned.1.call-start = ((), (), s32[]{:S(2)}) async-start(), calls=%async_computation.1 | async-start | bytes 1179648 | tf_op jit(solution)/shard_map/all_gather | solution.py:96
  1271.3 6.1 copy-start.9
  1271.3 2.6 copy-start.6
Sparse Core Ops, SparseCore 0:
  42.7 791.7 all-reduce.3
Sparse Core Ops, SparseCore 1:
  45.3 46.3 all-gather.4
  836.5 30.7 all-gather.2
where the time goes:
time: 1290 us
  waiting for transfers between devices  792 us (61%)
  blocking collectives  464 us (36%)
  between operations  15.7 us (1%)
    psum x1, waiting for transfers between devices, local(): lax.psum((grad_a_part, grad_b_part), 'dp')  791 us
    psum x1, blocking collectives, local(): lax.psum((grad_a_part, grad_b_part), 'dp')  434 us
    psum x1, blocking collectives, local(): acts_sum, grads_sum = lax.psum((acts_part, grads_part), 'tensor')  30.2 us
  transfers between devices with their start and end apart: 3, of which 1 were waited for; matrix products, arithmetic and copies ran while one was open for 0% of the time, Pallas kernels for 0%

commit v1 on v0

v1 whole, which is shorter than its diff:
```python
import math

import jax
import jax.numpy as jnp
from jax import lax
from jax.sharding import Mesh, PartitionSpec as P

HD = 128


adapter_scale = 2.0
learn_rate = 0.001
beta_one = 0.9
beta_two = 0.999
adam_eps = 1e-08
first_fix = 1.0 - 0.9**10
second_fix = 1.0 - 0.999**10

DP = ("x", "zh", "y")
PLANE = ("x", "y")
BF = jnp.bfloat16
F32 = jnp.float32


def adam_step(grad, moment, second):
    moment_new = beta_one * moment + (1.0 - beta_one) * grad
    second_new = beta_two * second + (1.0 - beta_two) * grad * grad
    return moment_new / first_fix / (jnp.sqrt(second_new / second_fix) + adam_eps)


def scatter(parts, axes):
    return lax.all_to_all(parts, axes, 0, 0, tiled=True)


def spread(value, axes):
    count = lax.axis_size(axes)
    return scatter(jnp.broadcast_to(value[None], (count,) + value.shape), axes)


def pack(rows):
    half = rows.shape[0] // 2
    return jnp.concatenate([rows[:half], rows[half:]], axis=1)


def unpack(packed):
    half = packed.shape[1] // 2
    return jnp.concatenate([packed[:, :half], packed[:, half:]], axis=0)


def local(
    trainer_token_input,
    cotangent,
    adapter_a,
    adapter_b,
    moment_a,
    second_a,
    moment_b,
    second_b,
    value_matrix,
    decode_states,
    new_keys,
    queries,
    cache_keys,
    cache_values,
    lengths,
):
    tensor = lax.axis_size("tensor")
    plane = lax.axis_size(PLANE)
    tokens, width = trainer_token_input.shape
    rank = adapter_a.shape[1]
    kv = cotangent.shape[1]
    rows, steps, _ = decode_states.shape
    count = rows * steps
    flat = decode_states.reshape(count, width)
    gathered = lax.all_gather(flat, "tensor", axis=0, tiled=False)

    acts_part = jnp.dot(trainer_token_input, adapter_a.astype(BF), preferred_element_type=F32)
    grads_part = jnp.dot(cotangent, adapter_b.astype(BF).T, preferred_element_type=F32)
    both = jnp.concatenate([acts_part, grads_part], axis=1).astype(BF)
    share = scatter(both.reshape(tensor, tokens // tensor, 2 * rank), "tensor")
    share = jnp.sum(share.astype(F32), axis=0).astype(BF)
    low = spread(share, "tensor").reshape(tokens, 2 * rank)
    acts, grads = low[:, :rank], low[:, rank:]

    scale_factor = adapter_scale / (tokens * lax.axis_size(DP))
    half = width // 2
    blank = jnp.zeros_like(grads)
    grad_a = jnp.dot(
        trainer_token_input[:, :half].T, jnp.concatenate([grads, blank], 1), preferred_element_type=F32
    ) + jnp.dot(
        trainer_token_input[:, half:].T, jnp.concatenate([blank, grads], 1), preferred_element_type=F32
    )
    grad_b = jnp.dot(acts.T, cotangent, preferred_element_type=F32)
    rows_a, rows_b = half // plane, rank // plane
    block = jnp.concatenate(
        [
            grad_a.reshape(plane, rows_a, 2 * rank),
            grad_b.reshape(plane, rows_b, kv),
            jnp.zeros((plane, -(rows_a + rows_b) % 8, kv), F32),
        ],
        axis=1,
    )
    shard = scatter((block * scale_factor).astype(BF), PLANE)
    shard = jnp.sum(shard.astype(F32), axis=0).astype(BF)
    shard = jnp.sum(spread(shard, ("zh",)).astype(F32), axis=0)

    place = lax.axis_index(PLANE)

    def piece_a(whole):
        low_rows = lax.dynamic_slice_in_dim(whole, place * rows_a, rows_a, 0)
        high_rows = lax.dynamic_slice_in_dim(whole, half + place * rows_a, rows_a, 0)
        return jnp.concatenate([low_rows, high_rows], axis=1)

    def piece_b(whole):
        return lax.dynamic_slice_in_dim(whole, place * rows_b, rows_b, 0)

    pad = jnp.ones((-(rows_a + rows_b) % 8, kv), F32)

    def piece(of_a, of_b):
        return jnp.concatenate([piece_a(of_a), piece_b(of_b), pad], axis=0)

    step = adam_step(shard, piece(moment_a, moment_b), piece(second_a, second_b)).astype(BF)
    every = spread(step, PLANE).astype(F32)
    step_a_packed = every[:, :rows_a].reshape(half, 2 * rank)
    step_b = every[:, rows_a : rows_a + rows_b].reshape(rank, kv)
    step_a = unpack(step_a_packed)
    new_a = (pack(adapter_a) - learn_rate * step_a_packed).astype(BF)
    new_b = (adapter_b - learn_rate * step_b).astype(BF)

    left = jnp.dot(flat[:, :half], new_a, preferred_element_type=F32)
    right = jnp.dot(flat[:, half:], new_a, preferred_element_type=F32)
    lane = lax.broadcasted_iota(jnp.int32, left.shape, 1)
    inner = jnp.where(lane < rank, left, right).astype(BF)
    inner = jnp.sum(spread(inner, "tensor").astype(F32), axis=0).astype(BF)
    twice = jnp.concatenate([new_b, new_b], axis=0)
    change = jnp.dot(inner, twice, preferred_element_type=F32)
    base = jnp.einsum(
        "tnd,tdk->nk", gathered, value_matrix.reshape(tensor, width, kv), preferred_element_type=F32
    )
    new_values = (base + adapter_scale * change).astype(BF)

    heads = queries.shape[2] // HD
    slots = cache_keys.shape[1]
    query = queries.reshape(rows, steps, heads, HD)
    keys = jnp.concatenate([cache_keys, new_keys], axis=1)
    scores = jnp.einsum("sjqd,skd->sqjk", query, keys, preferred_element_type=F32) * (
        1.0 / math.sqrt(HD)
    )
    position = jnp.arange(slots + steps, dtype=jnp.int32)
    current = jnp.arange(steps, dtype=jnp.int32)
    cache_ok = (position[None, None, :] < lengths[:, None, None]) & (position[None, None, :] < slots)
    new_ok = (position[None, None, :] >= slots) & (
        position[None, None, :] - slots <= current[None, :, None]
    )
    visible = (cache_ok | new_ok)[:, None, :, :]
    scores = jnp.where(visible, scores, -1e30)
    largest = jnp.max(scores, axis=-1, keepdims=True)
    expo = jnp.exp(scores - largest)
    weights = (expo / jnp.sum(expo, axis=-1, keepdims=True)).astype(BF)
    values = jnp.concatenate([cache_values, new_values.reshape(rows, steps, kv)], axis=1)
    out = jnp.einsum("sqjk,skd->sjqd", weights, values, preferred_element_type=F32)
    attended = out.reshape(rows, steps, heads * HD).astype(BF)
    return (step_a, step_b, attended)


def solution(mesh):
    fine = Mesh(mesh.devices.reshape(4, 4, 4, mesh.devices.shape[1]), DP + ("tensor",))
    return jax.shard_map(
        local,
        mesh=fine,
        in_specs=(
            P(DP, "tensor"),
            P(DP, "tensor"),
            P("tensor", None),
            P(None, "tensor"),
            P("tensor", None),
            P("tensor", None),
            P(None, "tensor"),
            P(None, "tensor"),
            P(None, "tensor"),
            P(DP, None, "tensor"),
            P(DP, None, "tensor"),
            P(DP, None, "tensor"),
            P(DP, None, "tensor"),
            P(DP, None, "tensor"),
            P(DP),
        ),
        out_specs=(P("tensor", None), P(None, "tensor"), P(DP, None, "tensor")),
        check_vma=False,
    )
```

time: 1290 us -> 116 us (0.09)
  the two profiles are of different devices: /device:TPU:32 before, /device:TPU:1 now
where the time goes in v1:
time: 116 us; the launch traced here: 115 us
  starting transfers between devices  42.5 us (37%)
  waiting for transfers between devices  34.9 us (30%)
  between operations  14.5 us (12%)
  local copies, waits for them, and re-layouts  11 us (9%)
  matrix products  10.2 us (9%)
  other arithmetic  2.01 us (2%)
    all_to_all x6, starting transfers between devices, scatter(): return lax.all_to_all(parts, axes, 0, 0, tiled=True)  42.5 us
    all_to_all x6, waiting for transfers between devices, scatter(): return lax.all_to_all(parts, axes, 0, 0, tiled=True)  34.9 us
    broadcast_in_dim x4, local copies, waits for them, and re-layouts, spread(): return scatter(jnp.broadcast_to(value[None], (count,) + value.shape), axes)  2.69 us
    dot_general x1, matrix products, local(): jnp.einsum('tnd,tdk->nk', gathered, value_matrix.reshape(tensor, width, k...  2.36 us
  transfers between devices with their start and end apart: 7, of which 6 were waited for; matrix products, arithmetic and copies ran while one was open for 13% of the time, Pallas kernels for 0%

profile of v1, /device:TPU:1, one launch (start us, length us, event | category | flops | bytes accessed | tf_op | source)
XLA Modules:
  0.0 115.1 jit_solution(16595996996264177893)
XLA Ops:
  7.2 0.0 copy-start
  7.2 1.5 %convolution_convert_fusion.2 = bf16[256,64]{0,1:T(8,128)(2,1)S(1)} fusion(bf16[256,1024]{1,0:T(8,128)(2,1)} %param.15, f32[1024,64]{0,1:T(8,128)} %param.17), kind=kOutput, calls=%fused_computation.17 | convolution fusion | flops 33636352 | bytes 819200 | tf_op jit(solution)/shard_map/dot_general | solution.py:77
  8.8 0.1 copy.47
  8.9 1.0 convolution_convert_fusion.1
  9.9 0.1 copy.48
  10.0 0.7 pad_maximum_fusion.1
  10.7 10.1 %all-to-all-start = ((bf16[8,32,128]{2,1,0:T(8,128)(2,1)}), bf16[8,32,128]{2,1,0:T(8,128)(2,1)S(1)}, u32[]{:S(2)}, u32[]{:S(2)}) async-start(bf16[8,32,128]{2,1,0:T(8,128)(2,1)} %pad_maximum_fusion.1), calls=%async_computation | async-start | bytes 131072 | tf_op jit(solution)/shard_map/all_to_all | solution.py:32
  20.9 0.0 all-gather.2.cloned.1.call-start
  20.9 1.7 %all_gather_reshape.3 = bf16[1,128,1024]{2,1,0:T(8,128)(2,1)} reshape(bf16[32,4,1024]{2,1,0:T(4,128)(2,1)} %param.24) | data formatting | bytes 524288 | tf_op jit(solution)/shard_map/all_gather;reshape | solution.py:75
  22.6 0.0 all-gather.2.cloned.1.call-update
  22.6 0.1 pad.18.clone
  22.7 0.1 fusion.41
  22.8 3.2 %all-to-all-done = bf16[8,32,128]{2,1,0:T(8,128)(2,1)S(1)} async-done(((bf16[8,32,128]{2,1,0:T(8,128)(2,1)}), bf16[8,32,128]{2,1,0:T(8,128)(2,1)S(1)}, u32[]{:S(2)}, u32[]{:S(2)}) %all-to-all-start) | async-done | bytes 65568 | tf_op jit(solution)/shard_map/all_to_all | solution.py:32
  26.0 0.6 broadcast_in_dim.21
  26.6 4.1 %all-to-all-start.1 = ((bf16[8,32,128]{2,1,0:T(8,128)(2,1)}), bf16[8,32,128]{2,1,0:T(8,128)(2,1)S(1)}, u32[]{:S(2)}, u32[]{:S(2)}) async-start(bf16[8,32,128]{2,1,0:T(8,128)(2,1)} %broadcast_in_dim.21), calls=%async_computation.1 | async-start | bytes 131072 | tf_op jit(solution)/shard_map/all_to_all | solution.py:32
  30.7 0.0 copy-done.2
  30.8 5.1 %all-to-all-done.1 = bf16[8,32,128]{2,1,0:T(8,128)(2,1)S(1)} async-done(((bf16[8,32,128]{2,1,0:T(8,128)(2,1)}), bf16[8,32,128]{2,1,0:T(8,128)(2,1)S(1)}, u32[]{:S(2)}, u32[]{:S(2)}) %all-to-all-start.1) | async-done | bytes 65568 | tf_op jit(solution)/shard_map/all_to_all | solution.py:32
  35.8 0.1 slice.48
  35.9 0.0 copy-start.3
  35.9 0.2 fusion.19
  36.2 0.3 fusion.6
  36.5 0.1 copy.49
  36.6 0.2 fusion.25
  36.8 0.8 fusion.11
  37.5 4.0 %all-to-all-start.2 = ((bf16[16,40,128]{2,1,0:T(8,128)(2,1)}), bf16[16,40,128]{2,1,0:T(8,128)(2,1)S(1)}, u32[]{:S(2)}, u32[]{:S(2)}) async-start(bf16[16,40,128]{2,1,0:T(8,128)(2,1)} %fusion.11), calls=%async_computation.2 | async-start | bytes 327680 | tf_op jit(solution)/shard_map/all_to_all | solution.py:32
  41.6 0.9 constant_dynamic-slice_fusion.2
  42.5 5.9 %all-to-all-done.2 = bf16[16,40,128]{2,1,0:T(8,128)(2,1)S(1)} async-done(((bf16[16,40,128]{2,1,0:T(8,128)(2,1)}), bf16[16,40,128]{2,1,0:T(8,128)(2,1)S(1)}, u32[]{:S(2)}, u32[]{:S(2)}) %all-to-all-start.2) | async-done | bytes 163872 | tf_op jit(solution)/shard_map/all_to_all | solution.py:32
  48.4 0.6 broadcast_in_dim.23
  49.1 12.2 %all-to-all-start.3 = ((bf16[4,40,128]{2,1,0:T(8,128)(2,1)}), bf16[4,40,128]{2,1,0:T(8,128)(2,1)S(1)}, u32[]{:S(2)}, u32[]{:S(2)}) async-start(bf16[4,40,128]{2,1,0:T(8,128)(2,1)} %broadcast_in_dim.23), calls=%async_computation.3 | async-start | bytes 81920 | tf_op jit(solution)/shard_map/all_to_all | solution.py:32
  61.2 0.1 copy.58
  61.3 0.1 copy.59
  61.4 0.1 copy.60
  61.5 0.1 copy.61
  61.6 0.1 pad.24.clone
  61.6 0.7 constant_dynamic-slice_fusion
  62.3 10.7 %all-to-all-done.3 = bf16[4,40,128]{2,1,0:T(8,128)(2,1)S(1)} async-done(((bf16[4,40,128]{2,1,0:T(8,128)(2,1)}), bf16[4,40,128]{2,1,0:T(8,128)(2,1)S(1)}, u32[]{:S(2)}, u32[]{:S(2)}) %all-to-all-start.3) | async-done | bytes 40992 | tf_op jit(solution)/shard_map/all_to_all | solution.py:32
  73.0 0.1 fusion.39
  73.1 0.7 broadcast_in_dim.24
  73.8 4.0 %all-to-all-start.4 = ((bf16[16,40,128]{2,1,0:T(8,128)(2,1)}), bf16[16,40,128]{2,1,0:T(8,128)(2,1)S(1)}, u32[]{:S(2)}, u32[]{:S(2)}) async-start(bf16[16,40,128]{2,1,0:T(8,128)(2,1)} %broadcast_in_dim.24), calls=%async_computation.4 | async-start | bytes 327680 | tf_op jit(solution)/shard_map/all_to_all | solution.py:32
  77.9 0.1 reshape.197
  77.9 0.0 copy-start.11
  78.0 0.1 copy.62
  78.1 0.1 copy.63
  78.2 1.8 %reshape.199 = bf16[32,4,8,128]{3,2,1,0:T(8,128)(2,1)} reshape(bf16[32,4,1024]{2,1,0:T(4,128)(2,1)} %param.26) | data formatting | bytes 524288 | tf_op jit(solution)/shard_map/reshape | solution.py:144
  80.0 4.7 %all-to-all-done.4 = bf16[16,40,128]{2,1,0:T(8,128)(2,1)S(1)} async-done(((bf16[16,40,128]{2,1,0:T(8,128)(2,1)}), bf16[16,40,128]{2,1,0:T(8,128)(2,1)S(1)}, u32[]{:S(2)}, u32[]{:S(2)}) %all-to-all-start.4) | async-done | bytes 163872 | tf_op jit(solution)/shard_map/all_to_all | solution.py:32
  84.7 0.1 fusion.16
  84.8 0.2 fusion.22
  85.0 0.2 fusion.10
  85.3 0.1 copy.54
  85.4 0.7 broadcast_in_dim.25
  86.1 8.1 %all-to-all-start.5 = ((bf16[8,128,128]{2,1,0:T(8,128)(2,1)}), bf16[8,128,128]{2,1,0:T(8,128)(2,1)S(1)}, u32[]{:S(2)}, u32[]{:S(2)}) async-start(bf16[8,128,128]{2,1,0:T(8,128)(2,1)} %broadcast_in_dim.25), calls=%async_computation.5 | async-start | bytes 524288 | tf_op jit(solution)/shard_map/all_to_all | solution.py:32
  94.2 0.0 copy-done.11
  94.2 0.0 copy-start.7
  94.2 2.2 %fusion.62 = f32[32,8,4]{1,2,0:T(4,128)} fusion(bf16[32,4,8,128]{3,2,1,0:T(8,128)(2,1)} %reshape.199, bf16[32,4,128]{2,1,0:T(4,128)(2,1)S(1)} %copy-done.11, bf16[32,32,128]{2,1,0:T(8,128)(2,1)} %param.27, pred[32,4,36]{2,1,0:T(4,128)(4,1)S(1)} %broadcast_or_fusion), kind=kOutput, calls=%fused_computation.90 | convolution fusion | flops 10174499 | bytes 565760 | tf_op jit(solution)/shard_map/sub | solution.py:158
  96.4 0.1 fusion.61
  96.6 0.9 copy.55
  97.6 5.4 %all-to-all-done.5 = bf16[8,128,128]{2,1,0:T(8,128)(2,1)S(1)} async-done(((bf16[8,128,128]{2,1,0:T(8,128)(2,1)}), bf16[8,128,128]{2,1,0:T(8,128)(2,1)S(1)}, u32[]{:S(2)}, u32[]{:S(2)}) %all-to-all-start.5) | async-done | bytes 262176 | tf_op jit(solution)/shard_map/all_to_all | solution.py:32
  103.0 0.0 all-gather.2.cloned.1.call-done
  103.0 0.0 copy-start.9
  103.0 0.0 copy-start.10
  103.0 2.4 %convolution_bitcast_fusion = f32[128,128]{1,0:T(8,128)S(1)} fusion(bf16[8,128,1024]{2,1,0:T(8,128)(2,1)} %all-gather.2.cloned.1.call-done, bf16[8,1024,128]{2,1,0:T(8,128)(2,1)S(1)} %bitcast.64), kind=kOutput, calls=%fused_computation.13 | convolution fusion | flops 268435456 | bytes 4259840 | tf_op jit(solution)/shard_map/tnd,tdk->nk/dot_general | solution.py:137
  105.4 0.1 fusion.9
  105.6 1.8 %fusion.5 = bf16[32,4,8,128]{3,2,1,0:T(8,128)(2,1)S(1)} fusion(bf16[32,4,128]{2,1,0:T(4,128)(2,1)S(1)} %bitcast.74, bf16[32,32,128]{2,1,0:T(8,128)(2,1)S(1)} %copy-done.9, f32[32,8,4]{1,2,0:T(4,128)S(1)} %copy-done.12, bf16[32,4,8,128]{3,2,1,0:T(8,128)(2,1)S(1)} %copy-done.4, bf16[32,4,128]{2,1,0:T(4,128)(2,1)S(1)} %copy-done.11, ...), kind=kOutput, calls=%fused_computation.7 | convolution fusion | flops 20370468 | bytes 1122816 | tf_op jit(solution)/shard_map/sqjk,skd->sjqd/dot_general | solution.py:161
  107.4 0.8 convert_element_type.71
  (35 shorter events, 0.3 us)
Async XLA Ops:
  7.2 95.8 %copy-start = (bf16[8192,128]{1,0:T(8,128)(2,1)S(1)}, bf16[8192,128]{1,0:T(8,128)(2,1)}, u32[]{:S(2)}) copy-start(bf16[8192,128]{1,0:T(8,128)(2,1)} %param.23) | copy-start | bytes 6291460
  7.2 28.7 %copy-start.1 = (bf16[256,1024]{1,0:T(8,128)(2,1)S(1)}, bf16[256,1024]{1,0:T(8,128)(2,1)}, u32[]{:S(2)}) copy-start(bf16[256,1024]{1,0:T(8,128)(2,1)} %param.15) | copy-start | bytes 1572868
  7.2 23.5 %copy-start.2 = (f32[1024,64]{0,1:T(8,128)S(1)}, f32[1024,64]{0,1:T(8,128)}, u32[]{:S(2)}) copy-start(f32[1024,64]{0,1:T(8,128)} %param.17) | copy-start | bytes 786436
  7.2 15.5 %copy-start.8 = (s32[32]{0:T(128)S(1)}, s32[32]{0:T(128)}, u32[]{:S(2)}) copy-start(s32[32]{0:T(128)} %param.29) | copy-start | bytes 388
  9.9 26.7 %copy-start.5 = (bf16[256,128]{1,0:T(8,128)(2,1)S(1)}, bf16[256,128]{1,0:T(8,128)(2,1)}, u32[]{:S(2)}) copy-start(bf16[256,128]{1,0:T(8,128)(2,1)} %param.16) | copy-start | bytes 196612
  10.7 15.2 %all-to-all-start = ((bf16[8,32,128]{2,1,0:T(8,128)(2,1)}), bf16[8,32,128]{2,1,0:T(8,128)(2,1)S(1)}, u32[]{:S(2)}, u32[]{:S(2)}) async-start(bf16[8,32,128]{2,1,0:T(8,128)(2,1)} %pad_maximum_fusion.1), calls=%async_computation | async-start | bytes 131072 | tf_op jit(solution)/shard_map/all_to_all | solution.py:32
  20.9 82.1 %all-gather.2.cloned.1.call-start = ((), (), s32[]{:S(2)}) async-start(), calls=%async_computation.6 | async-start | bytes 2359296 | tf_op jit(solution)/shard_map/all_gather | solution.py:75
  26.6 9.2 %all-to-all-start.1 = ((bf16[8,32,128]{2,1,0:T(8,128)(2,1)}), bf16[8,32,128]{2,1,0:T(8,128)(2,1)S(1)}, u32[]{:S(2)}, u32[]{:S(2)}) async-start(bf16[8,32,128]{2,1,0:T(8,128)(2,1)} %broadcast_in_dim.21), calls=%async_computation.1 | async-start | bytes 131072 | tf_op jit(solution)/shard_map/all_to_all | solution.py:32
  35.9 41.9 %copy-start.3 = (bf16[32,4,1024]{2,1,0:T(4,128)(2,1)S(1)}, bf16[32,4,1024]{2,1,0:T(4,128)(2,1)}, u32[]{:S(2)}) copy-start(bf16[32,4,1024]{2,1,0:T(4,128)(2,1)} %param.24) | copy-start | bytes 786436
  37.5 10.9 %all-to-all-start.2 = ((bf16[16,40,128]{2,1,0:T(8,128)(2,1)}), bf16[16,40,128]{2,1,0:T(8,128)(2,1)S(1)}, u32[]{:S(2)}, u32[]{:S(2)}) async-start(bf16[16,40,128]{2,1,0:T(8,128)(2,1)} %fusion.11), calls=%async_computation.2 | async-start | bytes 327680 | tf_op jit(solution)/shard_map/all_to_all | solution.py:32
  49.1 23.9 %all-to-all-start.3 = ((bf16[4,40,128]{2,1,0:T(8,128)(2,1)}), bf16[4,40,128]{2,1,0:T(8,128)(2,1)S(1)}, u32[]{:S(2)}, u32[]{:S(2)}) async-start(bf16[4,40,128]{2,1,0:T(8,128)(2,1)} %broadcast_in_dim.23), calls=%async_computation.3 | async-start | bytes 81920 | tf_op jit(solution)/shard_map/all_to_all | solution.py:32
  73.8 10.8 %all-to-all-start.4 = ((bf16[16,40,128]{2,1,0:T(8,128)(2,1)}), bf16[16,40,128]{2,1,0:T(8,128)(2,1)S(1)}, u32[]{:S(2)}, u32[]{:S(2)}) async-start(bf16[16,40,128]{2,1,0:T(8,128)(2,1)} %broadcast_in_dim.24), calls=%async_computation.4 | async-start | bytes 327680 | tf_op jit(solution)/shard_map/all_to_all | solution.py:32
  77.9 16.3 %copy-start.11 = (bf16[32,4,128]{2,1,0:T(4,128)(2,1)S(1)}, bf16[32,4,128]{2,1,0:T(4,128)(2,1)}, u32[]{:S(2)}) copy-start(bf16[32,4,128]{2,1,0:T(4,128)(2,1)} %param.25) | copy-start | bytes 98308
  86.1 16.8 %all-to-all-start.5 = ((bf16[8,128,128]{2,1,0:T(8,128)(2,1)}), bf16[8,128,128]{2,1,0:T(8,128)(2,1)S(1)}, u32[]{:S(2)}, u32[]{:S(2)}) async-start(bf16[8,128,128]{2,1,0:T(8,128)(2,1)} %broadcast_in_dim.25), calls=%async_computation.5 | async-start | bytes 524288 | tf_op jit(solution)/shard_map/all_to_all | solution.py:32
  94.2 3.3 %copy-start.7 = (f32[64,128]{1,0:T(8,128)S(1)}, f32[64,128]{1,0:T(8,128)}, u32[]{:S(2)}) copy-start(f32[64,128]{1,0:T(8,128)} %param.18) | copy-start | bytes 98308
  97.5 7.9 %copy-start.6 = (f32[16,4,128]{2,1,0:T(4,128)}, f32[16,4,128]{2,1,0:T(4,128)S(1)}, u32[]{:S(2)}) copy-start(f32[16,4,128]{2,1,0:T(4,128)S(1)} %slice.53) | copy-start | bytes 98308
  103.0 2.6 %copy-start.4 = (bf16[32,4,8,128]{3,2,1,0:T(8,128)(2,1)S(1)}, bf16[32,4,8,128]{3,2,1,0:T(8,128)(2,1)}, u32[]{:S(2)}) copy-start(bf16[32,4,8,128]{3,2,1,0:T(8,128)(2,1)} %reshape.199) | copy-start | bytes 786436
  103.0 2.6 %copy-start.9 = (bf16[32,32,128]{2,1,0:T(8,128)(2,1)S(1)}, bf16[32,32,128]{2,1,0:T(8,128)(2,1)}, u32[]{:S(2)}) copy-start(bf16[32,32,128]{2,1,0:T(8,128)(2,1)} %param.28) | copy-start | bytes 786436
  103.0 2.6 %copy-start.10 = (bf16[32,32,128]{2,1,0:T(8,128)(2,1)S(1)}, bf16[32,32,128]{2,1,0:T(8,128)(2,1)}, u32[]{:S(2)}) copy-start(bf16[32,32,128]{2,1,0:T(8,128)(2,1)} %param.27) | copy-start | bytes 786436
  103.0 2.6 %copy-start.12 = (f32[32,8,4]{1,2,0:T(4,128)S(1)}, f32[32,8,4]{1,2,0:T(4,128)}, u32[]{:S(2)}) copy-start(f32[32,8,4]{1,2,0:T(4,128)} %fusion.62) | copy-start | bytes 12292
Sparse Core Ops, SparseCore 0:
  24.3 41.9 all-gather.1

commit v2 on v0

v2 whole, which is shorter than its diff:
```python
import math

import jax
import jax.numpy as jnp
from jax import lax
from jax.experimental import pallas as pl
from jax.experimental.pallas import tpu as pltpu
from jax.sharding import Mesh, PartitionSpec as P

HD = 128


adapter_scale = 2.0
learn_rate = 0.001
beta_one = 0.9
beta_two = 0.999
adam_eps = 1e-08
first_fix = 1.0 - 0.9**10
second_fix = 1.0 - 0.999**10

DP = ("x", "zh", "y")
PLANE = ("x", "y")
TENSOR = ("zl", "core")
BF = jnp.bfloat16
F32 = jnp.float32


def adam_step(grad, moment, second):
    moment_new = beta_one * moment + (1.0 - beta_one) * grad
    second_new = beta_two * second + (1.0 - beta_two) * grad * grad
    return moment_new / first_fix / (jnp.sqrt(second_new / second_fix) + adam_eps)


def trade(parts, axes):
    return lax.all_to_all(parts, axes, 0, 0, tiled=True)


def swap(value):
    return lax.ppermute(value, "core", [(0, 1), (1, 0)])


def call(body, out, *args, flops=0, moved=0, **more):
    return pl.pallas_call(
        body,
        out_shape=out,
        cost_estimate=pl.CostEstimate(flops=flops, bytes_accessed=moved, transcendentals=0),
        compiler_params=pltpu.CompilerParams(vmem_limit_bytes=32 * 2**20),
        **more,
    )(*args)


def shape(dims, kind):
    return jax.ShapeDtypeStruct(dims, kind)


def columns_dot(a, b):
    return lax.dot_general(a, b, (((0,), (0,)), ((), ())), preferred_element_type=F32)


def rows_dot(a, b):
    return lax.dot_general(a, b, (((1,), (1,)), ((), ())), preferred_element_type=F32)


def turn(value):
    half = value.shape[1] // 2
    return jnp.concatenate([value[:, half:], value[:, :half]], axis=1)


def lanes(value):
    return lax.broadcasted_iota(jnp.int32, value.shape, 1)


def low_body(x_ref, cot_ref, a_ref, b_ref, mine_ref, theirs_ref):
    acts = jnp.dot(x_ref[...], a_ref[...].astype(BF), preferred_element_type=F32)
    grads = rows_dot(cot_ref[...], b_ref[...].astype(BF))
    both = jnp.concatenate([acts, grads], axis=1)
    half = both.shape[0] // 2
    first = lax.axis_index("core") == 0
    mine_ref[...] = jnp.where(first, both[:half], both[half:])
    theirs_ref[...] = jnp.where(first, both[half:], both[:half])


def pair_body(mine_ref, theirs_ref, out_ref):
    total = (mine_ref[...] + theirs_ref[...]).astype(BF)
    for i in range(out_ref.shape[0]):
        out_ref[i] = total


def gradient_body(scale, x_ref, cot_ref, mine_ref, theirs_ref, out_ref):
    mine, theirs = mine_ref[...].astype(F32), theirs_ref[...].astype(F32)
    first = lax.axis_index("core") == 0
    low = jnp.concatenate([jnp.where(first, mine, theirs), jnp.where(first, theirs, mine)], axis=0)
    rank = low.shape[1] // 2
    upper = jnp.where(lanes(low) >= rank, low, 0.0).astype(BF)
    lower = jnp.where(lanes(low) < rank, turn(low), 0.0).astype(BF)
    half = x_ref.shape[1] // 2
    grad_a = (columns_dot(x_ref[:, :half], lower) + columns_dot(x_ref[:, half:], upper)) * scale
    grad_b = columns_dot(low.astype(BF), cot_ref[...])[:rank] * scale
    count, deep, wide = out_ref.shape
    rows_a, rows_b = half // count, rank // count
    blank = jnp.zeros((deep - rows_a - rows_b, wide), F32)
    for i in range(count):
        parts = [grad_a[i * rows_a : (i + 1) * rows_a], grad_b[i * rows_b : (i + 1) * rows_b], blank]
        out_ref[i] = jnp.concatenate(parts, axis=0).astype(BF)


def total_of(ref):
    total = ref[0].astype(F32)
    for i in range(1, ref.shape[0]):
        total = total + ref[i].astype(F32)
    return total


def sum_body(in_ref, out_ref):
    total = total_of(in_ref)
    for i in range(out_ref.shape[0]):
        out_ref[i] = total


def adam_body(in_ref, moment_ref, second_ref, out_ref):
    step = adam_step(total_of(in_ref), moment_ref[...], second_ref[...]).astype(BF)
    for i in range(out_ref.shape[0]):
        out_ref[i] = step


def inner_body(step_ref, a_ref, flat_ref, out_ref):
    count = step_ref.shape[0]
    half = a_ref.shape[0]
    rows_a = half // count
    step = jnp.concatenate([step_ref[i][:rows_a].astype(F32) for i in range(count)], axis=0)
    new_a = (a_ref[...] - learn_rate * step).astype(BF)
    left = jnp.dot(flat_ref[:, :half], new_a, preferred_element_type=F32)
    right = jnp.dot(flat_ref[:, half:], new_a, preferred_element_type=F32)
    inner = left + turn(right)
    top = inner.shape[0] // 2
    inner = jnp.where(lanes(inner[:top]) < inner.shape[1] // 2, inner[:top], turn(inner[top:]))
    inner = inner.astype(BF)
    for i in range(out_ref.shape[0]):
        out_ref[i] = inner


def base_body(mine_ref, theirs_ref, *refs):
    *near, far_ref, value_ref, out_ref = refs
    core, chip = lax.axis_index("core"), lax.axis_index("zl")
    pairs = value_ref.shape[0]
    total = jnp.dot(mine_ref[...], value_ref[chip, core], preferred_element_type=F32)
    total += jnp.dot(theirs_ref[...], value_ref[chip, 1 - core], preferred_element_type=F32)
    for i in range(1, pairs):
        place = lax.rem(chip + (pairs - i), pairs)
        total += jnp.dot(near[i - 1][...], value_ref[place, core], preferred_element_type=F32)
        total += jnp.dot(far_ref[i - 1], value_ref[place, 1 - core], preferred_element_type=F32)
    out_ref[...] = total


def cache_body(steps, q_ref, k_ref, v_ref, new_ref, length_ref, out_ref, weight_ref):
    groups, wide = length_ref.shape
    tall = q_ref.shape[0] // groups
    heads = q_ref.shape[1] // HD
    slots = wide // (tall // steps)
    row = lax.broadcasted_iota(jnp.int32, (heads * tall, wide), 0) % tall
    column = lax.broadcasted_iota(jnp.int32, (heads * tall, wide), 1)
    same = row // steps == column // slots
    slot = column % slots
    scale = 1.0 / math.sqrt(HD)
    for g in range(groups):
        query = jnp.concatenate(
            [q_ref[g * tall : (g + 1) * tall, h * HD : (h + 1) * HD] for h in range(heads)], axis=0
        )
        old = rows_dot(query, k_ref[g * wide : (g + 1) * wide, :]) * scale
        old = jnp.where(same & (slot < length_ref[g : g + 1, :]), old, -1e30)
        new = rows_dot(query, new_ref[...]) * scale
        token = column - g * tall
        seen = (token >= 0) & (token < tall) & (token // steps == row // steps) & (token <= row)
        new = jnp.where(seen, new, -1e30)
        largest = jnp.maximum(
            jnp.max(old, axis=1, keepdims=True), jnp.max(new, axis=1, keepdims=True)
        )
        old, new = jnp.exp(old - largest), jnp.exp(new - largest)
        total = jnp.sum(old, axis=1, keepdims=True) + jnp.sum(new, axis=1, keepdims=True)
        at = slice(g * heads * tall, (g + 1) * heads * tall)
        weight_ref[at, :] = (new / total).astype(BF)
        out_ref[at, :] = jnp.dot(
            (old / total).astype(BF), v_ref[g * wide : (g + 1) * wide, :], preferred_element_type=F32
        )


def last_body(groups, inner_ref, twice_ref, base_ref, old_ref, weight_ref, out_ref):
    inner = total_of(inner_ref).astype(BF).astype(F32)
    rank = inner.shape[1] // 2
    lower = jnp.where(lanes(inner) < rank, inner, 0.0)
    upper = jnp.where(lanes(inner) >= rank, inner, 0.0)
    both = jnp.concatenate([lower, upper], axis=0).astype(BF)
    change = jnp.dot(both, twice_ref[...], preferred_element_type=F32)
    values = (base_ref[...] + adapter_scale * change).astype(BF)
    tall = out_ref.shape[0] // groups
    heads = out_ref.shape[1] // HD
    for g in range(groups):
        at = slice(g * heads * tall, (g + 1) * heads * tall)
        out = old_ref[at, :] + jnp.dot(weight_ref[at, :], values, preferred_element_type=F32)
        out = out.astype(BF)
        for h in range(heads):
            out_ref[g * tall : (g + 1) * tall, h * HD : (h + 1) * HD] = out[h * tall : (h + 1) * tall]


def local(
    trainer_token_input,
    cotangent,
    adapter_a,
    adapter_b,
    moment_a,
    second_a,
    moment_b,
    second_b,
    value_matrix,
    decode_states,
    new_keys,
    queries,
    cache_keys,
    cache_values,
    lengths,
):
    pairs = lax.axis_size("zl")
    tensor = lax.axis_size(TENSOR)
    plane = lax.axis_size(PLANE)
    tokens, width = trainer_token_input.shape
    rank = adapter_a.shape[1]
    kv = cotangent.shape[1]
    rows, steps, _ = decode_states.shape
    count = rows * steps
    slots = cache_keys.shape[1]
    half = width // 2
    two = 2 * rank
    flat = decode_states.reshape(count, width)

    mine, theirs = call(
        low_body,
        (shape((tokens // 2, two), F32), shape((tokens // 2, two), F32)),
        trainer_token_input,
        cotangent,
        adapter_a,
        adapter_b,
    )
    pair = call(pair_body, shape((pairs, tokens // 2, two), BF), mine, swap(theirs))
    mine = jnp.sum(trade(pair, "zl").astype(F32), axis=0).astype(BF)
    theirs = swap(mine)

    rows_a, rows_b = half // plane, rank // plane
    deep = rows_a + rows_b + -(rows_a + rows_b) % 16
    scale = adapter_scale / (tokens * lax.axis_size(DP))
    block = call(
        lambda *refs: gradient_body(scale, *refs),
        shape((plane, deep, two), BF),
        trainer_token_input,
        cotangent,
        mine,
        theirs,
    )

    block, send = lax.optimization_barrier((block, flat))
    shard = trade(block, PLANE)
    near = [
        lax.ppermute(send, "zl", [(i, (i + hop) % pairs) for i in range(pairs)])
        for hop in range(1, pairs)
    ]

    shard = call(sum_body, shape((lax.axis_size("zh"), deep, two), F32), shard)
    shard = trade(shard, "zh")
    shard, near = lax.optimization_barrier((shard, near))

    place = lax.axis_index(PLANE)

    def piece(of_a, of_b):
        low_rows = lax.dynamic_slice_in_dim(of_a, place * rows_a, rows_a, 0)
        high_rows = lax.dynamic_slice_in_dim(of_a, half + place * rows_a, rows_a, 0)
        b_rows = lax.dynamic_slice_in_dim(of_b, place * rows_b, rows_b, 0)
        pad = jnp.ones((deep - rows_a - rows_b, kv), F32)
        return jnp.concatenate([jnp.concatenate([low_rows, high_rows], axis=1), b_rows, pad], axis=0)

    step = call(
        adam_body,
        shape((plane, deep, two), BF),
        shard,
        piece(moment_a, moment_b),
        piece(second_a, second_b),
    )
    step = trade(step, PLANE)

    inner = call(
        inner_body,
        shape((tensor, count // 2, two), BF),
        step,
        jnp.concatenate([adapter_a[:half], adapter_a[half:]], axis=1),
        flat,
    )
    inner = trade(inner, TENSOR)

    step_a = step[:, :rows_a].astype(F32).reshape(half, two)
    step_a = jnp.concatenate([step_a[:, :rank], step_a[:, rank:]], axis=0)
    step_b = step[:, rows_a : rows_a + rows_b].astype(F32).reshape(rank, kv)
    new_b = (adapter_b - learn_rate * step_b).astype(BF)
    twice = jnp.concatenate([new_b, new_b], axis=0)

    far = swap(jnp.stack(near))
    base = call(
        base_body,
        shape((count, kv), F32),
        flat,
        swap(flat),
        *near,
        far,
        value_matrix.reshape(pairs, 2, width, kv),
        flops=2 * count * tensor * width * kv,
        moved=8 * 2**20,
    )

    groups = rows * slots // HD
    heads = queries.shape[2] // HD
    old, weights = call(
        lambda *refs: cache_body(steps, *refs),
        (shape((count * heads, HD), F32), shape((count * heads, count), BF)),
        queries.reshape(count, heads * HD),
        cache_keys.reshape(rows * slots, kv),
        cache_values.reshape(rows * slots, kv),
        new_keys.reshape(count, kv),
        jnp.repeat(lengths, slots).reshape(groups, HD),
        flops=2 * count * heads * HD * HD * 3,
        moved=8 * 2**20,
    )
    attended = call(
        lambda *refs: last_body(groups, *refs),
        shape((count, heads * HD), BF),
        inner,
        twice,
        base,
        old,
        weights,
    )
    return (step_a, step_b, attended.reshape(rows, steps, heads * HD))


def solution(mesh):
    sizes = (4, 4, 4, mesh.devices.shape[1] // 2, 2)
    fine = Mesh(mesh.devices.reshape(sizes), DP + TENSOR)
    return jax.shard_map(
        local,
        mesh=fine,
        in_specs=(
            P(DP, TENSOR),
            P(DP, TENSOR),
            P(TENSOR, None),
            P(None, TENSOR),
            P(TENSOR, None),
            P(TENSOR, None),
            P(None, TENSOR),
            P(None, TENSOR),
            P(None, TENSOR),
            P(DP, None, TENSOR),
            P(DP, None, TENSOR),
            P(DP, None, TENSOR),
            P(DP, None, TENSOR),
            P(DP, None, TENSOR),
            P(DP),
        ),
        out_specs=(P(TENSOR, None), P(None, TENSOR), P(DP, None, TENSOR)),
        check_vma=False,
    )
```

time: 1290 us -> 109 us (0.08)
  the two profiles are of different devices: /device:TPU:32 before, /device:TPU:1 now
where the time goes in v2:
time: 109 us; the launch traced here: 108 us
  starting transfers between devices  59.2 us (54%)
  local copies, waits for them, and re-layouts  15.2 us (14%)
  waiting for transfers between devices  12.7 us (12%)
  Pallas kernels  8.27 us (8%)
  blocking collectives  7.27 us (7%)
  other arithmetic  4.21 us (4%)
    all_to_all x4, starting transfers between devices, trade(): return lax.all_to_all(parts, axes, 0, 0, tiled=True)  30.3 us
    ppermute x4, starting transfers between devices, swap(): return lax.ppermute(value, 'core', [(0, 1), (1, 0)])  20 us
    all_to_all x4, waiting for transfers between devices, trade(): return lax.all_to_all(parts, axes, 0, 0, tiled=True)  10.7 us
    unnamed x47, local copies, waits for them, and re-layouts  10.4 us
    ppermute x3, starting transfers between devices, local(): lax.ppermute(send, 'zl', [(i, (i + hop) % pairs) for i in range(pairs)])  8.99 us
    pallas_call x9, Pallas kernels, call(): pl.pallas_call(body, out_shape=out, cost_estimate=pl.CostEstimate(flops=f...  8.27 us
    all_to_all x1, blocking collectives, trade(): return lax.all_to_all(parts, axes, 0, 0, tiled=True)  7.27 us
  transfers between devices with their start and end apart: 11, of which 3 were waited for; matrix products, arithmetic and copies ran while one was open for 10% of the time, Pallas kernels for 7%

profile of v2, /device:TPU:1, one launch (start us, length us, event | category | flops | bytes accessed | tf_op | source)
XLA Modules:
  0.0 108.0 jit_solution(4964498996716806834)
XLA Ops:
  0.6 0.0 copy-start.2
  0.6 0.0 copy-start.13
  0.7 1.2 %copy.27.a_ref = f32[1024,64]{1,0:T(8,128)S(1)} copy(f32[1024,64]{0,1:T(8,128)} %param.17) | data formatting | bytes 524288 | tf_op args[2]
  1.9 0.0 copy-start.1
  1.9 1.0 copy-done.1
  2.9 0.8 copy-done.12
  3.8 0.8 copy-done.14
  4.5 0.4 shard_map.166
  4.9 8.8 %collective-permute-start = (f32[128,128]{1,0:T(8,128)S(1)}, f32[128,128]{1,0:T(8,128)S(1)}, u32[]{:S(2)}, u32[]{:S(2)}) collective-permute-start(f32[128,128]{1,0:T(8,128)S(1)} %get-tuple-element.14), channel_id=1, source_target_pairs={{0,1},{1,0},{2,3},{3,2},{4,5},{5,4},{6,7},{7,6},{8,9},{9,8},{10,11... | collective-permute-start | bytes 196616 | tf_op jit(solution)/shard_map/ppermute | solution.py:39
  13.7 0.9 collective-permute-done.theirs_ref
  14.6 7.3 %all_to_all.25 = bf16[4,128,128]{2,1,0:T(8,128)(2,1)S(1)} all-to-all(bf16[4,128,128]{2,1,0:T(8,128)(2,1)S(1)} %shard_map.167), channel_id=1, replica_groups=mesh['x'=4,'zh'=4,'y'=4,'zl'=4,'core'=2] {'zl'}, dimensions={0} | all-to-all | bytes 262144 | tf_op jit(solution)/shard_map/all_to_all | solution.py:35
  21.9 3.8 %collective-permute-start.1 = (bf16[128,128]{1,0:T(8,128)(2,1)S(1)}, bf16[128,128]{1,0:T(8,128)(2,1)S(1)}, u32[]{:S(2)}, u32[]{:S(2)}) collective-permute-start(bf16[128,128]{1,0:T(8,128)(2,1)S(1)} %reduce_sum.12.refs_2_), channel_id=1, source_target_pairs={{0,1},{1,0},{2,3},{3,2},{4,5},{5,4},{6,7},{7,6},{8,9},{9,8},{10,11... | collective-permute-start | bytes 98312 | tf_op jit(solution)/shard_map/ppermute | solution.py:39
  25.7 1.0 reshape.41.flat_ref.mine_ref
  26.7 1.9 %collective-permute-start.5 = (bf16[128,1024]{1,0:T(8,128)(2,1)S(1)}, bf16[128,1024]{1,0:T(8,128)(2,1)}, u32[]{:S(2)}, u32[]{:S(2)}) collective-permute-start(bf16[128,1024]{1,0:T(8,128)(2,1)S(1)} %reshape.41.flat_ref.mine_ref), channel_id=1, source_target_pairs={{0,1},{1,0},{2,3},{3,2},{4,5},{5,4},{6,7},{7,6},{8,9},{9,8},{10,11... | collective-permute-start | bytes 786440 | tf_op jit(solution)/shard_map/ppermute | solution.py:39
  28.7 1.1 %shard_map.168 = bf16[16,48,128]{2,1,0:T(8,128)(2,1)} custom-call(bf16[256,1024]{1,0:T(8,128)(2,1)S(1)} %copy-done.2, bf16[256,128]{1,0:T(8,128)(2,1)S(1)} %copy-done.13, bf16[128,128]{1,0:T(8,128)(2,1)S(1)} %reduce_sum.12.refs_2_, bf16[128,128]{1,0:T(8,128)(2,1)S(1)} %collective-permute-done.1.refs_3_), custom_call_target="tpu_custom_call" | custom-call | tf_op jit(solution)/shard_map/pallas_call | solution.py:43
  29.8 4.6 %all-to-all-start.1 = ((bf16[16,48,128]{2,1,0:T(8,128)(2,1)}), bf16[16,48,128]{2,1,0:T(8,128)(2,1)S(1)}, u32[]{:S(2)}, u32[]{:S(2)}) async-start(bf16[16,48,128]{2,1,0:T(8,128)(2,1)} %shard_map.168), calls=%async_computation.1 | async-start | bytes 393216 | tf_op jit(solution)/shard_map/all_to_all | solution.py:35
  34.4 0.0 copy-start.19
  34.4 0.0 copy-start.8
  34.4 0.0 copy-start.9
  34.4 0.0 copy-start.17
  34.5 1.0 constant_dynamic-slice_fusion.2
  35.4 0.1 copy.36
  35.5 0.1 copy.37
  35.6 0.1 copy.38
  35.6 0.1 copy.39
  35.7 0.1 pad.16.clone
  35.8 0.7 constant_dynamic-slice_fusion
  36.5 2.6 %collective-permute-start.2 = (bf16[128,1024]{1,0:T(8,128)(2,1)S(1)}, bf16[128,1024]{1,0:T(8,128)(2,1)S(1)}, u32[]{:S(2)}, u32[]{:S(2)}) collective-permute-start(bf16[128,1024]{1,0:T(8,128)(2,1)S(1)} %reshape.41.flat_ref.mine_ref), channel_id=1, source_target_pairs={{0,2},{2,4},{4,6},{6,0},{1,3},{3,5},{5,7},{7,1},{8,10},{10,12},{12... | collective-permute-start | bytes 786440 | tf_op jit(solution)/shard_map/ppermute | solution.py:262
  39.1 2.9 %collective-permute-start.3 = (bf16[128,1024]{1,0:T(8,128)(2,1)S(1)}, bf16[128,1024]{1,0:T(8,128)(2,1)S(1)}, u32[]{:S(2)}, u32[]{:S(2)}) collective-permute-start(bf16[128,1024]{1,0:T(8,128)(2,1)S(1)} %reshape.41.flat_ref.mine_ref), channel_id=1, source_target_pairs={{0,4},{2,6},{4,0},{6,2},{1,5},{3,7},{5,1},{7,3},{8,12},{10,14},{12... | collective-permute-start | bytes 786440 | tf_op jit(solution)/shard_map/ppermute | solution.py:262
  42.0 3.6 %collective-permute-start.4 = (bf16[128,1024]{1,0:T(8,128)(2,1)S(1)}, bf16[128,1024]{1,0:T(8,128)(2,1)S(1)}, u32[]{:S(2)}, u32[]{:S(2)}) collective-permute-start(bf16[128,1024]{1,0:T(8,128)(2,1)S(1)} %reshape.41.flat_ref.mine_ref), channel_id=1, source_target_pairs={{0,6},{2,0},{4,2},{6,4},{1,7},{3,1},{5,3},{7,5},{8,14},{10,8},{12,... | collective-permute-start | bytes 786440 | tf_op jit(solution)/shard_map/ppermute | solution.py:262
  45.5 0.0 all-to-all-done.1.in_ref
  45.5 0.7 shard_map.169
  46.2 12.1 %all-to-all-start.2 = ((f32[4,48,128]{2,1,0:T(8,128)}), f32[4,48,128]{2,1,0:T(8,128)S(1)}, u32[]{:S(2)}, u32[]{:S(2)}) async-start(f32[4,48,128]{2,1,0:T(8,128)} %shard_map.169), calls=%async_computation.2 | async-start | bytes 196608 | tf_op jit(solution)/shard_map/all_to_all | solution.py:35
  58.3 0.1 maximum_maximum_fusion.1
  58.5 1.2 %collective-permute-done.3.refs_1_ = bf16[128,1024]{1,0:T(8,128)(2,1)S(1)} collective-permute-done((bf16[128,1024]{1,0:T(8,128)(2,1)S(1)}, bf16[128,1024]{1,0:T(8,128)(2,1)S(1)}, u32[]{:S(2)}, u32[]{:S(2)}) %collective-permute-start.3) | collective-permute-done | bytes 262176 | tf_op jit(solution)/shard_map/ppermute | solution.py:262
  59.7 10.6 %all-to-all-done.2.in_ref = f32[4,48,128]{2,1,0:T(8,128)S(1)} async-done(((f32[4,48,128]{2,1,0:T(8,128)}), f32[4,48,128]{2,1,0:T(8,128)S(1)}, u32[]{:S(2)}, u32[]{:S(2)}) %all-to-all-start.2) | async-done | bytes 98336 | tf_op jit(solution)/shard_map/all_to_all | solution.py:35
  70.3 0.7 shard_map.170
  71.0 6.6 %all-to-all-start.3 = ((bf16[16,48,128]{2,1,0:T(8,128)(2,1)}), bf16[16,48,128]{2,1,0:T(8,128)(2,1)S(1)}, u32[]{:S(2)}, u32[]{:S(2)}) async-start(bf16[16,48,128]{2,1,0:T(8,128)(2,1)} %shard_map.170), calls=%async_computation.3 | async-start | bytes 393216 | tf_op jit(solution)/shard_map/all_to_all | solution.py:35
  77.7 0.1 pad_maximum_fusion.2.a_ref
  77.8 0.1 reshape.47.refs_0_
  77.9 0.1 broadcast_in_dim.7
  78.0 0.1 broadcast_in_dim.8
  78.1 0.1 broadcast_in_dim.9.refs_4_
  78.1 0.0 copy-done.17
  78.2 2.8 %shard_map.173 = (f32[1024,128]{1,0:T(8,128)S(1)}, bf16[1024,128]{1,0:T(8,128)(2,1)S(1)}) custom-call(bf16[128,1024]{1,0:T(8,128)(2,1)S(1)} %reshape.47.refs_0_, bf16[1024,128]{1,0:T(8,128)(2,1)S(1)} %bitcast.16, bf16[1024,128]{1,0:T(8,128)(2,1)S(1)} %bitcast.17, bf16[128,128]{1,0:T(8,128)(2,1)S(1)} %bitcast.18, s32[8,128]{1,0:T(8,128)S(1)} %broadcast_in_dim.9.refs_4_), custom_call_target="tpu_custom_call" | custom-call | flops 100663296 | bytes 8388608 | tf_op jit(solution)/shard_map/pallas_call | solution.py:43
  80.9 0.0 copy-start.15
  81.0 1.1 pad_maximum_fusion
  82.0 0.1 copy-done.10
  82.1 5.5 %collective-permute-start.6 = (bf16[3,128,1024]{2,1,0:T(8,128)(2,1)}, bf16[3,128,1024]{2,1,0:T(8,128)(2,1)}, u32[]{:S(2)}, u32[]{:S(2)}) collective-permute-start(bf16[3,128,1024]{2,1,0:T(8,128)(2,1)} %pad_maximum_fusion), channel_id=1, source_target_pairs={{0,1},{1,0},{2,3},{3,2},{4,5},{5,4},{6,7},{7,6},{8,9},{9,8},{10,11... | collective-permute-start | bytes 2359304 | tf_op jit(solution)/shard_map/ppermute | solution.py:39
  87.6 0.3 shard_map.171
  87.9 0.7 copy-done.7
  88.6 6.9 %all-to-all-start.4 = ((bf16[8,64,128]{2,1,0:T(8,128)(2,1)}), bf16[8,64,128]{2,1,0:T(8,128)(2,1)S(1)}, u32[]{:S(2)}, u32[]{:S(2)}) async-start(bf16[8,64,128]{2,1,0:T(8,128)(2,1)} %copy-done.7), calls=%async_computation.4 | async-start | bytes 262144 | tf_op jit(solution)/shard_map/all_to_all | solution.py:35
  95.6 0.9 fusion.1
  96.4 0.6 subtract_convert_fusion
  97.0 1.1 copy.40
  98.1 1.7 %copy.41 = f32[512,64]{0,1:T(8,128)} copy(f32[512,64]{1,0:T(8,128)} %get-tuple-element.28) | data formatting | bytes 262144
  99.8 0.6 pad_maximum_fusion.3.refs_1_
  100.5 1.6 %pad_maximum_fusion.1 = f32[1024,64]{0,1:T(8,128)} fusion(f32[512,64]{0,1:T(8,128)} %copy.41, f32[512,64]{0,1:T(8,128)S(1)} %copy.40), kind=kLoop, calls=%fused_computation.1 | loop fusion | flops 65536 | bytes 524288 | tf_op jit(solution)/shard_map/concatenate | solution.py:298
  102.1 1.9 %shard_map.172.refs_2_ = f32[128,128]{1,0:T(8,128)S(1)} custom-call(bf16[128,1024]{1,0:T(8,128)(2,1)S(1)} %reshape.41.flat_ref.mine_ref, bf16[128,1024]{1,0:T(8,128)(2,1)} %collective-permute-done.5.theirs_ref, bf16[128,1024]{1,0:T(8,128)(2,1)S(1)} %collective-permute-done.2.refs_0_, bf16[128,1024]{1,0:T(8,128)(2,1)S(1)} %collective-permute-done.3.refs_1_, ...), custom_call_target="tpu_custom_call" | custom-call | flops 268435456 | bytes 8388608 | tf_op jit(solution)/shard_map/pallas_call | solution.py:43
  104.0 1.0 copy-done.6
  105.1 0.9 copy-done.11
  106.0 0.8 copy-done.16
  106.8 0.4 shard_map.174
  107.2 0.8 reshape.51
  (37 shorter events, 0.2 us)
Async XLA Ops:
  0.6 28.0 %copy-start.2 = (bf16[256,1024]{1,0:T(8,128)(2,1)S(1)}, bf16[256,1024]{1,0:T(8,128)(2,1)}, u32[]{:S(2)}) copy-start(bf16[256,1024]{1,0:T(8,128)(2,1)} %refs_0_.1) | copy-start | bytes 1572868
  0.6 28.0 %copy-start.13 = (bf16[256,128]{1,0:T(8,128)(2,1)S(1)}, bf16[256,128]{1,0:T(8,128)(2,1)}, u32[]{:S(2)}) copy-start(bf16[256,128]{1,0:T(8,128)(2,1)} %refs_1_.1) | copy-start | bytes 196612
  1.9 1.0 copy-start.1
  2.9 0.8 copy-start.12
  3.8 0.8 copy-start.14
  4.9 9.7 %collective-permute-start = (f32[128,128]{1,0:T(8,128)S(1)}, f32[128,128]{1,0:T(8,128)S(1)}, u32[]{:S(2)}, u32[]{:S(2)}) collective-permute-start(f32[128,128]{1,0:T(8,128)S(1)} %get-tuple-element.14), channel_id=1, source_target_pairs={{0,1},{1,0},{2,3},{3,2},{4,5},{5,4},{6,7},{7,6},{8,9},{9,8},{10,11... | collective-permute-start | bytes 196616 | tf_op jit(solution)/shard_map/ppermute | solution.py:39
  21.9 6.8 %collective-permute-start.1 = (bf16[128,128]{1,0:T(8,128)(2,1)S(1)}, bf16[128,128]{1,0:T(8,128)(2,1)S(1)}, u32[]{:S(2)}, u32[]{:S(2)}) collective-permute-start(bf16[128,128]{1,0:T(8,128)(2,1)S(1)} %reduce_sum.12.refs_2_), channel_id=1, source_target_pairs={{0,1},{1,0},{2,3},{3,2},{4,5},{5,4},{6,7},{7,6},{8,9},{9,8},{10,11... | collective-permute-start | bytes 98312 | tf_op jit(solution)/shard_map/ppermute | solution.py:39
  26.7 75.4 %collective-permute-start.5 = (bf16[128,1024]{1,0:T(8,128)(2,1)S(1)}, bf16[128,1024]{1,0:T(8,128)(2,1)}, u32[]{:S(2)}, u32[]{:S(2)}) collective-permute-start(bf16[128,1024]{1,0:T(8,128)(2,1)S(1)} %reshape.41.flat_ref.mine_ref), channel_id=1, source_target_pairs={{0,1},{1,0},{2,3},{3,2},{4,5},{5,4},{6,7},{7,6},{8,9},{9,8},{10,11... | collective-permute-start | bytes 786440 | tf_op jit(solution)/shard_map/ppermute | solution.py:39
  29.8 48.0 %copy-start.18 = (bf16[32,4,1024]{2,1,0:T(4,128)(2,1)S(1)}, bf16[32,4,1024]{2,1,0:T(4,128)(2,1)}, u32[]{:S(2)}) copy-start(bf16[32,4,1024]{2,1,0:T(4,128)(2,1)} %param.26) | copy-start | bytes 786436
  29.8 15.8 %all-to-all-start.1 = ((bf16[16,48,128]{2,1,0:T(8,128)(2,1)}), bf16[16,48,128]{2,1,0:T(8,128)(2,1)S(1)}, u32[]{:S(2)}, u32[]{:S(2)}) async-start(bf16[16,48,128]{2,1,0:T(8,128)(2,1)} %shard_map.168), calls=%async_computation.1 | async-start | bytes 393216 | tf_op jit(solution)/shard_map/all_to_all | solution.py:35
  34.4 43.5 %copy-start.19 = (s32[32]{0:T(128)S(1)}, s32[32]{0:T(128)}, u32[]{:S(2)}) copy-start(s32[32]{0:T(128)} %param.29) | copy-start | bytes 388
  34.4 43.7 %copy-start.8 = (bf16[32,32,128]{2,1,0:T(8,128)(2,1)S(1)}, bf16[32,32,128]{2,1,0:T(8,128)(2,1)}, u32[]{:S(2)}) copy-start(bf16[32,32,128]{2,1,0:T(8,128)(2,1)} %param.27) | copy-start | bytes 786436
  34.4 43.7 %copy-start.9 = (bf16[32,32,128]{2,1,0:T(8,128)(2,1)S(1)}, bf16[32,32,128]{2,1,0:T(8,128)(2,1)}, u32[]{:S(2)}) copy-start(bf16[32,32,128]{2,1,0:T(8,128)(2,1)} %param.28) | copy-start | bytes 786436
  34.4 43.7 %copy-start.17 = (bf16[32,4,128]{2,1,0:T(4,128)(2,1)S(1)}, bf16[32,4,128]{2,1,0:T(4,128)(2,1)}, u32[]{:S(2)}) copy-start(bf16[32,4,128]{2,1,0:T(4,128)(2,1)} %param.25) | copy-start | bytes 98308
  36.5 21.9 %collective-permute-start.2 = (bf16[128,1024]{1,0:T(8,128)(2,1)S(1)}, bf16[128,1024]{1,0:T(8,128)(2,1)S(1)}, u32[]{:S(2)}, u32[]{:S(2)}) collective-permute-start(bf16[128,1024]{1,0:T(8,128)(2,1)S(1)} %reshape.41.flat_ref.mine_ref), channel_id=1, source_target_pairs={{0,2},{2,4},{4,6},{6,0},{1,3},{3,5},{5,7},{7,1},{8,10},{10,12},{12... | collective-permute-start | bytes 786440 | tf_op jit(solution)/shard_map/ppermute | solution.py:262
  39.1 20.6 %collective-permute-start.3 = (bf16[128,1024]{1,0:T(8,128)(2,1)S(1)}, bf16[128,1024]{1,0:T(8,128)(2,1)S(1)}, u32[]{:S(2)}, u32[]{:S(2)}) collective-permute-start(bf16[128,1024]{1,0:T(8,128)(2,1)S(1)} %reshape.41.flat_ref.mine_ref), channel_id=1, source_target_pairs={{0,4},{2,6},{4,0},{6,2},{1,5},{3,7},{5,1},{7,3},{8,12},{10,14},{12... | collective-permute-start | bytes 786440 | tf_op jit(solution)/shard_map/ppermute | solution.py:262
  42.0 17.7 %collective-permute-start.4 = (bf16[128,1024]{1,0:T(8,128)(2,1)S(1)}, bf16[128,1024]{1,0:T(8,128)(2,1)S(1)}, u32[]{:S(2)}, u32[]{:S(2)}) collective-permute-start(bf16[128,1024]{1,0:T(8,128)(2,1)S(1)} %reshape.41.flat_ref.mine_ref), channel_id=1, source_target_pairs={{0,6},{2,0},{4,2},{6,4},{1,7},{3,1},{5,3},{7,5},{8,14},{10,8},{12,... | collective-permute-start | bytes 786440 | tf_op jit(solution)/shard_map/ppermute | solution.py:262
  46.2 24.1 %all-to-all-start.2 = ((f32[4,48,128]{2,1,0:T(8,128)}), f32[4,48,128]{2,1,0:T(8,128)S(1)}, u32[]{:S(2)}, u32[]{:S(2)}) async-start(f32[4,48,128]{2,1,0:T(8,128)} %shard_map.169), calls=%async_computation.2 | async-start | bytes 196608 | tf_op jit(solution)/shard_map/all_to_all | solution.py:35
  59.7 21.3 %copy-start.3 = (bf16[128,1024]{1,0:T(8,128)(2,1)}, bf16[128,1024]{1,0:T(8,128)(2,1)S(1)}, u32[]{:S(2)}) copy-start(bf16[128,1024]{1,0:T(8,128)(2,1)S(1)} %collective-permute-done.4.refs_2_) | copy-start | bytes 786436
  71.0 16.5 %all-to-all-start.3 = ((bf16[16,48,128]{2,1,0:T(8,128)(2,1)}), bf16[16,48,128]{2,1,0:T(8,128)(2,1)S(1)}, u32[]{:S(2)}, u32[]{:S(2)}) async-start(bf16[16,48,128]{2,1,0:T(8,128)(2,1)} %shard_map.170), calls=%async_computation.3 | async-start | bytes 393216 | tf_op jit(solution)/shard_map/all_to_all | solution.py:35
  80.9 1.1 %copy-start.5 = (f32[1024,128]{1,0:T(8,128)}, f32[1024,128]{1,0:T(8,128)S(1)}, u32[]{:S(2)}) copy-start(f32[1024,128]{1,0:T(8,128)S(1)} %get-tuple-element.21.refs_3_) | copy-start | bytes 1572868
  80.9 1.2 %copy-start.10 = (bf16[1024,128]{1,0:T(8,128)(2,1)}, bf16[1024,128]{1,0:T(8,128)(2,1)S(1)}, u32[]{:S(2)}) copy-start(bf16[1024,128]{1,0:T(8,128)(2,1)S(1)} %get-tuple-element.22.refs_4_) | copy-start | bytes 786436
  80.9 15.5 %copy-start.15 = (f32[64,128]{1,0:T(8,128)S(1)}, f32[64,128]{1,0:T(8,128)}, u32[]{:S(2)}) copy-start(f32[64,128]{1,0:T(8,128)} %b_ref.1) | copy-start | bytes 98308
  82.1 20.0 %copy-start = (bf16[8192,128]{1,0:T(8,128)(2,1)S(1)}, bf16[8192,128]{1,0:T(8,128)(2,1)}, u32[]{:S(2)}) copy-start(bf16[8192,128]{1,0:T(8,128)(2,1)} %param.23) | copy-start | bytes 6291460
  82.1 20.0 %collective-permute-start.6 = (bf16[3,128,1024]{2,1,0:T(8,128)(2,1)}, bf16[3,128,1024]{2,1,0:T(8,128)(2,1)}, u32[]{:S(2)}, u32[]{:S(2)}) collective-permute-start(bf16[3,128,1024]{2,1,0:T(8,128)(2,1)} %pad_maximum_fusion), channel_id=1, source_target_pairs={{0,1},{1,0},{2,3},{3,2},{4,5},{5,4},{6,7},{7,6},{8,9},{9,8},{10,11... | collective-permute-start | bytes 2359304 | tf_op jit(solution)/shard_map/ppermute | solution.py:39
  87.9 0.7 copy-start.7
  88.6 13.5 %copy-start.4 = (bf16[128,1024]{1,0:T(8,128)(2,1)S(1)}, bf16[128,1024]{1,0:T(8,128)(2,1)}, u32[]{:S(2)}) copy-start(bf16[128,1024]{1,0:T(8,128)(2,1)} %copy-done.3) | copy-start | bytes 786436
  88.6 15.4 %all-to-all-start.4 = ((bf16[8,64,128]{2,1,0:T(8,128)(2,1)}), bf16[8,64,128]{2,1,0:T(8,128)(2,1)S(1)}, u32[]{:S(2)}, u32[]{:S(2)}) async-start(bf16[8,64,128]{2,1,0:T(8,128)(2,1)} %copy-done.7), calls=%async_computation.4 | async-start | bytes 262144 | tf_op jit(solution)/shard_map/all_to_all | solution.py:35
  104.0 1.0 copy-start.6
  105.1 0.9 copy-start.11
  106.0 0.8 copy-start.16

commit v3 on v2

v3 whole, which is shorter than its diff:
```python
import math

import jax
import jax.numpy as jnp
from jax import lax
from jax.experimental import pallas as pl
from jax.experimental.pallas import tpu as pltpu
from jax.sharding import Mesh, PartitionSpec as P

HD = 128


adapter_scale = 2.0
learn_rate = 0.001
beta_one = 0.9
beta_two = 0.999
adam_eps = 1e-08
first_fix = 1.0 - 0.9**10
second_fix = 1.0 - 0.999**10

DP = ("x", "zh", "y")
PLANE = ("x", "y")
TENSOR = ("zl", "core")
BF = jnp.bfloat16
F32 = jnp.float32


def adam_step(grad, moment, second):
    moment_new = beta_one * moment + (1.0 - beta_one) * grad
    second_new = beta_two * second + (1.0 - beta_two) * grad * grad
    return moment_new / first_fix / (jnp.sqrt(second_new / second_fix) + adam_eps)


def trade(parts, axes):
    return lax.all_to_all(parts, axes, 0, 0, tiled=True)


def swap(value):
    return lax.ppermute(value, "core", [(0, 1), (1, 0)])


def reach(value, hop):
    return lax.ppermute(value, "zl", [(i, i ^ hop) for i in range(lax.axis_size("zl"))])


def call(body, out, *args, flops=0, moved=0, **more):
    return pl.pallas_call(
        body,
        out_shape=out,
        cost_estimate=pl.CostEstimate(flops=flops, bytes_accessed=moved, transcendentals=0),
        compiler_params=pltpu.CompilerParams(vmem_limit_bytes=16 * 2**20),
        **more,
    )(*args)


def far(value):
    return pltpu.with_memory_space_constraint(value, pltpu.HBM)


def shape(dims, kind):
    return jax.ShapeDtypeStruct(dims, kind)


def columns_dot(a, b):
    return lax.dot_general(a, b, (((0,), (0,)), ((), ())), preferred_element_type=F32)


def rows_dot(a, b):
    return lax.dot_general(a, b, (((1,), (1,)), ((), ())), preferred_element_type=F32)


def low_body(x_ref, cot_ref, a_ref, b_ref, mine_ref, theirs_ref):
    acts = rows_dot(x_ref[...], a_ref[...].astype(BF))
    grads = rows_dot(cot_ref[...], b_ref[...].astype(BF))
    both = jnp.concatenate([acts, grads], axis=1)
    half = both.shape[0] // 2
    first = lax.axis_index("core") == 0
    mine_ref[...] = jnp.where(first, both[:half], both[half:])
    theirs_ref[...] = jnp.where(first, both[half:], both[:half])


def pair_body(mine_ref, theirs_ref, out_ref):
    total = (mine_ref[...] + theirs_ref[...]).astype(BF)
    for i in range(out_ref.shape[0]):
        out_ref[i] = total


def stack(value, wide):
    return jnp.concatenate([value[:, i : i + wide] for i in range(0, value.shape[1], wide)], axis=0)


def unstack(value, tall):
    return jnp.concatenate([value[i : i + tall] for i in range(0, value.shape[0], tall)], axis=1)


def gradient_body(scale, x_ref, cot_ref, mine_ref, theirs_ref, out_ref):
    mine, theirs = mine_ref[...].astype(F32), theirs_ref[...].astype(F32)
    first = lax.axis_index("core") == 0
    low = jnp.concatenate([jnp.where(first, mine, theirs), jnp.where(first, theirs, mine)], axis=0)
    rank = low.shape[1] // 2
    low = low.astype(BF)
    count, deep, wide = out_ref.shape
    grad_a = stack(columns_dot(low, x_ref[...])[rank:], wide) * scale
    grad_b = columns_dot(low, cot_ref[...])[:rank] * scale
    rows_a, rows_b = grad_a.shape[0] // count, rank // count
    blank = jnp.zeros((deep - rows_a - rows_b, wide), F32)
    for i in range(count):
        parts = [grad_a[i * rows_a : (i + 1) * rows_a], grad_b[i * rows_b : (i + 1) * rows_b], blank]
        out_ref[i] = jnp.concatenate(parts, axis=0).astype(BF)


def total_of(ref):
    total = ref[0].astype(F32)
    for i in range(1, ref.shape[0]):
        total = total + ref[i].astype(F32)
    return total


def sum_body(in_ref, out_ref):
    total = total_of(in_ref)
    for i in range(out_ref.shape[0]):
        out_ref[i] = total


def shard_body(moment_a_ref, second_a_ref, moment_b_ref, second_b_ref, moment_ref, second_ref):
    deep, wide = moment_ref.shape
    rank = moment_a_ref.shape[0]
    count = lax.axis_size(PLANE)
    rows_a, rows_b = rank * moment_a_ref.shape[1] // wide // count, rank // count
    place = lax.axis_index(PLANE)
    column = pl.multiple_of(place * rows_a // rank * wide, wide)
    row = pl.multiple_of(lax.rem(place * rows_a, rank), rows_a)
    most = max(rows_b, 8)
    row_b = pl.multiple_of(place * rows_b // most * most, most)

    def piece(a_ref, b_ref):
        of_b = b_ref[pl.ds(row_b, most), :]
        chosen = of_b[:rows_b]
        for i in range(rows_b, most, rows_b):
            chosen = jnp.where(place * rows_b == row_b + i, of_b[i : i + rows_b], chosen)
        pad = jnp.ones((deep - rows_a - rows_b, wide), F32)
        return jnp.concatenate([a_ref[pl.ds(row, rows_a), pl.ds(column, wide)], chosen, pad], axis=0)

    moment_ref[...] = piece(moment_a_ref, moment_b_ref)
    second_ref[...] = piece(second_a_ref, second_b_ref)


def adam_body(in_ref, moment_ref, second_ref, out_ref):
    step = adam_step(total_of(in_ref), moment_ref[...], second_ref[...]).astype(BF)
    for i in range(out_ref.shape[0]):
        out_ref[i] = step


def step_of_a(step_ref, rank, width):
    count, _, wide = step_ref.shape
    rows_a = rank * width // wide // count
    step = jnp.concatenate([step_ref[i].astype(F32)[:rows_a] for i in range(count)], axis=0)
    return unstack(step, rank)


def inner_body(step_ref, a_ref, flat_ref, out_ref):
    rank, width = a_ref.shape
    new_a = (a_ref[...] - learn_rate * step_of_a(step_ref, rank, width)).astype(BF)
    inner = rows_dot(new_a, flat_ref[...]).astype(BF)
    for i in range(out_ref.shape[0]):
        out_ref[i] = inner


def step_body(step_ref, b_ref, step_a_ref, step_b_ref, new_b_ref):
    count = step_ref.shape[0]
    rank, width = step_a_ref.shape
    rows_a, rows_b = rank * width // step_ref.shape[2] // count, rank // count
    step_a_ref[...] = step_of_a(step_ref, rank, width)
    parts = [step_ref[i].astype(F32)[rows_a : rows_a + rows_b] for i in range(count)]
    step_b = jnp.concatenate(parts, axis=0)
    step_b_ref[...] = step_b
    new_b_ref[...] = (b_ref[...] - learn_rate * step_b).astype(BF)


def base_body(value_ref, *refs):
    pieces, out_ref, held, value, copied = refs[:4], *refs[4:]
    core, chip = lax.axis_index("core"), lax.axis_index("zl")
    chips = value.shape[0]
    half = chips // 2
    copies = []
    for i in range(chips):
        place = lax.bitwise_xor(chip, i)
        for j in range(2):
            copies.append(
                (
                    pltpu.make_async_copy(
                        pieces[2 * j + i // half].at[i % half], held.at[i, j], copied.at[i, j, 0]
                    ),
                    pltpu.make_async_copy(
                        value_ref.at[place, core if j == 0 else 1 - core], value.at[i, j], copied.at[i, j, 1]
                    ),
                )
            )
    for pair in copies:
        for copy in pair:
            copy.start()
    total = jnp.zeros(out_ref.shape, F32)
    for i in range(chips):
        for j in range(2):
            for copy in copies[2 * i + j]:
                copy.wait()
            total += jnp.dot(held[i, j], value[i, j], preferred_element_type=F32)
    out_ref[...] = total


def cache_body(steps, q_ref, k_ref, v_ref, new_ref, length_ref, out_ref, weight_ref):
    groups, wide = length_ref.shape
    tall = q_ref.shape[0] // groups
    heads = q_ref.shape[1] // HD
    slots = wide // (tall // steps)
    row = lax.broadcasted_iota(jnp.int32, (heads * tall, wide), 0) % tall
    column = lax.broadcasted_iota(jnp.int32, (heads * tall, wide), 1)
    same = row // steps == column // slots
    slot = column % slots
    scale = 1.0 / math.sqrt(HD)
    for g in range(groups):
        query = jnp.concatenate(
            [q_ref[g * tall : (g + 1) * tall, h * HD : (h + 1) * HD] for h in range(heads)], axis=0
        )
        old = rows_dot(query, k_ref[g * wide : (g + 1) * wide, :]) * scale
        old = jnp.where(same & (slot < length_ref[g : g + 1, :]), old, -1e30)
        new = rows_dot(query, new_ref[...]) * scale
        token = column - g * tall
        seen = (token >= 0) & (token < tall) & (token // steps == row // steps) & (token <= row)
        new = jnp.where(seen, new, -1e30)
        largest = jnp.maximum(
            jnp.max(old, axis=1, keepdims=True), jnp.max(new, axis=1, keepdims=True)
        )
        old, new = jnp.exp(old - largest), jnp.exp(new - largest)
        total = jnp.sum(old, axis=1, keepdims=True) + jnp.sum(new, axis=1, keepdims=True)
        at = slice(g * heads * tall, (g + 1) * heads * tall)
        weight_ref[at, :] = (new / total).astype(BF)
        out_ref[at, :] = jnp.dot(
            (old / total).astype(BF), v_ref[g * wide : (g + 1) * wide, :], preferred_element_type=F32
        )


def last_body(groups, inner_ref, new_b_ref, base_ref, old_ref, weight_ref, out_ref):
    inner = total_of(inner_ref).astype(BF)
    change = columns_dot(inner, new_b_ref[...])
    values = (base_ref[...] + adapter_scale * change).astype(BF)
    rows, steps, wide = out_ref.shape
    each = rows // groups
    tall = each * steps
    heads = wide // HD
    for g in range(groups):
        at = slice(g * heads * tall, (g + 1) * heads * tall)
        out = old_ref[at, :] + jnp.dot(weight_ref[at, :], values, preferred_element_type=F32)
        for h in range(heads):
            part = out[h * tall : (h + 1) * tall].reshape(each, steps, HD)
            out_ref[g * each : (g + 1) * each, :, h * HD : (h + 1) * HD] = part.astype(BF)


def local(
    trainer_token_input,
    cotangent,
    adapter_a,
    adapter_b,
    moment_a,
    second_a,
    moment_b,
    second_b,
    value_matrix,
    decode_states,
    new_keys,
    queries,
    cache_keys,
    cache_values,
    lengths,
):
    pairs = lax.axis_size("zl")
    tensor = lax.axis_size(TENSOR)
    plane = lax.axis_size(PLANE)
    tokens, width = trainer_token_input.shape
    rank = adapter_a.shape[1]
    kv = cotangent.shape[1]
    rows, steps, _ = decode_states.shape
    count = rows * steps
    slots = cache_keys.shape[1]
    two = 2 * rank
    flat = decode_states.reshape(count, width)
    a_turned = adapter_a.T

    half = shape((tokens // 2, two), F32)
    starts = (trainer_token_input, cotangent, a_turned, adapter_b)
    mine, theirs = call(low_body, (half, half), *map(far, starts))
    pair = call(pair_body, shape((pairs, tokens // 2, two), BF), mine, swap(theirs))

    pair, send = lax.optimization_barrier((pair, flat))
    next_chip = reach(send[None], 1)
    mine = jnp.sum(trade(pair, "zl").astype(F32), axis=0).astype(BF)
    theirs = swap(mine)

    rows_a, rows_b = rank * width // kv // plane, rank // plane
    deep = rows_a + rows_b + -(rows_a + rows_b) % 16
    scale = adapter_scale / (tokens * lax.axis_size(DP))
    block = call(
        lambda *refs: gradient_body(scale, *refs),
        shape((plane, deep, kv), BF),
        trainer_token_input,
        cotangent,
        mine,
        theirs,
    )

    block, mine_chip, next_chip = lax.optimization_barrier((block, flat[None], next_chip))
    near = jnp.concatenate([mine_chip, next_chip], axis=0)
    distant = reach(near, 2)
    shard = trade(block, PLANE)
    shard = call(sum_body, shape((lax.axis_size("zh"), deep, kv), F32), shard)
    shard, near_sent, moments = lax.optimization_barrier(
        (shard, near, (moment_a.T, second_a.T, moment_b, second_b))
    )
    shard = trade(shard, "zh")
    near_other = swap(near_sent)
    piece = shape((deep, kv), F32)
    moments = call(shard_body, (piece, piece), *map(far, moments))
    step = call(adam_body, shape((plane, deep, kv), BF), shard, *moments)
    step, distant, near_other, query = lax.optimization_barrier((step, distant, near_other, queries))
    step = trade(step, PLANE)
    distant_other = swap(distant)
    groups = rows * slots // HD
    heads = queries.shape[2] // HD
    old, weights = call(
        lambda *refs: cache_body(steps, *refs),
        (shape((count * heads, HD), F32), shape((count * heads, count), BF)),
        query.reshape(count, heads * HD),
        far(cache_keys.reshape(rows * slots, kv)),
        far(cache_values.reshape(rows * slots, kv)),
        new_keys.reshape(count, kv),
        jnp.repeat(lengths, slots).reshape(groups, HD),
        flops=2 * count * heads * HD * HD * 3,
        moved=8 * 2**20,
    )
    step, distant_other, old, weights = lax.optimization_barrier((step, distant_other, old, weights))

    inner = call(inner_body, shape((tensor, rank, count), BF), step, a_turned, flat)
    inner = trade(inner, TENSOR)
    step_a, step_b, new_b = call(
        step_body, (shape((rank, width), F32), shape((rank, kv), F32), shape((rank, kv), BF)), step, adapter_b
    )
    base = call(
        base_body,
        shape((count, kv), F32),
        *map(far, (value_matrix.reshape(pairs, 2, width, kv), near, distant, near_other, distant_other)),
        flops=2 * count * tensor * width * kv,
        moved=4 * 2**20,
        in_specs=[pl.BlockSpec(memory_space=pl.ANY)] * 5,
        scratch_shapes=[
            pltpu.VMEM((pairs, 2, count, width), BF),
            pltpu.VMEM((pairs, 2, width, kv), BF),
            pltpu.SemaphoreType.DMA((pairs, 2, 2)),
        ],
    )

    attended = call(
        lambda *refs: last_body(groups, *refs),
        shape((rows, steps, heads * HD), BF),
        inner,
        new_b,
        base,
        old,
        weights,
    )
    return (step_a.T, step_b, attended)


def solution(mesh):
    sizes = (4, 4, 4, mesh.devices.shape[1] // 2, 2)
    fine = Mesh(mesh.devices.reshape(sizes), DP + TENSOR)
    return jax.shard_map(
        local,
        mesh=fine,
        in_specs=(
            P(DP, TENSOR),
            P(DP, TENSOR),
            P(TENSOR, None),
            P(None, TENSOR),
            P(TENSOR, None),
            P(TENSOR, None),
            P(None, TENSOR),
            P(None, TENSOR),
            P(None, TENSOR),
            P(DP, None, TENSOR),
            P(DP, None, TENSOR),
            P(DP, None, TENSOR),
            P(DP, None, TENSOR),
            P(DP, None, TENSOR),
            P(DP),
        ),
        out_specs=(P(TENSOR, None), P(None, TENSOR), P(DP, None, TENSOR)),
        check_vma=False,
    )
```

time: 109 us -> 101 us (0.927)
  local copies, waits for them, and re-layouts: 15.2 us -> 1.47 us
  waiting for transfers between devices: 12.7 us -> 23.1 us
  blocking collectives: 7.27 us -> 0 us
  Pallas kernels: 8.27 us -> 15.1 us
  other arithmetic: 4.21 us -> 0.02 us
    all_to_all x4 -> x5, waiting for transfers between devices: 10.7 us -> 21.7 us  [trade(): return lax.all_to_all(parts, axes, 0, 0, tiled=True)]
    unnamed x47 -> x23, local copies, waits for them, and re-layouts: 10.4 us -> 0.07 us
    all_to_all x1 -> x0, blocking collectives: 7.27 us -> none  [trade(): return lax.all_to_all(parts, axes, 0, 0, tiled=True)]
    pallas_call x9 -> x11, Pallas kernels: 8.27 us -> 15.1 us  [call(): pl.pallas_call(body, out_shape=out, cost_estimate=pl.CostEstimate(flops=f...]
    all_to_all x4 -> x5, starting transfers between devices: 30.3 us -> 33.7 us  [trade(): return lax.all_to_all(parts, axes, 0, 0, tiled=True)]
    ppermute x3 -> x2, starting transfers between devices: 8.99 us -> 6.1 us  [reach(): lax.ppermute(value, 'zl', [(i, i ^ hop) for i in range(lax.axis_size('zl'...]
    concatenate x4 -> x0, other arithmetic: 2.46 us -> none  [the longest x1 1.62 us: local(): step_a = jnp.concatenate([step_a[:, :rank], step_a[:, rank:]], axis=0)]
    dynamic_slice x2 -> x0, local copies, waits for them, and re-layouts: 1.68 us -> none  [the longest x1 0.96 us: piece(): low_rows = lax.dynamic_slice_in_dim(of_a, place * rows_a, rows_a, 0)]
  transfers between devices with their start and end apart: 11 -> 11, of which waited for: 3 -> 7; matrix products, arithmetic and copies ran while one was open for 10% -> 1% of each run, Pallas kernels for 7% -> 11%
where the time goes in v3:
time: 101 us; the launch traced here: 100 us
  starting transfers between devices  59.9 us (59%)
  waiting for transfers between devices  23.1 us (23%)
  Pallas kernels  15.1 us (15%)
  local copies, waits for them, and re-layouts  1.47 us (1%)
    all_to_all x5, starting transfers between devices, trade(): return lax.all_to_all(parts, axes, 0, 0, tiled=True)  33.7 us
    all_to_all x5, waiting for transfers between devices, trade(): return lax.all_to_all(parts, axes, 0, 0, tiled=True)  21.7 us
    ppermute x4, starting transfers between devices, swap(): return lax.ppermute(value, 'core', [(0, 1), (1, 0)])  20 us
    pallas_call x11, Pallas kernels, call(): pl.pallas_call(body, out_shape=out, cost_estimate=pl.CostEstimate(flops=f...  15.1 us
    ppermute x2, starting transfers between devices, reach(): lax.ppermute(value, 'zl', [(i, i ^ hop) for i in range(lax.axis_size('zl'...  6.1 us
  transfers between devices with their start and end apart: 11, of which 7 were waited for; matrix products, arithmetic and copies ran while one was open for 1% of the time, Pallas kernels for 11%

profile of v3, /device:TPU:1, one launch (start us, length us, event | category | flops | bytes accessed | tf_op | source)
XLA Modules:
  0.0 100.5 jit_solution(9669925924605150706)
XLA Ops:
  0.6 0.0 copy-start.2
  0.6 0.0 copy-start
  0.6 0.0 copy-start.6
  0.7 1.6 %shard_map.166 = (f32[128,128]{1,0:T(8,128)S(1)}, f32[128,128]{1,0:T(8,128)S(1)}) custom-call(bf16[256,1024]{1,0:T(8,128)(2,1)} %refs_0_.1, bf16[256,128]{1,0:T(8,128)(2,1)} %refs_1_.1, f32[64,1024]{1,0:T(8,128)} %bitcast.9, f32[64,128]{1,0:T(8,128)} %b_ref.3), custom_call_target="tpu_custom_call" | custom-call | tf_op jit(solution)/shard_map/pallas_call | solution.py:47
  2.3 8.8 %collective-permute-start = (f32[128,128]{1,0:T(8,128)S(1)}, f32[128,128]{1,0:T(8,128)S(1)}, u32[]{:S(2)}, u32[]{:S(2)}) collective-permute-start(f32[128,128]{1,0:T(8,128)S(1)} %get-tuple-element.32), channel_id=1, source_target_pairs={{0,1},{1,0},{2,3},{3,2},{4,5},{5,4},{6,7},{7,6},{8,9},{9,8},{10,11... | collective-permute-start | bytes 196616 | tf_op jit(solution)/shard_map/ppermute | solution.py:39
  11.0 1.0 %reshape.26.flat_ref = bf16[128,1024]{1,0:T(8,128)(2,1)S(1)} reshape(bf16[32,4,1024]{2,1,0:T(4,128)(2,1)} %param.24) | data formatting | bytes 524288 | tf_op jit(solution)/shard_map/reshape | solution.py:286
  12.1 0.0 collective-permute-done.theirs_ref
  12.1 0.7 shard_map.167
  12.7 3.3 %all-to-all-start = ((bf16[4,128,128]{2,1,0:T(8,128)(2,1)}), bf16[4,128,128]{2,1,0:T(8,128)(2,1)S(1)}, u32[]{:S(2)}, u32[]{:S(2)}) async-start(bf16[4,128,128]{2,1,0:T(8,128)(2,1)} %shard_map.167), calls=%async_computation | async-start | bytes 262144 | tf_op jit(solution)/shard_map/all_to_all | solution.py:35
  16.1 3.3 %collective-permute-start.2 = (bf16[1,128,1024]{2,1,0:T(8,128)(2,1)S(1)}, bf16[1,128,1024]{2,1,0:T(8,128)(2,1)S(1)}, u32[]{:S(2)}, u32[]{:S(2)}) collective-permute-start(bf16[1,128,1024]{2,1,0:T(8,128)(2,1)S(1)} %bitcast.11), channel_id=1, source_target_pairs={{0,2},{2,0},{4,6},{6,4},{1,3},{3,1},{5,7},{7,5},{8,10},{10,8},{12,... | collective-permute-start | bytes 786440 | tf_op jit(solution)/shard_map/ppermute | solution.py:43
  19.4 1.5 %all-to-all-done = bf16[4,128,128]{2,1,0:T(8,128)(2,1)S(1)} async-done(((bf16[4,128,128]{2,1,0:T(8,128)(2,1)}), bf16[4,128,128]{2,1,0:T(8,128)(2,1)S(1)}, u32[]{:S(2)}, u32[]{:S(2)}) %all-to-all-start) | async-done | bytes 131104 | tf_op jit(solution)/shard_map/all_to_all | solution.py:35
  21.0 3.7 %collective-permute-start.1 = (bf16[128,128]{1,0:T(8,128)(2,1)S(1)}, bf16[128,128]{1,0:T(8,128)(2,1)S(1)}, u32[]{:S(2)}, u32[]{:S(2)}) collective-permute-start(bf16[128,128]{1,0:T(8,128)(2,1)S(1)} %reduce_sum.12.refs_2_), channel_id=1, source_target_pairs={{0,1},{1,0},{2,3},{3,2},{4,5},{5,4},{6,7},{7,6},{8,9},{9,8},{10,11... | collective-permute-start | bytes 98312 | tf_op jit(solution)/shard_map/ppermute | solution.py:39
  24.7 0.0 copy-done.6
  24.7 0.1 broadcast_in_dim_reshape.3
  24.7 0.0 copy-start.10
  24.8 0.0 copy-start.9
  24.8 0.7 collective-permute-done.1.refs_3_
  25.5 0.0 copy-done.2
  25.5 0.0 copy-done
  25.5 1.0 shard_map.168
  26.5 0.0 copy-start.4
  26.5 0.6 collective-permute-done.2
  27.1 3.5 %all-to-all-start.1 = ((bf16[16,48,128]{2,1,0:T(8,128)(2,1)}), bf16[16,48,128]{2,1,0:T(8,128)(2,1)S(1)}, u32[]{:S(2)}, u32[]{:S(2)}) async-start(bf16[16,48,128]{2,1,0:T(8,128)(2,1)} %shard_map.168), calls=%async_computation.1 | async-start | bytes 393216 | tf_op jit(solution)/shard_map/all_to_all | solution.py:35
  30.6 0.0 copy-start.1
  30.7 0.0 copy-start.5
  30.7 2.8 %collective-permute-start.3 = (bf16[2,128,1024]{2,1,0:T(8,128)(2,1)S(1)}, bf16[2,128,1024]{2,1,0:T(8,128)(2,1)S(1)}, u32[]{:S(2)}, u32[]{:S(2)}) collective-permute-start(bf16[2,128,1024]{2,1,0:T(8,128)(2,1)S(1)} %constant_dynamic-update-slice_fusion.refs_0_), channel_id=1, source_target_pairs={{0,4},{2,6},{4,0},{6,2},{1,5},{3,7},{5,1},{7,3},{8,12},{10,14},{12... | collective-permute-start | bytes 1572872 | tf_op jit(solution)/shard_map/ppermute | solution.py:43
  33.5 4.2 %all-to-all-done.1.in_ref = bf16[16,48,128]{2,1,0:T(8,128)(2,1)S(1)} async-done(((bf16[16,48,128]{2,1,0:T(8,128)(2,1)}), bf16[16,48,128]{2,1,0:T(8,128)(2,1)S(1)}, u32[]{:S(2)}, u32[]{:S(2)}) %all-to-all-start.1) | async-done | bytes 196640 | tf_op jit(solution)/shard_map/all_to_all | solution.py:35
  37.7 0.7 shard_map.169
  38.3 0.0 copy-start.3
  38.4 4.2 %collective-permute-start.4 = (bf16[2,128,1024]{2,1,0:T(8,128)(2,1)S(1)}, bf16[2,128,1024]{2,1,0:T(8,128)(2,1)S(1)}, u32[]{:S(2)}, u32[]{:S(2)}) collective-permute-start(bf16[2,128,1024]{2,1,0:T(8,128)(2,1)S(1)} %constant_dynamic-update-slice_fusion.refs_0_), channel_id=1, source_target_pairs={{0,1},{1,0},{2,3},{3,2},{4,5},{5,4},{6,7},{7,6},{8,9},{9,8},{10,11... | collective-permute-start | bytes 1572872 | tf_op jit(solution)/shard_map/ppermute | solution.py:39
  42.6 12.5 %all-to-all-start.2 = ((f32[4,48,128]{2,1,0:T(8,128)}), f32[4,48,128]{2,1,0:T(8,128)S(1)}, u32[]{:S(2)}, u32[]{:S(2)}) async-start(f32[4,48,128]{2,1,0:T(8,128)} %shard_map.169), calls=%async_computation.2 | async-start | bytes 196608 | tf_op jit(solution)/shard_map/all_to_all | solution.py:35
  55.1 1.0 %shard_map.170 = (f32[48,128]{1,0:T(8,128)S(1)}, f32[48,128]{1,0:T(8,128)S(1)}) custom-call(f32[64,1024]{1,0:T(8,128)} %bitcast.16, f32[64,1024]{1,0:T(8,128)} %bitcast.17, f32[64,128]{1,0:T(8,128)} %moment_b_ref, f32[64,128]{1,0:T(8,128)} %second_b_ref), custom_call_target="tpu_custom_call" | custom-call | tf_op jit(solution)/shard_map/pallas_call | solution.py:47
  56.2 11.0 %all-to-all-done.2.in_ref = f32[4,48,128]{2,1,0:T(8,128)S(1)} async-done(((f32[4,48,128]{2,1,0:T(8,128)}), f32[4,48,128]{2,1,0:T(8,128)S(1)}, u32[]{:S(2)}, u32[]{:S(2)}) %all-to-all-start.2) | async-done | bytes 98336 | tf_op jit(solution)/shard_map/all_to_all | solution.py:35
  67.2 0.7 shard_map.171
  67.9 0.0 collective-permute-done.3.refs_1_
  67.9 0.0 copy-start.7
  67.9 0.0 collective-permute-done.4.refs_2_
  67.9 0.0 copy-start.8
  67.9 3.3 %collective-permute-start.5 = (bf16[2,128,1024]{2,1,0:T(8,128)(2,1)S(1)}, bf16[2,128,1024]{2,1,0:T(8,128)(2,1)}, u32[]{:S(2)}, u32[]{:S(2)}) collective-permute-start(bf16[2,128,1024]{2,1,0:T(8,128)(2,1)S(1)} %collective-permute-done.3.refs_1_), channel_id=1, source_target_pairs={{0,1},{1,0},{2,3},{3,2},{4,5},{5,4},{6,7},{7,6},{8,9},{9,8},{10,11... | collective-permute-start | bytes 1572872 | tf_op jit(solution)/shard_map/ppermute | solution.py:39
  71.2 3.5 %all-to-all-start.3 = ((bf16[16,48,128]{2,1,0:T(8,128)(2,1)}), bf16[16,48,128]{2,1,0:T(8,128)(2,1)S(1)}, u32[]{:S(2)}, u32[]{:S(2)}) async-start(bf16[16,48,128]{2,1,0:T(8,128)(2,1)} %shard_map.171), calls=%async_computation.3 | async-start | bytes 393216 | tf_op jit(solution)/shard_map/all_to_all | solution.py:35
  74.8 0.0 copy-done.10
  74.8 0.1 broadcast_in_dim.11
  74.9 0.1 broadcast_in_dim.12
  74.9 0.1 broadcast_in_dim.13.refs_4_
  75.0 0.0 copy-done.9
  75.0 0.1 reshape.27.refs_0_
  75.1 0.0 copy-done.4
  75.1 3.8 %shard_map.172 = (f32[1024,128]{1,0:T(8,128)S(1)}, bf16[1024,128]{1,0:T(8,128)(2,1)S(1)}) custom-call(bf16[128,1024]{1,0:T(8,128)(2,1)S(1)} %reshape.27.refs_0_, bf16[1024,128]{1,0:T(8,128)(2,1)} %bitcast.14, bf16[1024,128]{1,0:T(8,128)(2,1)} %bitcast.15, bf16[128,128]{1,0:T(8,128)(2,1)S(1)} %bitcast.12, s32[8,128]{1,0:T(8,128)S(1)} %broadcast_in_dim.13.refs_4_), custom_call_target="tpu_custom_call" | custom-call | flops 100663296 | bytes 8388608 | tf_op jit(solution)/shard_map/pallas_call | solution.py:47
  78.9 2.9 %all-to-all-done.3.step_ref = bf16[16,48,128]{2,1,0:T(8,128)(2,1)S(1)} async-done(((bf16[16,48,128]{2,1,0:T(8,128)(2,1)}), bf16[16,48,128]{2,1,0:T(8,128)(2,1)S(1)}, u32[]{:S(2)}, u32[]{:S(2)}) %all-to-all-start.3) | async-done | bytes 196640 | tf_op jit(solution)/shard_map/all_to_all | solution.py:35
  81.8 0.0 collective-permute-done.5.refs_3_
  81.8 0.0 copy-done.1
  81.8 0.9 shard_map.174
  82.7 0.0 copy-done.5
  82.7 10.8 %all-to-all-start.4 = ((bf16[8,64,128]{2,1,0:T(8,128)(2,1)}), bf16[8,64,128]{2,1,0:T(8,128)(2,1)S(1)}, u32[]{:S(2)}, u32[]{:S(2)}) async-start(bf16[8,64,128]{2,1,0:T(8,128)(2,1)} %shard_map.174), calls=%async_computation.4 | async-start | bytes 262144 | tf_op jit(solution)/shard_map/all_to_all | solution.py:35
  93.5 0.0 copy-done.3
  93.5 0.7 shard_map.173
  94.2 0.0 copy-done.7
  94.2 0.0 copy-done.8
  94.3 2.9 %shard_map.175.refs_2_ = f32[128,128]{1,0:T(8,128)S(1)} custom-call(bf16[4,2,1024,128]{3,2,1,0:T(8,128)(2,1)} %bitcast.13, bf16[2,128,1024]{2,1,0:T(8,128)(2,1)} %copy-done.5, bf16[2,128,1024]{2,1,0:T(8,128)(2,1)} %copy-done.7, bf16[2,128,1024]{2,1,0:T(8,128)(2,1)} %copy-done.8, bf16[2,128,1024]{2,1,0:T(8,128)(2,1)} %collective-permute-done.5.refs_3_), custom_call_target="tpu_custom_call" | custom-call | flops 268435456 | bytes 4194304 | tf_op jit(solution)/shard_map/pallas_call | solution.py:47
  97.2 2.1 %all-to-all-done.4.refs_0_ = bf16[8,64,128]{2,1,0:T(8,128)(2,1)S(1)} async-done(((bf16[8,64,128]{2,1,0:T(8,128)(2,1)}), bf16[8,64,128]{2,1,0:T(8,128)(2,1)S(1)}, u32[]{:S(2)}, u32[]{:S(2)}) %all-to-all-start.4) | async-done | bytes 131104 | tf_op jit(solution)/shard_map/all_to_all | solution.py:35
  99.3 1.1 %shard_map.176 = bf16[32,4,1024]{2,1,0:T(4,128)(2,1)} custom-call(bf16[8,64,128]{2,1,0:T(8,128)(2,1)S(1)} %all-to-all-done.4.refs_0_, bf16[64,128]{1,0:T(8,128)(2,1)S(1)} %get-tuple-element.54.refs_1_, f32[128,128]{1,0:T(8,128)S(1)} %shard_map.175.refs_2_, f32[1024,128]{1,0:T(8,128)S(1)} %get-tuple-element.57.refs_3_, ...), custom_call_target="tpu_custom_call" | custom-call | tf_op jit(solution)/shard_map/pallas_call | solution.py:47
  (3 shorter events, 0.1 us)
Async XLA Ops:
  0.6 24.9 %copy-start.2 = (bf16[256,128]{1,0:T(8,128)(2,1)S(1)}, bf16[256,128]{1,0:T(8,128)(2,1)}, u32[]{:S(2)}) copy-start(bf16[256,128]{1,0:T(8,128)(2,1)} %refs_1_.1) | copy-start | bytes 196612
  0.6 24.9 %copy-start = (bf16[256,1024]{1,0:T(8,128)(2,1)S(1)}, bf16[256,1024]{1,0:T(8,128)(2,1)}, u32[]{:S(2)}) copy-start(bf16[256,1024]{1,0:T(8,128)(2,1)} %refs_0_.1) | copy-start | bytes 1572868
  0.6 24.0 %copy-start.6 = (bf16[32,4,1024]{2,1,0:T(4,128)(2,1)S(1)}, bf16[32,4,1024]{2,1,0:T(4,128)(2,1)}, u32[]{:S(2)}) copy-start(bf16[32,4,1024]{2,1,0:T(4,128)(2,1)} %param.24) | copy-start | bytes 786436
  2.3 9.8 %collective-permute-start = (f32[128,128]{1,0:T(8,128)S(1)}, f32[128,128]{1,0:T(8,128)S(1)}, u32[]{:S(2)}, u32[]{:S(2)}) collective-permute-start(f32[128,128]{1,0:T(8,128)S(1)} %get-tuple-element.32), channel_id=1, source_target_pairs={{0,1},{1,0},{2,3},{3,2},{4,5},{5,4},{6,7},{7,6},{8,9},{9,8},{10,11... | collective-permute-start | bytes 196616 | tf_op jit(solution)/shard_map/ppermute | solution.py:39
  12.7 8.2 %all-to-all-start = ((bf16[4,128,128]{2,1,0:T(8,128)(2,1)}), bf16[4,128,128]{2,1,0:T(8,128)(2,1)S(1)}, u32[]{:S(2)}, u32[]{:S(2)}) async-start(bf16[4,128,128]{2,1,0:T(8,128)(2,1)} %shard_map.167), calls=%async_computation | async-start | bytes 262144 | tf_op jit(solution)/shard_map/all_to_all | solution.py:35
  16.1 11.0 %collective-permute-start.2 = (bf16[1,128,1024]{2,1,0:T(8,128)(2,1)S(1)}, bf16[1,128,1024]{2,1,0:T(8,128)(2,1)S(1)}, u32[]{:S(2)}, u32[]{:S(2)}) collective-permute-start(bf16[1,128,1024]{2,1,0:T(8,128)(2,1)S(1)} %bitcast.11), channel_id=1, source_target_pairs={{0,2},{2,0},{4,6},{6,4},{1,3},{3,1},{5,7},{7,5},{8,10},{10,8},{12,... | collective-permute-start | bytes 786440 | tf_op jit(solution)/shard_map/ppermute | solution.py:43
  21.0 4.5 %collective-permute-start.1 = (bf16[128,128]{1,0:T(8,128)(2,1)S(1)}, bf16[128,128]{1,0:T(8,128)(2,1)S(1)}, u32[]{:S(2)}, u32[]{:S(2)}) collective-permute-start(bf16[128,128]{1,0:T(8,128)(2,1)S(1)} %reduce_sum.12.refs_2_), channel_id=1, source_target_pairs={{0,1},{1,0},{2,3},{3,2},{4,5},{5,4},{6,7},{7,6},{8,9},{9,8},{10,11... | collective-permute-start | bytes 98312 | tf_op jit(solution)/shard_map/ppermute | solution.py:39
  24.7 50.0 %copy-start.10 = (s32[32]{0:T(128)S(1)}, s32[32]{0:T(128)}, u32[]{:S(2)}) copy-start(s32[32]{0:T(128)} %param.29) | copy-start | bytes 388
  24.8 50.3 %copy-start.9 = (bf16[32,4,1024]{2,1,0:T(4,128)(2,1)S(1)}, bf16[32,4,1024]{2,1,0:T(4,128)(2,1)}, u32[]{:S(2)}) copy-start(bf16[32,4,1024]{2,1,0:T(4,128)(2,1)} %param.26) | copy-start | bytes 786436
  26.5 48.6 %copy-start.4 = (bf16[32,4,128]{2,1,0:T(4,128)(2,1)S(1)}, bf16[32,4,128]{2,1,0:T(4,128)(2,1)}, u32[]{:S(2)}) copy-start(bf16[32,4,128]{2,1,0:T(4,128)(2,1)} %param.25) | copy-start | bytes 98308
  27.1 10.6 %all-to-all-start.1 = ((bf16[16,48,128]{2,1,0:T(8,128)(2,1)}), bf16[16,48,128]{2,1,0:T(8,128)(2,1)S(1)}, u32[]{:S(2)}, u32[]{:S(2)}) async-start(bf16[16,48,128]{2,1,0:T(8,128)(2,1)} %shard_map.168), calls=%async_computation.1 | async-start | bytes 393216 | tf_op jit(solution)/shard_map/all_to_all | solution.py:35
  30.6 51.2 %copy-start.1 = (f32[1024,64]{0,1:T(8,128)S(1)}, f32[1024,64]{0,1:T(8,128)}, u32[]{:S(2)}) copy-start(f32[1024,64]{0,1:T(8,128)} %param.17) | copy-start | bytes 786436
  30.7 52.0 %copy-start.5 = (bf16[2,128,1024]{2,1,0:T(8,128)(2,1)}, bf16[2,128,1024]{2,1,0:T(8,128)(2,1)S(1)}, u32[]{:S(2)}) copy-start(bf16[2,128,1024]{2,1,0:T(8,128)(2,1)S(1)} %constant_dynamic-update-slice_fusion.refs_0_) | copy-start | bytes 1572868
  30.7 37.1 %collective-permute-start.3 = (bf16[2,128,1024]{2,1,0:T(8,128)(2,1)S(1)}, bf16[2,128,1024]{2,1,0:T(8,128)(2,1)S(1)}, u32[]{:S(2)}, u32[]{:S(2)}) collective-permute-start(bf16[2,128,1024]{2,1,0:T(8,128)(2,1)S(1)} %constant_dynamic-update-slice_fusion.refs_0_), channel_id=1, source_target_pairs={{0,4},{2,6},{4,0},{6,2},{1,5},{3,7},{5,1},{7,3},{8,12},{10,14},{12... | collective-permute-start | bytes 1572872 | tf_op jit(solution)/shard_map/ppermute | solution.py:43
  38.3 55.2 %copy-start.3 = (f32[64,128]{1,0:T(8,128)S(1)}, f32[64,128]{1,0:T(8,128)}, u32[]{:S(2)}) copy-start(f32[64,128]{1,0:T(8,128)} %b_ref.3) | copy-start | bytes 98308
  38.4 29.5 %collective-permute-start.4 = (bf16[2,128,1024]{2,1,0:T(8,128)(2,1)S(1)}, bf16[2,128,1024]{2,1,0:T(8,128)(2,1)S(1)}, u32[]{:S(2)}, u32[]{:S(2)}) collective-permute-start(bf16[2,128,1024]{2,1,0:T(8,128)(2,1)S(1)} %constant_dynamic-update-slice_fusion.refs_0_), channel_id=1, source_target_pairs={{0,1},{1,0},{2,3},{3,2},{4,5},{5,4},{6,7},{7,6},{8,9},{9,8},{10,11... | collective-permute-start | bytes 1572872 | tf_op jit(solution)/shard_map/ppermute | solution.py:39
  42.6 24.6 %all-to-all-start.2 = ((f32[4,48,128]{2,1,0:T(8,128)}), f32[4,48,128]{2,1,0:T(8,128)S(1)}, u32[]{:S(2)}, u32[]{:S(2)}) async-start(f32[4,48,128]{2,1,0:T(8,128)} %shard_map.169), calls=%async_computation.2 | async-start | bytes 196608 | tf_op jit(solution)/shard_map/all_to_all | solution.py:35
  67.9 26.4 %copy-start.7 = (bf16[2,128,1024]{2,1,0:T(8,128)(2,1)}, bf16[2,128,1024]{2,1,0:T(8,128)(2,1)S(1)}, u32[]{:S(2)}) copy-start(bf16[2,128,1024]{2,1,0:T(8,128)(2,1)S(1)} %collective-permute-done.3.refs_1_) | copy-start | bytes 1572868
  67.9 26.4 %copy-start.8 = (bf16[2,128,1024]{2,1,0:T(8,128)(2,1)}, bf16[2,128,1024]{2,1,0:T(8,128)(2,1)S(1)}, u32[]{:S(2)}) copy-start(bf16[2,128,1024]{2,1,0:T(8,128)(2,1)S(1)} %collective-permute-done.4.refs_2_) | copy-start | bytes 1572868
  67.9 13.9 %collective-permute-start.5 = (bf16[2,128,1024]{2,1,0:T(8,128)(2,1)S(1)}, bf16[2,128,1024]{2,1,0:T(8,128)(2,1)}, u32[]{:S(2)}, u32[]{:S(2)}) collective-permute-start(bf16[2,128,1024]{2,1,0:T(8,128)(2,1)S(1)} %collective-permute-done.3.refs_1_), channel_id=1, source_target_pairs={{0,1},{1,0},{2,3},{3,2},{4,5},{5,4},{6,7},{7,6},{8,9},{9,8},{10,11... | collective-permute-start | bytes 1572872 | tf_op jit(solution)/shard_map/ppermute | solution.py:39
  71.2 10.6 %all-to-all-start.3 = ((bf16[16,48,128]{2,1,0:T(8,128)(2,1)}), bf16[16,48,128]{2,1,0:T(8,128)(2,1)S(1)}, u32[]{:S(2)}, u32[]{:S(2)}) async-start(bf16[16,48,128]{2,1,0:T(8,128)(2,1)} %shard_map.171), calls=%async_computation.3 | async-start | bytes 393216 | tf_op jit(solution)/shard_map/all_to_all | solution.py:35
  82.7 16.6 %all-to-all-start.4 = ((bf16[8,64,128]{2,1,0:T(8,128)(2,1)}), bf16[8,64,128]{2,1,0:T(8,128)(2,1)S(1)}, u32[]{:S(2)}, u32[]{:S(2)}) async-start(bf16[8,64,128]{2,1,0:T(8,128)(2,1)} %shard_map.174), calls=%async_computation.4 | async-start | bytes 262144 | tf_op jit(solution)/shard_map/all_to_all | solution.py:35

commit v4 on v3

--- a/solution.py
+++ b/solution.py
@@ -184,7 +184,7 @@
     half = chips // 2
     copies = []
     for i in range(chips):
-        place = lax.bitwise_xor(chip, i)
+        place = lax.bitwise_xor(chip, i // half + i % half * half)
         for j in range(2):
             copies.append(
                 (
@@ -283,7 +283,7 @@
     count = rows * steps
     slots = cache_keys.shape[1]
     two = 2 * rank
-    flat = decode_states.reshape(count, width)
+    flat = lax.optimization_barrier(decode_states.reshape(count, width))
     a_turned = adapter_a.T
 
     half = shape((tokens // 2, two), F32)
@@ -292,7 +292,7 @@
     pair = call(pair_body, shape((pairs, tokens // 2, two), BF), mine, swap(theirs))
 
     pair, send = lax.optimization_barrier((pair, flat))
-    next_chip = reach(send[None], 1)
+    second_chip = reach(send[None], 2)
     mine = jnp.sum(trade(pair, "zl").astype(F32), axis=0).astype(BF)
     theirs = swap(mine)
 
@@ -308,22 +308,20 @@
         theirs,
     )
 
-    block, mine_chip, next_chip = lax.optimization_barrier((block, flat[None], next_chip))
-    near = jnp.concatenate([mine_chip, next_chip], axis=0)
-    distant = reach(near, 2)
     shard = trade(block, PLANE)
+    near = jnp.concatenate([send[None], second_chip], axis=0)
+    distant = reach(near, 1)
     shard = call(sum_body, shape((lax.axis_size("zh"), deep, kv), F32), shard)
-    shard, near_sent, moments = lax.optimization_barrier(
-        (shard, near, (moment_a.T, second_a.T, moment_b, second_b))
+    shard, moments = lax.optimization_barrier(
+        (shard, (moment_a.T, second_a.T, moment_b, second_b))
     )
     shard = trade(shard, "zh")
-    near_other = swap(near_sent)
     piece = shape((deep, kv), F32)
     moments = call(shard_body, (piece, piece), *map(far, moments))
+    near_other = swap(near)
     step = call(adam_body, shape((plane, deep, kv), BF), shard, *moments)
-    step, distant, near_other, query = lax.optimization_barrier((step, distant, near_other, queries))
+    step, query = lax.optimization_barrier((step, queries))
     step = trade(step, PLANE)
-    distant_other = swap(distant)
     groups = rows * slots // HD
     heads = queries.shape[2] // HD
     old, weights = call(
@@ -337,7 +335,8 @@
         flops=2 * count * heads * HD * HD * 3,
         moved=8 * 2**20,
     )
-    step, distant_other, old, weights = lax.optimization_barrier((step, distant_other, old, weights))
+    step, old, weights = lax.optimization_barrier((step, old, weights))
+    distant_other = swap(distant)
 
     inner = call(inner_body, shape((tensor, rank, count), BF), step, a_turned, flat)
     inner = trade(inner, TENSOR)

time: 101 us -> 93.1 us (0.922)
  starting transfers between devices: 59.9 us -> 54.9 us
  waiting for transfers between devices: 23.1 us -> 19.1 us
    all_to_all x5, starting transfers between devices: 33.7 us -> 29.2 us  [trade(): return lax.all_to_all(parts, axes, 0, 0, tiled=True)]
    all_to_all x5, waiting for transfers between devices: 21.7 us -> 18.2 us  [trade(): return lax.all_to_all(parts, axes, 0, 0, tiled=True)]
  transfers between devices with their start and end apart: 11 -> 11, of which waited for: 7 -> 5; matrix products, arithmetic and copies ran while one was open for 1% -> 2% of each run, Pallas kernels for 11% -> 13%
where the time goes in v4:
time: 93.1 us; the launch traced here: 92.1 us
  starting transfers between devices  54.9 us (59%)
  waiting for transfers between devices  19.1 us (21%)
  Pallas kernels  15.1 us (16%)
  local copies, waits for them, and re-layouts  2.15 us (2%)
    all_to_all x5, starting transfers between devices, trade(): return lax.all_to_all(parts, axes, 0, 0, tiled=True)  29.2 us
    ppermute x4, starting transfers between devices, swap(): return lax.ppermute(value, 'core', [(0, 1), (1, 0)])  19.5 us
    all_to_all x5, waiting for transfers between devices, trade(): return lax.all_to_all(parts, axes, 0, 0, tiled=True)  18.2 us
    pallas_call x11, Pallas kernels, call(): pl.pallas_call(body, out_shape=out, cost_estimate=pl.CostEstimate(flops=f...  15.1 us
    ppermute x2, starting transfers between devices, reach(): lax.ppermute(value, 'zl', [(i, i ^ hop) for i in range(lax.axis_size('zl'...  6.14 us
  transfers between devices with their start and end apart: 11, of which 5 were waited for; matrix products, arithmetic and copies ran while one was open for 2% of the time, Pallas kernels for 13%

profile of v4, /device:TPU:1, one launch (start us, length us, event | category | flops | bytes accessed | tf_op | source)
XLA Modules:
  0.0 92.1 jit_solution(8033885185603098121)
XLA Ops:
  0.6 0.0 copy-start.2
  0.6 0.0 copy-start
  0.6 1.6 %shard_map.166 = (f32[128,128]{1,0:T(8,128)S(1)}, f32[128,128]{1,0:T(8,128)S(1)}) custom-call(bf16[256,1024]{1,0:T(8,128)(2,1)} %refs_0_.1, bf16[256,128]{1,0:T(8,128)(2,1)} %refs_1_.1, f32[64,1024]{1,0:T(8,128)} %bitcast.11, f32[64,128]{1,0:T(8,128)} %b_ref.3), custom_call_target="tpu_custom_call" | custom-call | tf_op jit(solution)/shard_map/pallas_call | solution.py:47
  2.2 8.8 %collective-permute-start = (f32[128,128]{1,0:T(8,128)S(1)}, f32[128,128]{1,0:T(8,128)S(1)}, u32[]{:S(2)}, u32[]{:S(2)}) collective-permute-start(f32[128,128]{1,0:T(8,128)S(1)} %get-tuple-element.25), channel_id=1, source_target_pairs={{0,1},{1,0},{2,3},{3,2},{4,5},{5,4},{6,7},{7,6},{8,9},{9,8},{10,11... | collective-permute-start | bytes 196616 | tf_op jit(solution)/shard_map/ppermute | solution.py:39
  11.0 1.0 %reshape.26.flat_ref = bf16[128,1024]{1,0:T(8,128)(2,1)S(1)} reshape(bf16[32,4,1024]{2,1,0:T(4,128)(2,1)} %param.24) | data formatting | bytes 524288 | tf_op jit(solution)/shard_map/reshape | solution.py:286
  12.0 0.0 collective-permute-done.theirs_ref
  12.1 0.7 shard_map.167
  12.7 3.3 %all-to-all-start = ((bf16[4,128,128]{2,1,0:T(8,128)(2,1)}), bf16[4,128,128]{2,1,0:T(8,128)(2,1)S(1)}, u32[]{:S(2)}, u32[]{:S(2)}) async-start(bf16[4,128,128]{2,1,0:T(8,128)(2,1)} %shard_map.167), calls=%async_computation | async-start | bytes 262144 | tf_op jit(solution)/shard_map/all_to_all | solution.py:35
  16.1 4.2 %collective-permute-start.2 = (bf16[1,128,1024]{2,1,0:T(8,128)(2,1)S(1)}, bf16[1,128,1024]{2,1,0:T(8,128)(2,1)S(1)}, u32[]{:S(2)}, u32[]{:S(2)}) collective-permute-start(bf16[1,128,1024]{2,1,0:T(8,128)(2,1)S(1)} %bitcast.9), channel_id=1, source_target_pairs={{0,4},{2,6},{4,0},{6,2},{1,5},{3,7},{5,1},{7,3},{8,12},{10,14},{12... | collective-permute-start | bytes 786440 | tf_op jit(solution)/shard_map/ppermute | solution.py:43
  20.3 0.6 all-to-all-done
  20.9 0.0 copy-start.9
  20.9 0.0 copy-start.8
  21.0 4.0 %collective-permute-start.1 = (bf16[128,128]{1,0:T(8,128)(2,1)S(1)}, bf16[128,128]{1,0:T(8,128)(2,1)S(1)}, u32[]{:S(2)}, u32[]{:S(2)}) collective-permute-start(bf16[128,128]{1,0:T(8,128)(2,1)S(1)} %reduce_sum.12.refs_2_), channel_id=1, source_target_pairs={{0,1},{1,0},{2,3},{3,2},{4,5},{5,4},{6,7},{7,6},{8,9},{9,8},{10,11... | collective-permute-start | bytes 98312 | tf_op jit(solution)/shard_map/ppermute | solution.py:39
  24.9 0.8 collective-permute-done.1.refs_3_
  25.8 0.0 copy-done.2
  25.8 0.0 copy-done
  25.8 1.0 %shard_map.168 = bf16[16,48,128]{2,1,0:T(8,128)(2,1)} custom-call(bf16[256,1024]{1,0:T(8,128)(2,1)S(1)} %copy-done, bf16[256,128]{1,0:T(8,128)(2,1)S(1)} %copy-done.2, bf16[128,128]{1,0:T(8,128)(2,1)S(1)} %reduce_sum.12.refs_2_, bf16[128,128]{1,0:T(8,128)(2,1)S(1)} %collective-permute-done.1.refs_3_), custom_call_target="tpu_custom_call" | custom-call | tf_op jit(solution)/shard_map/pallas_call | solution.py:47
  26.7 0.0 copy-start.4
  26.7 10.2 %all-to-all-start.1 = ((bf16[16,48,128]{2,1,0:T(8,128)(2,1)}), bf16[16,48,128]{2,1,0:T(8,128)(2,1)S(1)}, u32[]{:S(2)}, u32[]{:S(2)}) async-start(bf16[16,48,128]{2,1,0:T(8,128)(2,1)} %shard_map.168), calls=%async_computation.1 | async-start | bytes 393216 | tf_op jit(solution)/shard_map/all_to_all | solution.py:35
  37.0 0.0 copy-start.1
  37.0 0.0 collective-permute-done.2
  37.0 0.1 pad_maximum_fusion.refs_0_
  37.1 0.0 copy-start.5
  37.1 1.9 %collective-permute-start.3 = (bf16[2,128,1024]{2,1,0:T(8,128)(2,1)S(1)}, bf16[2,128,1024]{2,1,0:T(8,128)(2,1)S(1)}, u32[]{:S(2)}, u32[]{:S(2)}) collective-permute-start(bf16[2,128,1024]{2,1,0:T(8,128)(2,1)S(1)} %pad_maximum_fusion.refs_0_), channel_id=1, source_target_pairs={{0,2},{2,0},{4,6},{6,4},{1,3},{3,1},{5,7},{7,5},{8,10},{10,8},{12,... | collective-permute-start | bytes 1572872 | tf_op jit(solution)/shard_map/ppermute | solution.py:43
  39.0 5.0 %all-to-all-done.1.in_ref = bf16[16,48,128]{2,1,0:T(8,128)(2,1)S(1)} async-done(((bf16[16,48,128]{2,1,0:T(8,128)(2,1)}), bf16[16,48,128]{2,1,0:T(8,128)(2,1)S(1)}, u32[]{:S(2)}, u32[]{:S(2)}) %all-to-all-start.1) | async-done | bytes 196640 | tf_op jit(solution)/shard_map/all_to_all | solution.py:35
  44.0 0.7 shard_map.169
  44.7 0.0 copy-start.3
  44.7 8.3 %all-to-all-start.2 = ((f32[4,48,128]{2,1,0:T(8,128)}), f32[4,48,128]{2,1,0:T(8,128)S(1)}, u32[]{:S(2)}, u32[]{:S(2)}) async-start(f32[4,48,128]{2,1,0:T(8,128)} %shard_map.169), calls=%async_computation.2 | async-start | bytes 196608 | tf_op jit(solution)/shard_map/all_to_all | solution.py:35
  53.0 1.0 %shard_map.170 = (f32[48,128]{1,0:T(8,128)S(1)}, f32[48,128]{1,0:T(8,128)S(1)}) custom-call(f32[64,1024]{1,0:T(8,128)} %bitcast.17, f32[64,1024]{1,0:T(8,128)} %bitcast.18, f32[64,128]{1,0:T(8,128)} %moment_b_ref, f32[64,128]{1,0:T(8,128)} %second_b_ref), custom_call_target="tpu_custom_call" | custom-call | tf_op jit(solution)/shard_map/pallas_call | solution.py:47
  54.1 11.2 %all-to-all-done.2.in_ref = f32[4,48,128]{2,1,0:T(8,128)S(1)} async-done(((f32[4,48,128]{2,1,0:T(8,128)}), f32[4,48,128]{2,1,0:T(8,128)S(1)}, u32[]{:S(2)}, u32[]{:S(2)}) %all-to-all-start.2) | async-done | bytes 98336 | tf_op jit(solution)/shard_map/all_to_all | solution.py:35
  65.3 0.7 shard_map.171
  66.0 3.5 %all-to-all-start.3 = ((bf16[16,48,128]{2,1,0:T(8,128)(2,1)}), bf16[16,48,128]{2,1,0:T(8,128)(2,1)S(1)}, u32[]{:S(2)}, u32[]{:S(2)}) async-start(bf16[16,48,128]{2,1,0:T(8,128)(2,1)} %shard_map.171), calls=%async_computation.3 | async-start | bytes 393216 | tf_op jit(solution)/shard_map/all_to_all | solution.py:35
  69.6 4.9 %collective-permute-start.4 = (bf16[2,128,1024]{2,1,0:T(8,128)(2,1)S(1)}, bf16[2,128,1024]{2,1,0:T(8,128)(2,1)S(1)}, u32[]{:S(2)}, u32[]{:S(2)}) collective-permute-start(bf16[2,128,1024]{2,1,0:T(8,128)(2,1)S(1)} %pad_maximum_fusion.refs_0_), channel_id=1, source_target_pairs={{0,1},{1,0},{2,3},{3,2},{4,5},{5,4},{6,7},{7,6},{8,9},{9,8},{10,11... | collective-permute-start | bytes 1572872 | tf_op jit(solution)/shard_map/ppermute | solution.py:39
  74.4 0.0 collective-permute-done.3.refs_1_
  74.4 0.0 copy-start.6
  74.4 1.9 %collective-permute-start.5 = (bf16[2,128,1024]{2,1,0:T(8,128)(2,1)S(1)}, bf16[2,128,1024]{2,1,0:T(8,128)(2,1)}, u32[]{:S(2)}, u32[]{:S(2)}) collective-permute-start(bf16[2,128,1024]{2,1,0:T(8,128)(2,1)S(1)} %collective-permute-done.3.refs_1_), channel_id=1, source_target_pairs={{0,1},{1,0},{2,3},{3,2},{4,5},{5,4},{6,7},{7,6},{8,9},{9,8},{10,11... | collective-permute-start | bytes 1572872 | tf_op jit(solution)/shard_map/ppermute | solution.py:39
  76.4 0.0 copy-done.9
  76.4 0.1 broadcast_in_dim.11
  76.5 0.1 broadcast_in_dim.12
  76.5 0.1 broadcast_in_dim.13.refs_4_
  76.6 0.0 copy-done.8
  76.6 0.1 reshape.27.refs_0_
  76.7 0.0 copy-done.4
  76.7 3.8 %shard_map.172 = (f32[1024,128]{1,0:T(8,128)S(1)}, bf16[1024,128]{1,0:T(8,128)(2,1)S(1)}) custom-call(bf16[128,1024]{1,0:T(8,128)(2,1)S(1)} %reshape.27.refs_0_, bf16[1024,128]{1,0:T(8,128)(2,1)} %bitcast.15, bf16[1024,128]{1,0:T(8,128)(2,1)} %bitcast.16, bf16[128,128]{1,0:T(8,128)(2,1)S(1)} %bitcast.13, s32[8,128]{1,0:T(8,128)S(1)} %broadcast_in_dim.13.refs_4_), custom_call_target="tpu_custom_call" | custom-call | flops 100663296 | bytes 8388608 | tf_op jit(solution)/shard_map/pallas_call | solution.py:47
  80.5 0.0 all-to-all-done.3.step_ref
  80.5 0.0 copy-done.1
  80.5 0.9 shard_map.174
  81.4 0.0 copy-done.5
  81.4 3.8 %all-to-all-start.4 = ((bf16[8,64,128]{2,1,0:T(8,128)(2,1)}), bf16[8,64,128]{2,1,0:T(8,128)(2,1)S(1)}, u32[]{:S(2)}, u32[]{:S(2)}) async-start(bf16[8,64,128]{2,1,0:T(8,128)(2,1)} %shard_map.174), calls=%async_computation.4 | async-start | bytes 262144 | tf_op jit(solution)/shard_map/all_to_all | solution.py:35
  85.2 0.0 copy-done.3
  85.2 0.7 shard_map.173
  85.9 0.0 collective-permute-done.4.refs_2_
  85.9 0.0 copy-start.7
  85.9 0.0 collective-permute-done.5.refs_3_
  85.9 0.0 copy-done.6
  85.9 0.8 copy-done.7
  86.7 2.9 %shard_map.175.refs_2_ = f32[128,128]{1,0:T(8,128)S(1)} custom-call(bf16[4,2,1024,128]{3,2,1,0:T(8,128)(2,1)} %bitcast.14, bf16[2,128,1024]{2,1,0:T(8,128)(2,1)} %copy-done.5, bf16[2,128,1024]{2,1,0:T(8,128)(2,1)} %copy-done.6, bf16[2,128,1024]{2,1,0:T(8,128)(2,1)} %copy-done.7, bf16[2,128,1024]{2,1,0:T(8,128)(2,1)} %collective-permute-done.5.refs_3_), custom_call_target="tpu_custom_call" | custom-call | flops 268435456 | bytes 4194304 | tf_op jit(solution)/shard_map/pallas_call | solution.py:47
  89.6 1.4 %all-to-all-done.4.refs_0_ = bf16[8,64,128]{2,1,0:T(8,128)(2,1)S(1)} async-done(((bf16[8,64,128]{2,1,0:T(8,128)(2,1)}), bf16[8,64,128]{2,1,0:T(8,128)(2,1)S(1)}, u32[]{:S(2)}, u32[]{:S(2)}) %all-to-all-start.4) | async-done | bytes 131104 | tf_op jit(solution)/shard_map/all_to_all | solution.py:35
  91.0 1.1 %shard_map.176 = bf16[32,4,1024]{2,1,0:T(4,128)(2,1)} custom-call(bf16[8,64,128]{2,1,0:T(8,128)(2,1)S(1)} %all-to-all-done.4.refs_0_, bf16[64,128]{1,0:T(8,128)(2,1)S(1)} %get-tuple-element.41.refs_1_, f32[128,128]{1,0:T(8,128)S(1)} %shard_map.175.refs_2_, f32[1024,128]{1,0:T(8,128)S(1)} %get-tuple-element.43.refs_3_, ...), custom_call_target="tpu_custom_call" | custom-call | tf_op jit(solution)/shard_map/pallas_call | solution.py:47
  (1 shorter events, 0.0 us)
Async XLA Ops:
  0.6 25.1 %copy-start.2 = (bf16[256,128]{1,0:T(8,128)(2,1)S(1)}, bf16[256,128]{1,0:T(8,128)(2,1)}, u32[]{:S(2)}) copy-start(bf16[256,128]{1,0:T(8,128)(2,1)} %refs_1_.1) | copy-start | bytes 196612
  0.6 25.1 %copy-start = (bf16[256,1024]{1,0:T(8,128)(2,1)S(1)}, bf16[256,1024]{1,0:T(8,128)(2,1)}, u32[]{:S(2)}) copy-start(bf16[256,1024]{1,0:T(8,128)(2,1)} %refs_0_.1) | copy-start | bytes 1572868
  2.2 9.8 %collective-permute-start = (f32[128,128]{1,0:T(8,128)S(1)}, f32[128,128]{1,0:T(8,128)S(1)}, u32[]{:S(2)}, u32[]{:S(2)}) collective-permute-start(f32[128,128]{1,0:T(8,128)S(1)} %get-tuple-element.25), channel_id=1, source_target_pairs={{0,1},{1,0},{2,3},{3,2},{4,5},{5,4},{6,7},{7,6},{8,9},{9,8},{10,11... | collective-permute-start | bytes 196616 | tf_op jit(solution)/shard_map/ppermute | solution.py:39
  12.7 8.2 %all-to-all-start = ((bf16[4,128,128]{2,1,0:T(8,128)(2,1)}), bf16[4,128,128]{2,1,0:T(8,128)(2,1)S(1)}, u32[]{:S(2)}, u32[]{:S(2)}) async-start(bf16[4,128,128]{2,1,0:T(8,128)(2,1)} %shard_map.167), calls=%async_computation | async-start | bytes 262144 | tf_op jit(solution)/shard_map/all_to_all | solution.py:35
  16.1 20.9 %collective-permute-start.2 = (bf16[1,128,1024]{2,1,0:T(8,128)(2,1)S(1)}, bf16[1,128,1024]{2,1,0:T(8,128)(2,1)S(1)}, u32[]{:S(2)}, u32[]{:S(2)}) collective-permute-start(bf16[1,128,1024]{2,1,0:T(8,128)(2,1)S(1)} %bitcast.9), channel_id=1, source_target_pairs={{0,4},{2,6},{4,0},{6,2},{1,5},{3,7},{5,1},{7,3},{8,12},{10,14},{12... | collective-permute-start | bytes 786440 | tf_op jit(solution)/shard_map/ppermute | solution.py:43
  20.9 55.5 %copy-start.9 = (s32[32]{0:T(128)S(1)}, s32[32]{0:T(128)}, u32[]{:S(2)}) copy-start(s32[32]{0:T(128)} %param.29) | copy-start | bytes 388
  20.9 55.7 %copy-start.8 = (bf16[32,4,1024]{2,1,0:T(4,128)(2,1)S(1)}, bf16[32,4,1024]{2,1,0:T(4,128)(2,1)}, u32[]{:S(2)}) copy-start(bf16[32,4,1024]{2,1,0:T(4,128)(2,1)} %param.26) | copy-start | bytes 786436
  21.0 4.8 %collective-permute-start.1 = (bf16[128,128]{1,0:T(8,128)(2,1)S(1)}, bf16[128,128]{1,0:T(8,128)(2,1)S(1)}, u32[]{:S(2)}, u32[]{:S(2)}) collective-permute-start(bf16[128,128]{1,0:T(8,128)(2,1)S(1)} %reduce_sum.12.refs_2_), channel_id=1, source_target_pairs={{0,1},{1,0},{2,3},{3,2},{4,5},{5,4},{6,7},{7,6},{8,9},{9,8},{10,11... | collective-permute-start | bytes 98312 | tf_op jit(solution)/shard_map/ppermute | solution.py:39
  26.7 50.0 %copy-start.4 = (bf16[32,4,128]{2,1,0:T(4,128)(2,1)S(1)}, bf16[32,4,128]{2,1,0:T(4,128)(2,1)}, u32[]{:S(2)}) copy-start(bf16[32,4,128]{2,1,0:T(4,128)(2,1)} %param.25) | copy-start | bytes 98308
  26.7 17.3 %all-to-all-start.1 = ((bf16[16,48,128]{2,1,0:T(8,128)(2,1)}), bf16[16,48,128]{2,1,0:T(8,128)(2,1)S(1)}, u32[]{:S(2)}, u32[]{:S(2)}) async-start(bf16[16,48,128]{2,1,0:T(8,128)(2,1)} %shard_map.168), calls=%async_computation.1 | async-start | bytes 393216 | tf_op jit(solution)/shard_map/all_to_all | solution.py:35
  37.0 43.5 %copy-start.1 = (f32[1024,64]{0,1:T(8,128)S(1)}, f32[1024,64]{0,1:T(8,128)}, u32[]{:S(2)}) copy-start(f32[1024,64]{0,1:T(8,128)} %param.17) | copy-start | bytes 786436
  37.1 44.3 %copy-start.5 = (bf16[2,128,1024]{2,1,0:T(8,128)(2,1)}, bf16[2,128,1024]{2,1,0:T(8,128)(2,1)S(1)}, u32[]{:S(2)}) copy-start(bf16[2,128,1024]{2,1,0:T(8,128)(2,1)S(1)} %pad_maximum_fusion.refs_0_) | copy-start | bytes 1572868
  37.1 37.3 %collective-permute-start.3 = (bf16[2,128,1024]{2,1,0:T(8,128)(2,1)S(1)}, bf16[2,128,1024]{2,1,0:T(8,128)(2,1)S(1)}, u32[]{:S(2)}, u32[]{:S(2)}) collective-permute-start(bf16[2,128,1024]{2,1,0:T(8,128)(2,1)S(1)} %pad_maximum_fusion.refs_0_), channel_id=1, source_target_pairs={{0,2},{2,0},{4,6},{6,4},{1,3},{3,1},{5,7},{7,5},{8,10},{10,8},{12,... | collective-permute-start | bytes 1572872 | tf_op jit(solution)/shard_map/ppermute | solution.py:43
  44.7 40.5 %copy-start.3 = (f32[64,128]{1,0:T(8,128)S(1)}, f32[64,128]{1,0:T(8,128)}, u32[]{:S(2)}) copy-start(f32[64,128]{1,0:T(8,128)} %b_ref.3) | copy-start | bytes 98308
  44.7 20.6 %all-to-all-start.2 = ((f32[4,48,128]{2,1,0:T(8,128)}), f32[4,48,128]{2,1,0:T(8,128)S(1)}, u32[]{:S(2)}, u32[]{:S(2)}) async-start(f32[4,48,128]{2,1,0:T(8,128)} %shard_map.169), calls=%async_computation.2 | async-start | bytes 196608 | tf_op jit(solution)/shard_map/all_to_all | solution.py:35
  66.0 14.5 %all-to-all-start.3 = ((bf16[16,48,128]{2,1,0:T(8,128)(2,1)}), bf16[16,48,128]{2,1,0:T(8,128)(2,1)S(1)}, u32[]{:S(2)}, u32[]{:S(2)}) async-start(bf16[16,48,128]{2,1,0:T(8,128)(2,1)} %shard_map.171), calls=%async_computation.3 | async-start | bytes 393216 | tf_op jit(solution)/shard_map/all_to_all | solution.py:35
  69.6 16.3 %collective-permute-start.4 = (bf16[2,128,1024]{2,1,0:T(8,128)(2,1)S(1)}, bf16[2,128,1024]{2,1,0:T(8,128)(2,1)S(1)}, u32[]{:S(2)}, u32[]{:S(2)}) collective-permute-start(bf16[2,128,1024]{2,1,0:T(8,128)(2,1)S(1)} %pad_maximum_fusion.refs_0_), channel_id=1, source_target_pairs={{0,1},{1,0},{2,3},{3,2},{4,5},{5,4},{6,7},{7,6},{8,9},{9,8},{10,11... | collective-permute-start | bytes 1572872 | tf_op jit(solution)/shard_map/ppermute | solution.py:39
  74.4 11.5 %copy-start.6 = (bf16[2,128,1024]{2,1,0:T(8,128)(2,1)}, bf16[2,128,1024]{2,1,0:T(8,128)(2,1)S(1)}, u32[]{:S(2)}) copy-start(bf16[2,128,1024]{2,1,0:T(8,128)(2,1)S(1)} %collective-permute-done.3.refs_1_) | copy-start | bytes 1572868
  74.4 11.5 %collective-permute-start.5 = (bf16[2,128,1024]{2,1,0:T(8,128)(2,1)S(1)}, bf16[2,128,1024]{2,1,0:T(8,128)(2,1)}, u32[]{:S(2)}, u32[]{:S(2)}) collective-permute-start(bf16[2,128,1024]{2,1,0:T(8,128)(2,1)S(1)} %collective-permute-done.3.refs_1_), channel_id=1, source_target_pairs={{0,1},{1,0},{2,3},{3,2},{4,5},{5,4},{6,7},{7,6},{8,9},{9,8},{10,11... | collective-permute-start | bytes 1572872 | tf_op jit(solution)/shard_map/ppermute | solution.py:39
  81.4 9.6 %all-to-all-start.4 = ((bf16[8,64,128]{2,1,0:T(8,128)(2,1)}), bf16[8,64,128]{2,1,0:T(8,128)(2,1)S(1)}, u32[]{:S(2)}, u32[]{:S(2)}) async-start(bf16[8,64,128]{2,1,0:T(8,128)(2,1)} %shard_map.174), calls=%async_computation.4 | async-start | bytes 262144 | tf_op jit(solution)/shard_map/all_to_all | solution.py:35
  85.9 0.8 copy-start.7

commit v5 on v4

--- a/solution.py
+++ b/solution.py
@@ -312,31 +312,31 @@
     near = jnp.concatenate([send[None], second_chip], axis=0)
     distant = reach(near, 1)
     shard = call(sum_body, shape((lax.axis_size("zh"), deep, kv), F32), shard)
-    shard, moments = lax.optimization_barrier(
-        (shard, (moment_a.T, second_a.T, moment_b, second_b))
+    shard, query, moments = lax.optimization_barrier(
+        (shard, queries, (moment_a.T, second_a.T, moment_b, second_b))
     )
     shard = trade(shard, "zh")
     piece = shape((deep, kv), F32)
     moments = call(shard_body, (piece, piece), *map(far, moments))
-    near_other = swap(near)
-    step = call(adam_body, shape((plane, deep, kv), BF), shard, *moments)
-    step, query = lax.optimization_barrier((step, queries))
-    step = trade(step, PLANE)
+
     groups = rows * slots // HD
     heads = queries.shape[2] // HD
     old, weights = call(
         lambda *refs: cache_body(steps, *refs),
         (shape((count * heads, HD), F32), shape((count * heads, count), BF)),
         query.reshape(count, heads * HD),
-        far(cache_keys.reshape(rows * slots, kv)),
-        far(cache_values.reshape(rows * slots, kv)),
+        cache_keys.reshape(rows * slots, kv),
+        cache_values.reshape(rows * slots, kv),
         new_keys.reshape(count, kv),
         jnp.repeat(lengths, slots).reshape(groups, HD),
         flops=2 * count * heads * HD * HD * 3,
         moved=8 * 2**20,
     )
-    step, old, weights = lax.optimization_barrier((step, old, weights))
-    distant_other = swap(distant)
+    shard, old, weights = lax.optimization_barrier((shard, old, weights))
+    step = call(adam_body, shape((plane, deep, kv), BF), shard, *moments)
+    distant_sent, near_sent, _ = lax.optimization_barrier((distant, near, step))
+    distant_other, near_other = swap(distant_sent), swap(near_sent)
+    step = trade(step, PLANE)
 
     inner = call(inner_body, shape((tensor, rank, count), BF), step, a_turned, flat)
     inner = trade(inner, TENSOR)

time: 93.1 us -> 92.3 us (level)
  starting transfers between devices: 54.9 us -> 58.2 us
  waiting for transfers between devices: 19.1 us -> 16.1 us
  Pallas kernels: 15.1 us -> 14.1 us
    all_to_all x5, starting transfers between devices: 29.2 us -> 32.5 us  [trade(): return lax.all_to_all(parts, axes, 0, 0, tiled=True)]
    all_to_all x5, waiting for transfers between devices: 18.2 us -> 15.2 us  [trade(): return lax.all_to_all(parts, axes, 0, 0, tiled=True)]
    pallas_call x11, Pallas kernels: 15.1 us -> 14.1 us  [call(): pl.pallas_call(body, out_shape=out, cost_estimate=pl.CostEstimate(flops=f...]
  transfers between devices with their start and end apart: 11 -> 11, of which waited for: 5 -> 6; matrix products, arithmetic and copies ran while one was open for 2% -> 2% of each run, Pallas kernels for 13% -> 12%
where the time goes in v5:
time: 92.3 us; the launch traced here: 91.5 us
  starting transfers between devices  58.2 us (63%)
  waiting for transfers between devices  16.1 us (17%)
  Pallas kernels  14.1 us (15%)
  local copies, waits for them, and re-layouts  2.16 us (2%)
    all_to_all x5, starting transfers between devices, trade(): return lax.all_to_all(parts, axes, 0, 0, tiled=True)  32.5 us
    ppermute x4, starting transfers between devices, swap(): return lax.ppermute(value, 'core', [(0, 1), (1, 0)])  19.4 us
    all_to_all x5, waiting for transfers between devices, trade(): return lax.all_to_all(parts, axes, 0, 0, tiled=True)  15.2 us
    pallas_call x11, Pallas kernels, call(): pl.pallas_call(body, out_shape=out, cost_estimate=pl.CostEstimate(flops=f...  14.1 us
    ppermute x2, starting transfers between devices, reach(): lax.ppermute(value, 'zl', [(i, i ^ hop) for i in range(lax.axis_size('zl'...  6.25 us
  transfers between devices with their start and end apart: 11, of which 6 were waited for; matrix products, arithmetic and copies ran while one was open for 2% of the time, Pallas kernels for 12%

profile of v5, /device:TPU:1, one launch (start us, length us, event | category | flops | bytes accessed | tf_op | source)
XLA Modules:
  0.0 91.5 jit_solution(12927357070097873448)
XLA Ops:
  0.6 0.0 copy-start.4
  0.6 0.0 copy-start
  0.6 1.6 %shard_map.166 = (f32[128,128]{1,0:T(8,128)S(1)}, f32[128,128]{1,0:T(8,128)S(1)}) custom-call(bf16[256,1024]{1,0:T(8,128)(2,1)} %refs_0_.1, bf16[256,128]{1,0:T(8,128)(2,1)} %refs_1_.1, f32[64,1024]{1,0:T(8,128)} %bitcast.11, f32[64,128]{1,0:T(8,128)} %b_ref.3), custom_call_target="tpu_custom_call" | custom-call | tf_op jit(solution)/shard_map/pallas_call | solution.py:47
  2.2 0.0 copy-start.11
  2.2 0.0 copy-start.10
  2.3 8.9 %collective-permute-start = (f32[128,128]{1,0:T(8,128)S(1)}, f32[128,128]{1,0:T(8,128)S(1)}, u32[]{:S(2)}, u32[]{:S(2)}) collective-permute-start(f32[128,128]{1,0:T(8,128)S(1)} %get-tuple-element.26), channel_id=1, source_target_pairs={{0,1},{1,0},{2,3},{3,2},{4,5},{5,4},{6,7},{7,6},{8,9},{9,8},{10,11... | collective-permute-start | bytes 196616 | tf_op jit(solution)/shard_map/ppermute | solution.py:39
  11.2 1.0 %reshape.26.flat_ref = bf16[128,1024]{1,0:T(8,128)(2,1)S(1)} reshape(bf16[32,4,1024]{2,1,0:T(4,128)(2,1)} %param.24) | data formatting | bytes 524288 | tf_op jit(solution)/shard_map/reshape | solution.py:286
  12.2 0.0 collective-permute-done.theirs_ref
  12.2 0.7 shard_map.167
  12.9 3.3 %all-to-all-start = ((bf16[4,128,128]{2,1,0:T(8,128)(2,1)}), bf16[4,128,128]{2,1,0:T(8,128)(2,1)S(1)}, u32[]{:S(2)}, u32[]{:S(2)}) async-start(bf16[4,128,128]{2,1,0:T(8,128)(2,1)} %shard_map.167), calls=%async_computation | async-start | bytes 262144 | tf_op jit(solution)/shard_map/all_to_all | solution.py:35
  16.2 0.0 copy-start.2
  16.2 0.0 copy-start.3
  16.2 0.0 copy-start.6
  16.2 4.3 %collective-permute-start.2 = (bf16[1,128,1024]{2,1,0:T(8,128)(2,1)S(1)}, bf16[1,128,1024]{2,1,0:T(8,128)(2,1)S(1)}, u32[]{:S(2)}, u32[]{:S(2)}) collective-permute-start(bf16[1,128,1024]{2,1,0:T(8,128)(2,1)S(1)} %bitcast.9), channel_id=1, source_target_pairs={{0,4},{2,6},{4,0},{6,2},{1,5},{3,7},{5,1},{7,3},{8,12},{10,14},{12... | collective-permute-start | bytes 786440 | tf_op jit(solution)/shard_map/ppermute | solution.py:43
  20.6 0.5 all-to-all-done
  21.1 3.8 %collective-permute-start.1 = (bf16[128,128]{1,0:T(8,128)(2,1)S(1)}, bf16[128,128]{1,0:T(8,128)(2,1)S(1)}, u32[]{:S(2)}, u32[]{:S(2)}) collective-permute-start(bf16[128,128]{1,0:T(8,128)(2,1)S(1)} %reduce_sum.12.refs_2_), channel_id=1, source_target_pairs={{0,1},{1,0},{2,3},{3,2},{4,5},{5,4},{6,7},{7,6},{8,9},{9,8},{10,11... | collective-permute-start | bytes 98312 | tf_op jit(solution)/shard_map/ppermute | solution.py:39
  24.9 0.8 collective-permute-done.1.refs_3_
  25.7 0.0 copy-done.4
  25.7 0.0 copy-done
  25.8 1.0 %shard_map.168 = bf16[16,48,128]{2,1,0:T(8,128)(2,1)} custom-call(bf16[256,1024]{1,0:T(8,128)(2,1)S(1)} %copy-done, bf16[256,128]{1,0:T(8,128)(2,1)S(1)} %copy-done.4, bf16[128,128]{1,0:T(8,128)(2,1)S(1)} %reduce_sum.12.refs_2_, bf16[128,128]{1,0:T(8,128)(2,1)S(1)} %collective-permute-done.1.refs_3_), custom_call_target="tpu_custom_call" | custom-call | tf_op jit(solution)/shard_map/pallas_call | solution.py:47
  26.7 10.1 %all-to-all-start.1 = ((bf16[16,48,128]{2,1,0:T(8,128)(2,1)}), bf16[16,48,128]{2,1,0:T(8,128)(2,1)S(1)}, u32[]{:S(2)}, u32[]{:S(2)}) async-start(bf16[16,48,128]{2,1,0:T(8,128)(2,1)} %shard_map.168), calls=%async_computation.1 | async-start | bytes 393216 | tf_op jit(solution)/shard_map/all_to_all | solution.py:35
  36.8 0.0 copy-start.1
  36.8 0.0 collective-permute-done.2
  36.9 0.1 pad_maximum_fusion.refs_0_
  36.9 0.0 copy-start.7
  36.9 1.9 %collective-permute-start.3 = (bf16[2,128,1024]{2,1,0:T(8,128)(2,1)S(1)}, bf16[2,128,1024]{2,1,0:T(8,128)(2,1)S(1)}, u32[]{:S(2)}, u32[]{:S(2)}) collective-permute-start(bf16[2,128,1024]{2,1,0:T(8,128)(2,1)S(1)} %pad_maximum_fusion.refs_0_), channel_id=1, source_target_pairs={{0,2},{2,0},{4,6},{6,4},{1,3},{3,1},{5,7},{7,5},{8,10},{10,8},{12,... | collective-permute-start | bytes 1572872 | tf_op jit(solution)/shard_map/ppermute | solution.py:43
  38.9 5.0 %all-to-all-done.1.in_ref = bf16[16,48,128]{2,1,0:T(8,128)(2,1)S(1)} async-done(((bf16[16,48,128]{2,1,0:T(8,128)(2,1)}), bf16[16,48,128]{2,1,0:T(8,128)(2,1)S(1)}, u32[]{:S(2)}, u32[]{:S(2)}) %all-to-all-start.1) | async-done | bytes 196640 | tf_op jit(solution)/shard_map/all_to_all | solution.py:35
  43.9 0.7 shard_map.169
  44.5 0.0 copy-start.5
  44.5 8.3 %all-to-all-start.2 = ((f32[4,48,128]{2,1,0:T(8,128)}), f32[4,48,128]{2,1,0:T(8,128)S(1)}, u32[]{:S(2)}, u32[]{:S(2)}) async-start(f32[4,48,128]{2,1,0:T(8,128)} %shard_map.169), calls=%async_computation.2 | async-start | bytes 196608 | tf_op jit(solution)/shard_map/all_to_all | solution.py:35
  52.9 0.0 copy-done.11
  52.9 0.1 broadcast_in_dim.11
  52.9 0.1 broadcast_in_dim.12
  53.0 0.1 broadcast_in_dim.13.refs_4_
  53.1 0.0 copy-done.10
  53.1 0.1 reshape.27.refs_0_
  53.2 1.0 %shard_map.171 = (f32[48,128]{1,0:T(8,128)S(1)}, f32[48,128]{1,0:T(8,128)S(1)}) custom-call(f32[64,1024]{1,0:T(8,128)} %bitcast.17, f32[64,1024]{1,0:T(8,128)} %bitcast.18, f32[64,128]{1,0:T(8,128)} %moment_b_ref, f32[64,128]{1,0:T(8,128)} %second_b_ref), custom_call_target="tpu_custom_call" | custom-call | tf_op jit(solution)/shard_map/pallas_call | solution.py:47
  54.2 0.0 copy-done.2
  54.2 0.0 copy-done.3
  54.2 0.0 copy-done.6
  54.3 2.8 %shard_map.170 = (f32[1024,128]{1,0:T(8,128)S(1)}, bf16[1024,128]{1,0:T(8,128)(2,1)S(1)}) custom-call(bf16[128,1024]{1,0:T(8,128)(2,1)S(1)} %reshape.27.refs_0_, bf16[1024,128]{1,0:T(8,128)(2,1)S(1)} %bitcast.13, bf16[1024,128]{1,0:T(8,128)(2,1)S(1)} %bitcast.14, bf16[128,128]{1,0:T(8,128)(2,1)S(1)} %bitcast.15, s32[8,128]{1,0:T(8,128)S(1)} %broadcast_in_dim.13.refs_4_), custom_call_target="tpu_custom_call" | custom-call | flops 100663296 | bytes 8388608 | tf_op jit(solution)/shard_map/pallas_call | solution.py:47
  57.0 8.2 %all-to-all-done.2.in_ref = f32[4,48,128]{2,1,0:T(8,128)S(1)} async-done(((f32[4,48,128]{2,1,0:T(8,128)}), f32[4,48,128]{2,1,0:T(8,128)S(1)}, u32[]{:S(2)}, u32[]{:S(2)}) %all-to-all-start.2) | async-done | bytes 98336 | tf_op jit(solution)/shard_map/all_to_all | solution.py:35
  65.2 0.7 shard_map.172
  65.9 3.5 %all-to-all-start.3 = ((bf16[16,48,128]{2,1,0:T(8,128)(2,1)}), bf16[16,48,128]{2,1,0:T(8,128)(2,1)S(1)}, u32[]{:S(2)}, u32[]{:S(2)}) async-start(bf16[16,48,128]{2,1,0:T(8,128)(2,1)} %shard_map.172), calls=%async_computation.3 | async-start | bytes 393216 | tf_op jit(solution)/shard_map/all_to_all | solution.py:35
  69.4 0.0 collective-permute-done.3.refs_1_
  69.5 0.0 copy-start.8
  69.5 4.7 %collective-permute-start.4 = (bf16[2,128,1024]{2,1,0:T(8,128)(2,1)S(1)}, bf16[2,128,1024]{2,1,0:T(8,128)(2,1)S(1)}, u32[]{:S(2)}, u32[]{:S(2)}) collective-permute-start(bf16[2,128,1024]{2,1,0:T(8,128)(2,1)S(1)} %pad_maximum_fusion.refs_0_), channel_id=1, source_target_pairs={{0,1},{1,0},{2,3},{3,2},{4,5},{5,4},{6,7},{7,6},{8,9},{9,8},{10,11... | collective-permute-start | bytes 1572872 | tf_op jit(solution)/shard_map/ppermute | solution.py:39
  74.2 1.9 %collective-permute-start.5 = (bf16[2,128,1024]{2,1,0:T(8,128)(2,1)S(1)}, bf16[2,128,1024]{2,1,0:T(8,128)(2,1)}, u32[]{:S(2)}, u32[]{:S(2)}) collective-permute-start(bf16[2,128,1024]{2,1,0:T(8,128)(2,1)S(1)} %collective-permute-done.3.refs_1_), channel_id=1, source_target_pairs={{0,1},{1,0},{2,3},{3,2},{4,5},{5,4},{6,7},{7,6},{8,9},{9,8},{10,11... | collective-permute-start | bytes 1572872 | tf_op jit(solution)/shard_map/ppermute | solution.py:39
  76.1 0.2 all-to-all-done.3.step_ref
  76.3 0.0 copy-done.1
  76.3 0.9 shard_map.174
  77.2 0.0 copy-done.7
  77.2 7.3 %all-to-all-start.4 = ((bf16[8,64,128]{2,1,0:T(8,128)(2,1)}), bf16[8,64,128]{2,1,0:T(8,128)(2,1)S(1)}, u32[]{:S(2)}, u32[]{:S(2)}) async-start(bf16[8,64,128]{2,1,0:T(8,128)(2,1)} %shard_map.174), calls=%async_computation.4 | async-start | bytes 262144 | tf_op jit(solution)/shard_map/all_to_all | solution.py:35
  84.5 0.0 copy-done.5
  84.5 0.7 shard_map.173
  85.2 0.0 collective-permute-done.4.refs_2_
  85.2 0.0 copy-start.9
  85.2 0.0 collective-permute-done.5.refs_3_
  85.2 0.0 copy-done.8
  85.2 0.8 copy-done.9
  86.0 2.9 %shard_map.175.refs_2_ = f32[128,128]{1,0:T(8,128)S(1)} custom-call(bf16[4,2,1024,128]{3,2,1,0:T(8,128)(2,1)} %bitcast.16, bf16[2,128,1024]{2,1,0:T(8,128)(2,1)} %copy-done.7, bf16[2,128,1024]{2,1,0:T(8,128)(2,1)} %copy-done.8, bf16[2,128,1024]{2,1,0:T(8,128)(2,1)} %copy-done.9, bf16[2,128,1024]{2,1,0:T(8,128)(2,1)} %collective-permute-done.5.refs_3_), custom_call_target="tpu_custom_call" | custom-call | flops 268435456 | bytes 4194304 | tf_op jit(solution)/shard_map/pallas_call | solution.py:47
  89.0 1.4 %all-to-all-done.4.refs_0_ = bf16[8,64,128]{2,1,0:T(8,128)(2,1)S(1)} async-done(((bf16[8,64,128]{2,1,0:T(8,128)(2,1)}), bf16[8,64,128]{2,1,0:T(8,128)(2,1)S(1)}, u32[]{:S(2)}, u32[]{:S(2)}) %all-to-all-start.4) | async-done | bytes 131104 | tf_op jit(solution)/shard_map/all_to_all | solution.py:35
  90.3 1.1 %shard_map.176 = bf16[32,4,1024]{2,1,0:T(4,128)(2,1)} custom-call(bf16[8,64,128]{2,1,0:T(8,128)(2,1)S(1)} %all-to-all-done.4.refs_0_, bf16[64,128]{1,0:T(8,128)(2,1)S(1)} %get-tuple-element.41.refs_1_, f32[128,128]{1,0:T(8,128)S(1)} %shard_map.175.refs_2_, f32[1024,128]{1,0:T(8,128)S(1)} %get-tuple-element.45.refs_3_, ...), custom_call_target="tpu_custom_call" | custom-call | tf_op jit(solution)/shard_map/pallas_call | solution.py:47
  (1 shorter events, 0.0 us)
Async XLA Ops:
  0.6 25.1 %copy-start.4 = (bf16[256,128]{1,0:T(8,128)(2,1)S(1)}, bf16[256,128]{1,0:T(8,128)(2,1)}, u32[]{:S(2)}) copy-start(bf16[256,128]{1,0:T(8,128)(2,1)} %refs_1_.1) | copy-start | bytes 196612
  0.6 25.1 %copy-start = (bf16[256,1024]{1,0:T(8,128)(2,1)S(1)}, bf16[256,1024]{1,0:T(8,128)(2,1)}, u32[]{:S(2)}) copy-start(bf16[256,1024]{1,0:T(8,128)(2,1)} %refs_0_.1) | copy-start | bytes 1572868
  2.2 50.6 %copy-start.11 = (s32[32]{0:T(128)S(1)}, s32[32]{0:T(128)}, u32[]{:S(2)}) copy-start(s32[32]{0:T(128)} %param.29) | copy-start | bytes 388
  2.2 50.9 %copy-start.10 = (bf16[32,4,1024]{2,1,0:T(4,128)(2,1)S(1)}, bf16[32,4,1024]{2,1,0:T(4,128)(2,1)}, u32[]{:S(2)}) copy-start(bf16[32,4,1024]{2,1,0:T(4,128)(2,1)} %param.26) | copy-start | bytes 786436
  2.3 9.9 %collective-permute-start = (f32[128,128]{1,0:T(8,128)S(1)}, f32[128,128]{1,0:T(8,128)S(1)}, u32[]{:S(2)}, u32[]{:S(2)}) collective-permute-start(f32[128,128]{1,0:T(8,128)S(1)} %get-tuple-element.26), channel_id=1, source_target_pairs={{0,1},{1,0},{2,3},{3,2},{4,5},{5,4},{6,7},{7,6},{8,9},{9,8},{10,11... | collective-permute-start | bytes 196616 | tf_op jit(solution)/shard_map/ppermute | solution.py:39
  12.9 8.2 %all-to-all-start = ((bf16[4,128,128]{2,1,0:T(8,128)(2,1)}), bf16[4,128,128]{2,1,0:T(8,128)(2,1)S(1)}, u32[]{:S(2)}, u32[]{:S(2)}) async-start(bf16[4,128,128]{2,1,0:T(8,128)(2,1)} %shard_map.167), calls=%async_computation | async-start | bytes 262144 | tf_op jit(solution)/shard_map/all_to_all | solution.py:35
  16.2 38.0 %copy-start.2 = (bf16[32,32,128]{2,1,0:T(8,128)(2,1)S(1)}, bf16[32,32,128]{2,1,0:T(8,128)(2,1)}, u32[]{:S(2)}) copy-start(bf16[32,32,128]{2,1,0:T(8,128)(2,1)} %param.27) | copy-start | bytes 786436
  16.2 38.0 %copy-start.3 = (bf16[32,32,128]{2,1,0:T(8,128)(2,1)S(1)}, bf16[32,32,128]{2,1,0:T(8,128)(2,1)}, u32[]{:S(2)}) copy-start(bf16[32,32,128]{2,1,0:T(8,128)(2,1)} %param.28) | copy-start | bytes 786436
  16.2 38.0 %copy-start.6 = (bf16[32,4,128]{2,1,0:T(4,128)(2,1)S(1)}, bf16[32,4,128]{2,1,0:T(4,128)(2,1)}, u32[]{:S(2)}) copy-start(bf16[32,4,128]{2,1,0:T(4,128)(2,1)} %param.25) | copy-start | bytes 98308
  16.2 20.6 %collective-permute-start.2 = (bf16[1,128,1024]{2,1,0:T(8,128)(2,1)S(1)}, bf16[1,128,1024]{2,1,0:T(8,128)(2,1)S(1)}, u32[]{:S(2)}, u32[]{:S(2)}) collective-permute-start(bf16[1,128,1024]{2,1,0:T(8,128)(2,1)S(1)} %bitcast.9), channel_id=1, source_target_pairs={{0,4},{2,6},{4,0},{6,2},{1,5},{3,7},{5,1},{7,3},{8,12},{10,14},{12... | collective-permute-start | bytes 786440 | tf_op jit(solution)/shard_map/ppermute | solution.py:43
  21.1 4.7 %collective-permute-start.1 = (bf16[128,128]{1,0:T(8,128)(2,1)S(1)}, bf16[128,128]{1,0:T(8,128)(2,1)S(1)}, u32[]{:S(2)}, u32[]{:S(2)}) collective-permute-start(bf16[128,128]{1,0:T(8,128)(2,1)S(1)} %reduce_sum.12.refs_2_), channel_id=1, source_target_pairs={{0,1},{1,0},{2,3},{3,2},{4,5},{5,4},{6,7},{7,6},{8,9},{9,8},{10,11... | collective-permute-start | bytes 98312 | tf_op jit(solution)/shard_map/ppermute | solution.py:39
  26.7 17.2 %all-to-all-start.1 = ((bf16[16,48,128]{2,1,0:T(8,128)(2,1)}), bf16[16,48,128]{2,1,0:T(8,128)(2,1)S(1)}, u32[]{:S(2)}, u32[]{:S(2)}) async-start(bf16[16,48,128]{2,1,0:T(8,128)(2,1)} %shard_map.168), calls=%async_computation.1 | async-start | bytes 393216 | tf_op jit(solution)/shard_map/all_to_all | solution.py:35
  36.8 39.5 %copy-start.1 = (f32[1024,64]{0,1:T(8,128)S(1)}, f32[1024,64]{0,1:T(8,128)}, u32[]{:S(2)}) copy-start(f32[1024,64]{0,1:T(8,128)} %param.17) | copy-start | bytes 786436
  36.9 40.3 %copy-start.7 = (bf16[2,128,1024]{2,1,0:T(8,128)(2,1)}, bf16[2,128,1024]{2,1,0:T(8,128)(2,1)S(1)}, u32[]{:S(2)}) copy-start(bf16[2,128,1024]{2,1,0:T(8,128)(2,1)S(1)} %pad_maximum_fusion.refs_0_) | copy-start | bytes 1572868
  36.9 32.5 %collective-permute-start.3 = (bf16[2,128,1024]{2,1,0:T(8,128)(2,1)S(1)}, bf16[2,128,1024]{2,1,0:T(8,128)(2,1)S(1)}, u32[]{:S(2)}, u32[]{:S(2)}) collective-permute-start(bf16[2,128,1024]{2,1,0:T(8,128)(2,1)S(1)} %pad_maximum_fusion.refs_0_), channel_id=1, source_target_pairs={{0,2},{2,0},{4,6},{6,4},{1,3},{3,1},{5,7},{7,5},{8,10},{10,8},{12,... | collective-permute-start | bytes 1572872 | tf_op jit(solution)/shard_map/ppermute | solution.py:43
  44.5 39.9 %copy-start.5 = (f32[64,128]{1,0:T(8,128)S(1)}, f32[64,128]{1,0:T(8,128)}, u32[]{:S(2)}) copy-start(f32[64,128]{1,0:T(8,128)} %b_ref.3) | copy-start | bytes 98308
  44.5 20.6 %all-to-all-start.2 = ((f32[4,48,128]{2,1,0:T(8,128)}), f32[4,48,128]{2,1,0:T(8,128)S(1)}, u32[]{:S(2)}, u32[]{:S(2)}) async-start(f32[4,48,128]{2,1,0:T(8,128)} %shard_map.169), calls=%async_computation.2 | async-start | bytes 196608 | tf_op jit(solution)/shard_map/all_to_all | solution.py:35
  65.9 10.4 %all-to-all-start.3 = ((bf16[16,48,128]{2,1,0:T(8,128)(2,1)}), bf16[16,48,128]{2,1,0:T(8,128)(2,1)S(1)}, u32[]{:S(2)}, u32[]{:S(2)}) async-start(bf16[16,48,128]{2,1,0:T(8,128)(2,1)} %shard_map.172), calls=%async_computation.3 | async-start | bytes 393216 | tf_op jit(solution)/shard_map/all_to_all | solution.py:35
  69.5 15.8 %copy-start.8 = (bf16[2,128,1024]{2,1,0:T(8,128)(2,1)}, bf16[2,128,1024]{2,1,0:T(8,128)(2,1)S(1)}, u32[]{:S(2)}) copy-start(bf16[2,128,1024]{2,1,0:T(8,128)(2,1)S(1)} %collective-permute-done.3.refs_1_) | copy-start | bytes 1572868
  69.5 15.8 %collective-permute-start.4 = (bf16[2,128,1024]{2,1,0:T(8,128)(2,1)S(1)}, bf16[2,128,1024]{2,1,0:T(8,128)(2,1)S(1)}, u32[]{:S(2)}, u32[]{:S(2)}) collective-permute-start(bf16[2,128,1024]{2,1,0:T(8,128)(2,1)S(1)} %pad_maximum_fusion.refs_0_), channel_id=1, source_target_pairs={{0,1},{1,0},{2,3},{3,2},{4,5},{5,4},{6,7},{7,6},{8,9},{9,8},{10,11... | collective-permute-start | bytes 1572872 | tf_op jit(solution)/shard_map/ppermute | solution.py:39
  74.2 11.0 %collective-permute-start.5 = (bf16[2,128,1024]{2,1,0:T(8,128)(2,1)S(1)}, bf16[2,128,1024]{2,1,0:T(8,128)(2,1)}, u32[]{:S(2)}, u32[]{:S(2)}) collective-permute-start(bf16[2,128,1024]{2,1,0:T(8,128)(2,1)S(1)} %collective-permute-done.3.refs_1_), channel_id=1, source_target_pairs={{0,1},{1,0},{2,3},{3,2},{4,5},{5,4},{6,7},{7,6},{8,9},{9,8},{10,11... | collective-permute-start | bytes 1572872 | tf_op jit(solution)/shard_map/ppermute | solution.py:39
  77.2 13.1 %all-to-all-start.4 = ((bf16[8,64,128]{2,1,0:T(8,128)(2,1)}), bf16[8,64,128]{2,1,0:T(8,128)(2,1)S(1)}, u32[]{:S(2)}, u32[]{:S(2)}) async-start(bf16[8,64,128]{2,1,0:T(8,128)(2,1)} %shard_map.174), calls=%async_computation.4 | async-start | bytes 262144 | tf_op jit(solution)/shard_map/all_to_all | solution.py:35
  85.2 0.8 copy-start.9

commit v6 on v5

--- a/solution.py
+++ b/solution.py
@@ -69,20 +69,14 @@
     return lax.dot_general(a, b, (((1,), (1,)), ((), ())), preferred_element_type=F32)
 
 
-def low_body(x_ref, cot_ref, a_ref, b_ref, mine_ref, theirs_ref):
+def low_body(x_ref, cot_ref, a_ref, b_ref, out_ref):
     acts = rows_dot(x_ref[...], a_ref[...].astype(BF))
     grads = rows_dot(cot_ref[...], b_ref[...].astype(BF))
-    both = jnp.concatenate([acts, grads], axis=1)
-    half = both.shape[0] // 2
-    first = lax.axis_index("core") == 0
-    mine_ref[...] = jnp.where(first, both[:half], both[half:])
-    theirs_ref[...] = jnp.where(first, both[half:], both[:half])
-
-
-def pair_body(mine_ref, theirs_ref, out_ref):
-    total = (mine_ref[...] + theirs_ref[...]).astype(BF)
+    both = jnp.concatenate([acts, grads], axis=1).astype(BF)
+    tall = out_ref.shape[1]
     for i in range(out_ref.shape[0]):
-        out_ref[i] = total
+        core = i % 2
+        out_ref[i] = both[core * tall : (core + 1) * tall]
 
 
 def stack(value, wide):
@@ -286,18 +280,20 @@
     flat = lax.optimization_barrier(decode_states.reshape(count, width))
     a_turned = adapter_a.T
 
-    half = shape((tokens // 2, two), F32)
     starts = (trainer_token_input, cotangent, a_turned, adapter_b)
-    mine, theirs = call(low_body, (half, half), *map(far, starts))
-    pair = call(pair_body, shape((pairs, tokens // 2, two), BF), mine, swap(theirs))
-
-    pair, send = lax.optimization_barrier((pair, flat))
+    parts = call(low_body, shape((tensor, tokens // 2, two), BF), *map(far, starts))
+
+    send, _ = lax.optimization_barrier((flat, parts))
     second_chip = reach(send[None], 2)
-    mine = jnp.sum(trade(pair, "zl").astype(F32), axis=0).astype(BF)
+    mine = jnp.sum(trade(parts, TENSOR).astype(F32), axis=0).astype(BF)
+    mine, moments = lax.optimization_barrier((mine, (moment_a.T, second_a.T, moment_b, second_b)))
     theirs = swap(mine)
-
     rows_a, rows_b = rank * width // kv // plane, rank // plane
     deep = rows_a + rows_b + -(rows_a + rows_b) % 16
+    piece = shape((deep, kv), F32)
+    moments = call(shard_body, (piece, piece), *map(far, moments))
+    theirs, moments = lax.optimization_barrier((theirs, moments))
+
     scale = adapter_scale / (tokens * lax.axis_size(DP))
     block = call(
         lambda *refs: gradient_body(scale, *refs),
@@ -312,12 +308,8 @@
     near = jnp.concatenate([send[None], second_chip], axis=0)
     distant = reach(near, 1)
     shard = call(sum_body, shape((lax.axis_size("zh"), deep, kv), F32), shard)
-    shard, query, moments = lax.optimization_barrier(
-        (shard, queries, (moment_a.T, second_a.T, moment_b, second_b))
-    )
+    shard, query = lax.optimization_barrier((shard, queries))
     shard = trade(shard, "zh")
-    piece = shape((deep, kv), F32)
-    moments = call(shard_body, (piece, piece), *map(far, moments))
 
     groups = rows * slots // HD
     heads = queries.shape[2] // HD
@@ -346,7 +338,11 @@
     base = call(
         base_body,
         shape((count, kv), F32),
-        *map(far, (value_matrix.reshape(pairs, 2, width, kv), near, distant, near_other, distant_other)),
+        far(value_matrix.reshape(pairs, 2, width, kv)),
+        near,
+        distant,
+        near_other,
+        distant_other,
         flops=2 * count * tensor * width * kv,
         moved=4 * 2**20,
         in_specs=[pl.BlockSpec(memory_space=pl.ANY)] * 5,

time: 92.3 us -> 96.7 us (1.048)
  waiting for transfers between devices: 16.1 us -> 24.6 us
  starting transfers between devices: 58.2 us -> 54.2 us
    ppermute x4 -> x3, starting transfers between devices: 19.4 us -> 10 us  [swap(): return lax.ppermute(value, 'core', [(0, 1), (1, 0)])]
    all_to_all x5, waiting for transfers between devices: 15.2 us -> 24.6 us  [trade(): return lax.all_to_all(parts, axes, 0, 0, tiled=True)]
    all_to_all x5, starting transfers between devices: 32.5 us -> 37.9 us  [trade(): return lax.all_to_all(parts, axes, 0, 0, tiled=True)]
    pallas_call x11 -> x10, Pallas kernels: 14.1 us -> 14 us  [call(): pl.pallas_call(body, out_shape=out, cost_estimate=pl.CostEstimate(flops=f...]
  transfers between devices with their start and end apart: 11 -> 10, of which waited for: 6 -> 5; matrix products, arithmetic and copies ran while one was open for 2% -> 2% of each run, Pallas kernels for 12% -> 11%
where the time goes in v6:
time: 96.7 us; the launch traced here: 95.9 us
  starting transfers between devices  54.2 us (56%)
  waiting for transfers between devices  24.6 us (25%)
  Pallas kernels  14 us (14%)
  local copies, waits for them, and re-layouts  2.11 us (2%)
    all_to_all x5, starting transfers between devices, trade(): return lax.all_to_all(parts, axes, 0, 0, tiled=True)  37.9 us
    all_to_all x5, waiting for transfers between devices, trade(): return lax.all_to_all(parts, axes, 0, 0, tiled=True)  24.6 us
    pallas_call x10, Pallas kernels, call(): pl.pallas_call(body, out_shape=out, cost_estimate=pl.CostEstimate(flops=f...  14 us
    ppermute x3, starting transfers between devices, swap(): return lax.ppermute(value, 'core', [(0, 1), (1, 0)])  10 us
    ppermute x2, starting transfers between devices, reach(): lax.ppermute(value, 'zl', [(i, i ^ hop) for i in range(lax.axis_size('zl'...  6.26 us
  transfers between devices with their start and end apart: 10, of which 5 were waited for; matrix products, arithmetic and copies ran while one was open for 2% of the time, Pallas kernels for 11%

profile of v6, /device:TPU:1, one launch (start us, length us, event | category | flops | bytes accessed | tf_op | source)
XLA Modules:
  0.0 95.9 jit_solution(17648613939169215051)
XLA Ops:
  0.6 0.0 copy-start.6
  0.6 0.0 copy-start
  0.6 2.3 %shard_map.166 = bf16[8,128,128]{2,1,0:T(8,128)(2,1)} custom-call(bf16[256,1024]{1,0:T(8,128)(2,1)} %refs_0_.1, bf16[256,128]{1,0:T(8,128)(2,1)} %refs_1_.1, f32[64,1024]{1,0:T(8,128)} %bitcast.11, f32[64,128]{1,0:T(8,128)} %b_ref.3), custom_call_target="tpu_custom_call" | custom-call | tf_op jit(solution)/shard_map/pallas_call | solution.py:47
  2.9 10.2 %all-to-all-start = ((bf16[8,128,128]{2,1,0:T(8,128)(2,1)}), bf16[8,128,128]{2,1,0:T(8,128)(2,1)S(1)}, u32[]{:S(2)}, u32[]{:S(2)}) async-start(bf16[8,128,128]{2,1,0:T(8,128)(2,1)} %shard_map.166), calls=%async_computation | async-start | bytes 524288 | tf_op jit(solution)/shard_map/all_to_all | solution.py:35
  13.1 0.0 copy-start.10
  13.1 0.0 copy-start.9
  13.1 1.1 %reshape.30.flat_ref = bf16[128,1024]{1,0:T(8,128)(2,1)S(1)} reshape(bf16[32,4,1024]{2,1,0:T(4,128)(2,1)} %param.24) | data formatting | bytes 524288 | tf_op jit(solution)/shard_map/reshape | solution.py:280
  14.2 0.0 copy-start.2
  14.2 0.0 copy-start.3
  14.2 0.0 copy-start.8
  14.2 4.3 %collective-permute-start.1 = (bf16[1,128,1024]{2,1,0:T(8,128)(2,1)S(1)}, bf16[1,128,1024]{2,1,0:T(8,128)(2,1)S(1)}, u32[]{:S(2)}, u32[]{:S(2)}) collective-permute-start(bf16[1,128,1024]{2,1,0:T(8,128)(2,1)S(1)} %bitcast.9), channel_id=1, source_target_pairs={{0,4},{2,6},{4,0},{6,2},{1,5},{3,7},{5,1},{7,3},{8,12},{10,14},{12... | collective-permute-start | bytes 786440 | tf_op jit(solution)/shard_map/ppermute | solution.py:43
  18.6 9.0 %all-to-all-done = bf16[8,128,128]{2,1,0:T(8,128)(2,1)S(1)} async-done(((bf16[8,128,128]{2,1,0:T(8,128)(2,1)}), bf16[8,128,128]{2,1,0:T(8,128)(2,1)S(1)}, u32[]{:S(2)}, u32[]{:S(2)}) %all-to-all-start) | async-done | bytes 262176 | tf_op jit(solution)/shard_map/all_to_all | solution.py:35
  27.6 3.3 %collective-permute-start = (bf16[128,128]{1,0:T(8,128)(2,1)S(1)}, bf16[128,128]{1,0:T(8,128)(2,1)S(1)}, u32[]{:S(2)}, u32[]{:S(2)}) collective-permute-start(bf16[128,128]{1,0:T(8,128)(2,1)S(1)} %reduce_sum.12.refs_2_), channel_id=1, source_target_pairs={{0,1},{1,0},{2,3},{3,2},{4,5},{5,4},{6,7},{7,6},{8,9},{9,8},{10,11... | collective-permute-start | bytes 98312 | tf_op jit(solution)/shard_map/ppermute | solution.py:39
  30.9 1.0 %shard_map.167 = (f32[48,128]{1,0:T(8,128)S(1)}, f32[48,128]{1,0:T(8,128)S(1)}) custom-call(f32[64,1024]{1,0:T(8,128)} %bitcast.17, f32[64,1024]{1,0:T(8,128)} %bitcast.18, f32[64,128]{1,0:T(8,128)} %moment_b_ref, f32[64,128]{1,0:T(8,128)} %second_b_ref), custom_call_target="tpu_custom_call" | custom-call | tf_op jit(solution)/shard_map/pallas_call | solution.py:47
  32.0 0.0 collective-permute-done.refs_3_
  32.0 0.0 copy-done.6
  32.0 0.0 copy-done
  32.0 1.0 %shard_map.168 = bf16[16,48,128]{2,1,0:T(8,128)(2,1)} custom-call(bf16[256,1024]{1,0:T(8,128)(2,1)S(1)} %copy-done, bf16[256,128]{1,0:T(8,128)(2,1)S(1)} %copy-done.6, bf16[128,128]{1,0:T(8,128)(2,1)S(1)} %reduce_sum.12.refs_2_, bf16[128,128]{1,0:T(8,128)(2,1)S(1)} %collective-permute-done.refs_3_), custom_call_target="tpu_custom_call" | custom-call | tf_op jit(solution)/shard_map/pallas_call | solution.py:47
  33.0 0.0 copy-start.1
  33.0 4.1 %all-to-all-start.1 = ((bf16[16,48,128]{2,1,0:T(8,128)(2,1)}), bf16[16,48,128]{2,1,0:T(8,128)(2,1)S(1)}, u32[]{:S(2)}, u32[]{:S(2)}) async-start(bf16[16,48,128]{2,1,0:T(8,128)(2,1)} %shard_map.168), calls=%async_computation.1 | async-start | bytes 393216 | tf_op jit(solution)/shard_map/all_to_all | solution.py:35
  37.1 0.0 collective-permute-done.1
  37.1 0.1 pad_maximum_fusion.refs_0_
  37.2 0.0 copy-start.7
  37.2 1.9 %collective-permute-start.2 = (bf16[2,128,1024]{2,1,0:T(8,128)(2,1)S(1)}, bf16[2,128,1024]{2,1,0:T(8,128)(2,1)S(1)}, u32[]{:S(2)}, u32[]{:S(2)}) collective-permute-start(bf16[2,128,1024]{2,1,0:T(8,128)(2,1)S(1)} %pad_maximum_fusion.refs_0_), channel_id=1, source_target_pairs={{0,2},{2,0},{4,6},{6,4},{1,3},{3,1},{5,7},{7,5},{8,10},{10,8},{12,... | collective-permute-start | bytes 1572872 | tf_op jit(solution)/shard_map/ppermute | solution.py:43
  39.1 5.0 %all-to-all-done.1.in_ref = bf16[16,48,128]{2,1,0:T(8,128)(2,1)S(1)} async-done(((bf16[16,48,128]{2,1,0:T(8,128)(2,1)}), bf16[16,48,128]{2,1,0:T(8,128)(2,1)S(1)}, u32[]{:S(2)}, u32[]{:S(2)}) %all-to-all-start.1) | async-done | bytes 196640 | tf_op jit(solution)/shard_map/all_to_all | solution.py:35
  44.1 0.7 shard_map.169
  44.8 12.2 %all-to-all-start.2 = ((f32[4,48,128]{2,1,0:T(8,128)}), f32[4,48,128]{2,1,0:T(8,128)S(1)}, u32[]{:S(2)}, u32[]{:S(2)}) async-start(f32[4,48,128]{2,1,0:T(8,128)} %shard_map.169), calls=%async_computation.2 | async-start | bytes 196608 | tf_op jit(solution)/shard_map/all_to_all | solution.py:35
  57.0 0.0 copy-done.10
  57.0 0.1 broadcast_in_dim.11
  57.1 0.1 broadcast_in_dim.12
  57.2 0.1 broadcast_in_dim.13.refs_4_
  57.3 0.0 copy-done.9
  57.3 0.1 reshape.26.refs_0_
  57.3 0.0 copy-done.2
  57.3 0.0 copy-done.3
  57.4 0.0 copy-done.8
  57.4 2.8 %shard_map.170 = (f32[1024,128]{1,0:T(8,128)S(1)}, bf16[1024,128]{1,0:T(8,128)(2,1)S(1)}) custom-call(bf16[128,1024]{1,0:T(8,128)(2,1)S(1)} %reshape.26.refs_0_, bf16[1024,128]{1,0:T(8,128)(2,1)S(1)} %bitcast.13, bf16[1024,128]{1,0:T(8,128)(2,1)S(1)} %bitcast.14, bf16[128,128]{1,0:T(8,128)(2,1)S(1)} %bitcast.15, s32[8,128]{1,0:T(8,128)S(1)} %broadcast_in_dim.13.refs_4_), custom_call_target="tpu_custom_call" | custom-call | flops 100663296 | bytes 8388608 | tf_op jit(solution)/shard_map/pallas_call | solution.py:47
  60.1 0.0 copy-start.4
  60.1 0.7 copy-done.4
  60.8 8.2 %all-to-all-done.2.in_ref = f32[4,48,128]{2,1,0:T(8,128)S(1)} async-done(((f32[4,48,128]{2,1,0:T(8,128)}), f32[4,48,128]{2,1,0:T(8,128)S(1)}, u32[]{:S(2)}, u32[]{:S(2)}) %all-to-all-start.2) | async-done | bytes 98336 | tf_op jit(solution)/shard_map/all_to_all | solution.py:35
  69.0 0.7 shard_map.171
  69.8 4.0 %all-to-all-start.3 = ((bf16[16,48,128]{2,1,0:T(8,128)(2,1)}), bf16[16,48,128]{2,1,0:T(8,128)(2,1)S(1)}, u32[]{:S(2)}, u32[]{:S(2)}) async-start(bf16[16,48,128]{2,1,0:T(8,128)(2,1)} %shard_map.171), calls=%async_computation.3 | async-start | bytes 393216 | tf_op jit(solution)/shard_map/all_to_all | solution.py:35
  73.8 0.0 collective-permute-done.2.refs_1_
  73.8 4.8 %collective-permute-start.3 = (bf16[2,128,1024]{2,1,0:T(8,128)(2,1)S(1)}, bf16[2,128,1024]{2,1,0:T(8,128)(2,1)S(1)}, u32[]{:S(2)}, u32[]{:S(2)}) collective-permute-start(bf16[2,128,1024]{2,1,0:T(8,128)(2,1)S(1)} %pad_maximum_fusion.refs_0_), channel_id=1, source_target_pairs={{0,1},{1,0},{2,3},{3,2},{4,5},{5,4},{6,7},{7,6},{8,9},{9,8},{10,11... | collective-permute-start | bytes 1572872 | tf_op jit(solution)/shard_map/ppermute | solution.py:39
  78.6 1.9 %collective-permute-start.4 = (bf16[2,128,1024]{2,1,0:T(8,128)(2,1)S(1)}, bf16[2,128,1024]{2,1,0:T(8,128)(2,1)S(1)}, u32[]{:S(2)}, u32[]{:S(2)}) collective-permute-start(bf16[2,128,1024]{2,1,0:T(8,128)(2,1)S(1)} %collective-permute-done.2.refs_1_), channel_id=1, source_target_pairs={{0,1},{1,0},{2,3},{3,2},{4,5},{5,4},{6,7},{7,6},{8,9},{9,8},{10,11... | collective-permute-start | bytes 1572872 | tf_op jit(solution)/shard_map/ppermute | solution.py:39
  80.5 0.2 all-to-all-done.3.step_ref
  80.7 0.0 copy-done.1
  80.7 0.9 shard_map.173
  81.6 7.4 %all-to-all-start.4 = ((bf16[8,64,128]{2,1,0:T(8,128)(2,1)}), bf16[8,64,128]{2,1,0:T(8,128)(2,1)S(1)}, u32[]{:S(2)}, u32[]{:S(2)}) async-start(bf16[8,64,128]{2,1,0:T(8,128)(2,1)} %shard_map.173), calls=%async_computation.4 | async-start | bytes 262144 | tf_op jit(solution)/shard_map/all_to_all | solution.py:35
  88.9 0.0 copy-done.7
  88.9 0.7 shard_map.172
  89.7 0.0 collective-permute-done.3.refs_2_
  89.7 0.0 collective-permute-done.4.refs_3_
  89.7 0.0 copy-start.5
  89.7 2.9 %shard_map.174.refs_2_ = f32[128,128]{1,0:T(8,128)S(1)} custom-call(bf16[4,2,1024,128]{3,2,1,0:T(8,128)(2,1)} %bitcast.16, bf16[2,128,1024]{2,1,0:T(8,128)(2,1)S(1)} %pad_maximum_fusion.refs_0_, bf16[2,128,1024]{2,1,0:T(8,128)(2,1)S(1)} %collective-permute-done.2.refs_1_, bf16[2,128,1024]{2,1,0:T(8,128)(2,1)S(1)} %collective-permute-done.3.refs_2_, ...), custom_call_target="tpu_custom_call" | custom-call | flops 268435456 | bytes 4194304 | tf_op jit(solution)/shard_map/pallas_call | solution.py:47
  92.5 2.2 %all-to-all-done.4.refs_0_ = bf16[8,64,128]{2,1,0:T(8,128)(2,1)S(1)} async-done(((bf16[8,64,128]{2,1,0:T(8,128)(2,1)}), bf16[8,64,128]{2,1,0:T(8,128)(2,1)S(1)}, u32[]{:S(2)}, u32[]{:S(2)}) %all-to-all-start.4) | async-done | bytes 131104 | tf_op jit(solution)/shard_map/all_to_all | solution.py:35
  94.8 0.0 copy-done.5
  94.8 1.1 %shard_map.175 = bf16[32,4,1024]{2,1,0:T(4,128)(2,1)} custom-call(bf16[8,64,128]{2,1,0:T(8,128)(2,1)S(1)} %all-to-all-done.4.refs_0_, bf16[64,128]{1,0:T(8,128)(2,1)S(1)} %get-tuple-element.43.refs_1_, f32[128,128]{1,0:T(8,128)S(1)} %shard_map.174.refs_2_, f32[1024,128]{1,0:T(8,128)S(1)} %get-tuple-element.47.refs_3_, bf16[1024,128]{1,0:T(8,128)(2,1)S(1)} %copy-done.5), custom_call_target="tpu_custom_call" | custom-call | tf_op jit(solution)/shard_map/pallas_call | solution.py:47
  (1 shorter events, 0.0 us)
Async XLA Ops:
  0.6 31.4 %copy-start.6 = (bf16[256,128]{1,0:T(8,128)(2,1)S(1)}, bf16[256,128]{1,0:T(8,128)(2,1)}, u32[]{:S(2)}) copy-start(bf16[256,128]{1,0:T(8,128)(2,1)} %refs_1_.1) | copy-start | bytes 196612
  0.6 31.4 %copy-start = (bf16[256,1024]{1,0:T(8,128)(2,1)S(1)}, bf16[256,1024]{1,0:T(8,128)(2,1)}, u32[]{:S(2)}) copy-start(bf16[256,1024]{1,0:T(8,128)(2,1)} %refs_0_.1) | copy-start | bytes 1572868
  2.9 24.7 %all-to-all-start = ((bf16[8,128,128]{2,1,0:T(8,128)(2,1)}), bf16[8,128,128]{2,1,0:T(8,128)(2,1)S(1)}, u32[]{:S(2)}, u32[]{:S(2)}) async-start(bf16[8,128,128]{2,1,0:T(8,128)(2,1)} %shard_map.166), calls=%async_computation | async-start | bytes 524288 | tf_op jit(solution)/shard_map/all_to_all | solution.py:35
  13.1 43.9 %copy-start.10 = (s32[32]{0:T(128)S(1)}, s32[32]{0:T(128)}, u32[]{:S(2)}) copy-start(s32[32]{0:T(128)} %param.29) | copy-start | bytes 388
  13.1 44.1 %copy-start.9 = (bf16[32,4,1024]{2,1,0:T(4,128)(2,1)S(1)}, bf16[32,4,1024]{2,1,0:T(4,128)(2,1)}, u32[]{:S(2)}) copy-start(bf16[32,4,1024]{2,1,0:T(4,128)(2,1)} %param.26) | copy-start | bytes 786436
  14.2 43.1 %copy-start.2 = (bf16[32,32,128]{2,1,0:T(8,128)(2,1)S(1)}, bf16[32,32,128]{2,1,0:T(8,128)(2,1)}, u32[]{:S(2)}) copy-start(bf16[32,32,128]{2,1,0:T(8,128)(2,1)} %param.27) | copy-start | bytes 786436
  14.2 43.1 %copy-start.3 = (bf16[32,32,128]{2,1,0:T(8,128)(2,1)S(1)}, bf16[32,32,128]{2,1,0:T(8,128)(2,1)}, u32[]{:S(2)}) copy-start(bf16[32,32,128]{2,1,0:T(8,128)(2,1)} %param.28) | copy-start | bytes 786436
  14.2 43.1 %copy-start.8 = (bf16[32,4,128]{2,1,0:T(4,128)(2,1)S(1)}, bf16[32,4,128]{2,1,0:T(4,128)(2,1)}, u32[]{:S(2)}) copy-start(bf16[32,4,128]{2,1,0:T(4,128)(2,1)} %param.25) | copy-start | bytes 98308
  14.2 22.9 %collective-permute-start.1 = (bf16[1,128,1024]{2,1,0:T(8,128)(2,1)S(1)}, bf16[1,128,1024]{2,1,0:T(8,128)(2,1)S(1)}, u32[]{:S(2)}, u32[]{:S(2)}) collective-permute-start(bf16[1,128,1024]{2,1,0:T(8,128)(2,1)S(1)} %bitcast.9), channel_id=1, source_target_pairs={{0,4},{2,6},{4,0},{6,2},{1,5},{3,7},{5,1},{7,3},{8,12},{10,14},{12... | collective-permute-start | bytes 786440 | tf_op jit(solution)/shard_map/ppermute | solution.py:43
  27.6 4.4 %collective-permute-start = (bf16[128,128]{1,0:T(8,128)(2,1)S(1)}, bf16[128,128]{1,0:T(8,128)(2,1)S(1)}, u32[]{:S(2)}, u32[]{:S(2)}) collective-permute-start(bf16[128,128]{1,0:T(8,128)(2,1)S(1)} %reduce_sum.12.refs_2_), channel_id=1, source_target_pairs={{0,1},{1,0},{2,3},{3,2},{4,5},{5,4},{6,7},{7,6},{8,9},{9,8},{10,11... | collective-permute-start | bytes 98312 | tf_op jit(solution)/shard_map/ppermute | solution.py:39
  33.0 47.7 %copy-start.1 = (f32[1024,64]{0,1:T(8,128)S(1)}, f32[1024,64]{0,1:T(8,128)}, u32[]{:S(2)}) copy-start(f32[1024,64]{0,1:T(8,128)} %param.17) | copy-start | bytes 786436
  33.0 11.1 %all-to-all-start.1 = ((bf16[16,48,128]{2,1,0:T(8,128)(2,1)}), bf16[16,48,128]{2,1,0:T(8,128)(2,1)S(1)}, u32[]{:S(2)}, u32[]{:S(2)}) async-start(bf16[16,48,128]{2,1,0:T(8,128)(2,1)} %shard_map.168), calls=%async_computation.1 | async-start | bytes 393216 | tf_op jit(solution)/shard_map/all_to_all | solution.py:35
  37.2 51.8 %copy-start.7 = (f32[64,128]{1,0:T(8,128)S(1)}, f32[64,128]{1,0:T(8,128)}, u32[]{:S(2)}) copy-start(f32[64,128]{1,0:T(8,128)} %b_ref.3) | copy-start | bytes 98308
  37.2 36.6 %collective-permute-start.2 = (bf16[2,128,1024]{2,1,0:T(8,128)(2,1)S(1)}, bf16[2,128,1024]{2,1,0:T(8,128)(2,1)S(1)}, u32[]{:S(2)}, u32[]{:S(2)}) collective-permute-start(bf16[2,128,1024]{2,1,0:T(8,128)(2,1)S(1)} %pad_maximum_fusion.refs_0_), channel_id=1, source_target_pairs={{0,2},{2,0},{4,6},{6,4},{1,3},{3,1},{5,7},{7,5},{8,10},{10,8},{12,... | collective-permute-start | bytes 1572872 | tf_op jit(solution)/shard_map/ppermute | solution.py:43
  44.8 24.3 %all-to-all-start.2 = ((f32[4,48,128]{2,1,0:T(8,128)}), f32[4,48,128]{2,1,0:T(8,128)S(1)}, u32[]{:S(2)}, u32[]{:S(2)}) async-start(f32[4,48,128]{2,1,0:T(8,128)} %shard_map.169), calls=%async_computation.2 | async-start | bytes 196608 | tf_op jit(solution)/shard_map/all_to_all | solution.py:35
  60.1 0.7 copy-start.4
  69.8 11.0 %all-to-all-start.3 = ((bf16[16,48,128]{2,1,0:T(8,128)(2,1)}), bf16[16,48,128]{2,1,0:T(8,128)(2,1)S(1)}, u32[]{:S(2)}, u32[]{:S(2)}) async-start(bf16[16,48,128]{2,1,0:T(8,128)(2,1)} %shard_map.171), calls=%async_computation.3 | async-start | bytes 393216 | tf_op jit(solution)/shard_map/all_to_all | solution.py:35
  73.8 15.9 %collective-permute-start.3 = (bf16[2,128,1024]{2,1,0:T(8,128)(2,1)S(1)}, bf16[2,128,1024]{2,1,0:T(8,128)(2,1)S(1)}, u32[]{:S(2)}, u32[]{:S(2)}) collective-permute-start(bf16[2,128,1024]{2,1,0:T(8,128)(2,1)S(1)} %pad_maximum_fusion.refs_0_), channel_id=1, source_target_pairs={{0,1},{1,0},{2,3},{3,2},{4,5},{5,4},{6,7},{7,6},{8,9},{9,8},{10,11... | collective-permute-start | bytes 1572872 | tf_op jit(solution)/shard_map/ppermute | solution.py:39
  78.6 11.1 %collective-permute-start.4 = (bf16[2,128,1024]{2,1,0:T(8,128)(2,1)S(1)}, bf16[2,128,1024]{2,1,0:T(8,128)(2,1)S(1)}, u32[]{:S(2)}, u32[]{:S(2)}) collective-permute-start(bf16[2,128,1024]{2,1,0:T(8,128)(2,1)S(1)} %collective-permute-done.2.refs_1_), channel_id=1, source_target_pairs={{0,1},{1,0},{2,3},{3,2},{4,5},{5,4},{6,7},{7,6},{8,9},{9,8},{10,11... | collective-permute-start | bytes 1572872 | tf_op jit(solution)/shard_map/ppermute | solution.py:39
  81.6 13.2 %all-to-all-start.4 = ((bf16[8,64,128]{2,1,0:T(8,128)(2,1)}), bf16[8,64,128]{2,1,0:T(8,128)(2,1)S(1)}, u32[]{:S(2)}, u32[]{:S(2)}) async-start(bf16[8,64,128]{2,1,0:T(8,128)(2,1)} %shard_map.173), calls=%async_computation.4 | async-start | bytes 262144 | tf_op jit(solution)/shard_map/all_to_all | solution.py:35
  89.7 5.1 %copy-start.5 = (bf16[1024,128]{1,0:T(8,128)(2,1)S(1)}, bf16[1024,128]{1,0:T(8,128)(2,1)}, u32[]{:S(2)}) copy-start(bf16[1024,128]{1,0:T(8,128)(2,1)} %copy-done.4) | copy-start | bytes 786436

commit v7 on v5

--- a/solution.py
+++ b/solution.py
@@ -294,10 +294,14 @@
     pair, send = lax.optimization_barrier((pair, flat))
     second_chip = reach(send[None], 2)
     mine = jnp.sum(trade(pair, "zl").astype(F32), axis=0).astype(BF)
+    mine, moments = lax.optimization_barrier((mine, (moment_a.T, second_a.T, moment_b, second_b)))
     theirs = swap(mine)
-
     rows_a, rows_b = rank * width // kv // plane, rank // plane
     deep = rows_a + rows_b + -(rows_a + rows_b) % 16
+    piece = shape((deep, kv), F32)
+    moments = call(shard_body, (piece, piece), *map(far, moments))
+    theirs, moments = lax.optimization_barrier((theirs, moments))
+
     scale = adapter_scale / (tokens * lax.axis_size(DP))
     block = call(
         lambda *refs: gradient_body(scale, *refs),
@@ -312,12 +316,8 @@
     near = jnp.concatenate([send[None], second_chip], axis=0)
     distant = reach(near, 1)
     shard = call(sum_body, shape((lax.axis_size("zh"), deep, kv), F32), shard)
-    shard, query, moments = lax.optimization_barrier(
-        (shard, queries, (moment_a.T, second_a.T, moment_b, second_b))
-    )
+    shard, query = lax.optimization_barrier((shard, queries))
     shard = trade(shard, "zh")
-    piece = shape((deep, kv), F32)
-    moments = call(shard_body, (piece, piece), *map(far, moments))
 
     groups = rows * slots // HD
     heads = queries.shape[2] // HD
@@ -346,7 +346,11 @@
     base = call(
         base_body,
         shape((count, kv), F32),
-        *map(far, (value_matrix.reshape(pairs, 2, width, kv), near, distant, near_other, distant_other)),
+        far(value_matrix.reshape(pairs, 2, width, kv)),
+        near,
+        distant,
+        near_other,
+        distant_other,
         flops=2 * count * tensor * width * kv,
         moved=4 * 2**20,
         in_specs=[pl.BlockSpec(memory_space=pl.ANY)] * 5,

time: 92.3 us -> 92.4 us (level)
  waiting for transfers between devices: 16.1 us -> 17.5 us
    all_to_all x5, waiting for transfers between devices: 15.2 us -> 17.5 us  [trade(): return lax.all_to_all(parts, axes, 0, 0, tiled=True)]
  transfers between devices with their start and end apart: 11 -> 11, of which waited for: 6 -> 5; matrix products, arithmetic and copies ran while one was open for 2% -> 2% of each run, Pallas kernels for 12% -> 12%
where the time goes in v7:
time: 92.4 us; the launch traced here: 91.5 us
  starting transfers between devices  57.8 us (63%)
  waiting for transfers between devices  17.5 us (19%)
  Pallas kernels  13.9 us (15%)
  local copies, waits for them, and re-layouts  1.37 us (1%)
    all_to_all x5, starting transfers between devices, trade(): return lax.all_to_all(parts, axes, 0, 0, tiled=True)  32.4 us
    ppermute x4, starting transfers between devices, swap(): return lax.ppermute(value, 'core', [(0, 1), (1, 0)])  19.1 us
    all_to_all x5, waiting for transfers between devices, trade(): return lax.all_to_all(parts, axes, 0, 0, tiled=True)  17.5 us
    pallas_call x11, Pallas kernels, call(): pl.pallas_call(body, out_shape=out, cost_estimate=pl.CostEstimate(flops=f...  13.9 us
    ppermute x2, starting transfers between devices, reach(): lax.ppermute(value, 'zl', [(i, i ^ hop) for i in range(lax.axis_size('zl'...  6.25 us
  transfers between devices with their start and end apart: 11, of which 5 were waited for; matrix products, arithmetic and copies ran while one was open for 2% of the time, Pallas kernels for 12%

profile of v7, /device:TPU:1, one launch (start us, length us, event | category | flops | bytes accessed | tf_op | source)
XLA Modules:
  0.0 91.5 jit_solution(14467534054008571660)
XLA Ops:
  0.6 0.0 copy-start.4
  0.6 0.0 copy-start
  0.6 1.6 %shard_map.166 = (f32[128,128]{1,0:T(8,128)S(1)}, f32[128,128]{1,0:T(8,128)S(1)}) custom-call(bf16[256,1024]{1,0:T(8,128)(2,1)} %refs_0_.1, bf16[256,128]{1,0:T(8,128)(2,1)} %refs_1_.1, f32[64,1024]{1,0:T(8,128)} %bitcast.11, f32[64,128]{1,0:T(8,128)} %b_ref.3), custom_call_target="tpu_custom_call" | custom-call | tf_op jit(solution)/shard_map/pallas_call | solution.py:47
  2.2 8.8 %collective-permute-start = (f32[128,128]{1,0:T(8,128)S(1)}, f32[128,128]{1,0:T(8,128)S(1)}, u32[]{:S(2)}, u32[]{:S(2)}) collective-permute-start(f32[128,128]{1,0:T(8,128)S(1)} %get-tuple-element.30), channel_id=1, source_target_pairs={{0,1},{1,0},{2,3},{3,2},{4,5},{5,4},{6,7},{7,6},{8,9},{9,8},{10,11... | collective-permute-start | bytes 196616 | tf_op jit(solution)/shard_map/ppermute | solution.py:39
  11.0 1.0 %reshape.26.flat_ref = bf16[128,1024]{1,0:T(8,128)(2,1)S(1)} reshape(bf16[32,4,1024]{2,1,0:T(4,128)(2,1)} %param.24) | data formatting | bytes 524288 | tf_op jit(solution)/shard_map/reshape | solution.py:286
  12.0 0.0 copy-start.8
  12.1 0.0 copy-start.7
  12.1 0.0 collective-permute-done.theirs_ref
  12.1 0.7 shard_map.167
  12.7 3.3 %all-to-all-start = ((bf16[4,128,128]{2,1,0:T(8,128)(2,1)}), bf16[4,128,128]{2,1,0:T(8,128)(2,1)S(1)}, u32[]{:S(2)}, u32[]{:S(2)}) async-start(bf16[4,128,128]{2,1,0:T(8,128)(2,1)} %shard_map.167), calls=%async_computation | async-start | bytes 262144 | tf_op jit(solution)/shard_map/all_to_all | solution.py:35
  16.1 0.0 copy-start.2
  16.1 0.0 copy-start.3
  16.1 0.0 copy-start.6
  16.1 4.3 %collective-permute-start.2 = (bf16[1,128,1024]{2,1,0:T(8,128)(2,1)S(1)}, bf16[1,128,1024]{2,1,0:T(8,128)(2,1)S(1)}, u32[]{:S(2)}, u32[]{:S(2)}) collective-permute-start(bf16[1,128,1024]{2,1,0:T(8,128)(2,1)S(1)} %bitcast.9), channel_id=1, source_target_pairs={{0,4},{2,6},{4,0},{6,2},{1,5},{3,7},{5,1},{7,3},{8,12},{10,14},{12... | collective-permute-start | bytes 786440 | tf_op jit(solution)/shard_map/ppermute | solution.py:43
  20.4 0.5 all-to-all-done
  21.0 3.8 %collective-permute-start.1 = (bf16[128,128]{1,0:T(8,128)(2,1)S(1)}, bf16[128,128]{1,0:T(8,128)(2,1)S(1)}, u32[]{:S(2)}, u32[]{:S(2)}) collective-permute-start(bf16[128,128]{1,0:T(8,128)(2,1)S(1)} %reduce_sum.12.refs_2_), channel_id=1, source_target_pairs={{0,1},{1,0},{2,3},{3,2},{4,5},{5,4},{6,7},{7,6},{8,9},{9,8},{10,11... | collective-permute-start | bytes 98312 | tf_op jit(solution)/shard_map/ppermute | solution.py:39
  24.8 1.0 %shard_map.168 = (f32[48,128]{1,0:T(8,128)S(1)}, f32[48,128]{1,0:T(8,128)S(1)}) custom-call(f32[64,1024]{1,0:T(8,128)} %bitcast.17, f32[64,1024]{1,0:T(8,128)} %bitcast.18, f32[64,128]{1,0:T(8,128)} %moment_b_ref, f32[64,128]{1,0:T(8,128)} %second_b_ref), custom_call_target="tpu_custom_call" | custom-call | tf_op jit(solution)/shard_map/pallas_call | solution.py:47
  25.8 0.0 collective-permute-done.1.refs_3_
  25.8 0.0 copy-done.4
  25.8 0.0 copy-done
  25.9 1.0 %shard_map.169 = bf16[16,48,128]{2,1,0:T(8,128)(2,1)} custom-call(bf16[256,1024]{1,0:T(8,128)(2,1)S(1)} %copy-done, bf16[256,128]{1,0:T(8,128)(2,1)S(1)} %copy-done.4, bf16[128,128]{1,0:T(8,128)(2,1)S(1)} %reduce_sum.12.refs_2_, bf16[128,128]{1,0:T(8,128)(2,1)S(1)} %collective-permute-done.1.refs_3_), custom_call_target="tpu_custom_call" | custom-call | tf_op jit(solution)/shard_map/pallas_call | solution.py:47
  26.8 0.0 copy-start.1
  26.8 10.3 %all-to-all-start.1 = ((bf16[16,48,128]{2,1,0:T(8,128)(2,1)}), bf16[16,48,128]{2,1,0:T(8,128)(2,1)S(1)}, u32[]{:S(2)}, u32[]{:S(2)}) async-start(bf16[16,48,128]{2,1,0:T(8,128)(2,1)} %shard_map.169), calls=%async_computation.1 | async-start | bytes 393216 | tf_op jit(solution)/shard_map/all_to_all | solution.py:35
  37.1 0.0 collective-permute-done.2
  37.1 0.1 pad_maximum_fusion.refs_0_
  37.2 0.0 copy-start.5
  37.2 1.9 %collective-permute-start.3 = (bf16[2,128,1024]{2,1,0:T(8,128)(2,1)S(1)}, bf16[2,128,1024]{2,1,0:T(8,128)(2,1)S(1)}, u32[]{:S(2)}, u32[]{:S(2)}) collective-permute-start(bf16[2,128,1024]{2,1,0:T(8,128)(2,1)S(1)} %pad_maximum_fusion.refs_0_), channel_id=1, source_target_pairs={{0,2},{2,0},{4,6},{6,4},{1,3},{3,1},{5,7},{7,5},{8,10},{10,8},{12,... | collective-permute-start | bytes 1572872 | tf_op jit(solution)/shard_map/ppermute | solution.py:43
  39.1 5.0 %all-to-all-done.1.in_ref = bf16[16,48,128]{2,1,0:T(8,128)(2,1)S(1)} async-done(((bf16[16,48,128]{2,1,0:T(8,128)(2,1)}), bf16[16,48,128]{2,1,0:T(8,128)(2,1)S(1)}, u32[]{:S(2)}, u32[]{:S(2)}) %all-to-all-start.1) | async-done | bytes 196640 | tf_op jit(solution)/shard_map/all_to_all | solution.py:35
  44.1 0.7 shard_map.170
  44.8 8.2 %all-to-all-start.2 = ((f32[4,48,128]{2,1,0:T(8,128)}), f32[4,48,128]{2,1,0:T(8,128)S(1)}, u32[]{:S(2)}, u32[]{:S(2)}) async-start(f32[4,48,128]{2,1,0:T(8,128)} %shard_map.170), calls=%async_computation.2 | async-start | bytes 196608 | tf_op jit(solution)/shard_map/all_to_all | solution.py:35
  53.0 0.0 copy-done.8
  53.0 0.1 broadcast_in_dim.11
  53.0 0.1 broadcast_in_dim.12
  53.1 0.1 broadcast_in_dim.13.refs_4_
  53.2 0.0 copy-done.7
  53.2 0.1 reshape.27.refs_0_
  53.3 0.0 copy-done.2
  53.3 0.0 copy-done.3
  53.3 0.0 copy-done.6
  53.3 2.8 %shard_map.171 = (f32[1024,128]{1,0:T(8,128)S(1)}, bf16[1024,128]{1,0:T(8,128)(2,1)S(1)}) custom-call(bf16[128,1024]{1,0:T(8,128)(2,1)S(1)} %reshape.27.refs_0_, bf16[1024,128]{1,0:T(8,128)(2,1)S(1)} %bitcast.13, bf16[1024,128]{1,0:T(8,128)(2,1)S(1)} %bitcast.14, bf16[128,128]{1,0:T(8,128)(2,1)S(1)} %bitcast.15, s32[8,128]{1,0:T(8,128)S(1)} %broadcast_in_dim.13.refs_4_), custom_call_target="tpu_custom_call" | custom-call | flops 100663296 | bytes 8388608 | tf_op jit(solution)/shard_map/pallas_call | solution.py:47
  56.1 9.3 %all-to-all-done.2.in_ref = f32[4,48,128]{2,1,0:T(8,128)S(1)} async-done(((f32[4,48,128]{2,1,0:T(8,128)}), f32[4,48,128]{2,1,0:T(8,128)S(1)}, u32[]{:S(2)}, u32[]{:S(2)}) %all-to-all-start.2) | async-done | bytes 98336 | tf_op jit(solution)/shard_map/all_to_all | solution.py:35
  65.4 0.7 shard_map.172
  66.1 3.6 %all-to-all-start.3 = ((bf16[16,48,128]{2,1,0:T(8,128)(2,1)}), bf16[16,48,128]{2,1,0:T(8,128)(2,1)S(1)}, u32[]{:S(2)}, u32[]{:S(2)}) async-start(bf16[16,48,128]{2,1,0:T(8,128)(2,1)} %shard_map.172), calls=%async_computation.3 | async-start | bytes 393216 | tf_op jit(solution)/shard_map/all_to_all | solution.py:35
  69.7 0.0 collective-permute-done.3.refs_1_
  69.7 4.6 %collective-permute-start.4 = (bf16[2,128,1024]{2,1,0:T(8,128)(2,1)S(1)}, bf16[2,128,1024]{2,1,0:T(8,128)(2,1)S(1)}, u32[]{:S(2)}, u32[]{:S(2)}) collective-permute-start(bf16[2,128,1024]{2,1,0:T(8,128)(2,1)S(1)} %pad_maximum_fusion.refs_0_), channel_id=1, source_target_pairs={{0,1},{1,0},{2,3},{3,2},{4,5},{5,4},{6,7},{7,6},{8,9},{9,8},{10,11... | collective-permute-start | bytes 1572872 | tf_op jit(solution)/shard_map/ppermute | solution.py:39
  74.3 1.9 %collective-permute-start.5 = (bf16[2,128,1024]{2,1,0:T(8,128)(2,1)S(1)}, bf16[2,128,1024]{2,1,0:T(8,128)(2,1)}, u32[]{:S(2)}, u32[]{:S(2)}) collective-permute-start(bf16[2,128,1024]{2,1,0:T(8,128)(2,1)S(1)} %collective-permute-done.3.refs_1_), channel_id=1, source_target_pairs={{0,1},{1,0},{2,3},{3,2},{4,5},{5,4},{6,7},{7,6},{8,9},{9,8},{10,11... | collective-permute-start | bytes 1572872 | tf_op jit(solution)/shard_map/ppermute | solution.py:39
  76.2 0.4 all-to-all-done.3.step_ref
  76.6 0.0 copy-done.1
  76.6 0.9 shard_map.174
  77.5 7.1 %all-to-all-start.4 = ((bf16[8,64,128]{2,1,0:T(8,128)(2,1)}), bf16[8,64,128]{2,1,0:T(8,128)(2,1)S(1)}, u32[]{:S(2)}, u32[]{:S(2)}) async-start(bf16[8,64,128]{2,1,0:T(8,128)(2,1)} %shard_map.174), calls=%async_computation.4 | async-start | bytes 262144 | tf_op jit(solution)/shard_map/all_to_all | solution.py:35
  84.6 0.0 copy-done.5
  84.6 0.7 shard_map.173
  85.3 0.0 collective-permute-done.4.refs_2_
  85.3 0.0 collective-permute-done.5.refs_3_
  85.3 2.8 %shard_map.175.refs_2_ = f32[128,128]{1,0:T(8,128)S(1)} custom-call(bf16[4,2,1024,128]{3,2,1,0:T(8,128)(2,1)} %bitcast.16, bf16[2,128,1024]{2,1,0:T(8,128)(2,1)S(1)} %pad_maximum_fusion.refs_0_, bf16[2,128,1024]{2,1,0:T(8,128)(2,1)S(1)} %collective-permute-done.3.refs_1_, bf16[2,128,1024]{2,1,0:T(8,128)(2,1)S(1)} %collective-permute-done.4.refs_2_, ...), custom_call_target="tpu_custom_call" | custom-call | flops 268435456 | bytes 4194304 | tf_op jit(solution)/shard_map/pallas_call | solution.py:47
  88.1 2.3 %all-to-all-done.4.refs_0_ = bf16[8,64,128]{2,1,0:T(8,128)(2,1)S(1)} async-done(((bf16[8,64,128]{2,1,0:T(8,128)(2,1)}), bf16[8,64,128]{2,1,0:T(8,128)(2,1)S(1)}, u32[]{:S(2)}, u32[]{:S(2)}) %all-to-all-start.4) | async-done | bytes 131104 | tf_op jit(solution)/shard_map/all_to_all | solution.py:35
  90.4 1.1 %shard_map.176 = bf16[32,4,1024]{2,1,0:T(4,128)(2,1)} custom-call(bf16[8,64,128]{2,1,0:T(8,128)(2,1)S(1)} %all-to-all-done.4.refs_0_, bf16[64,128]{1,0:T(8,128)(2,1)S(1)} %get-tuple-element.49.refs_1_, f32[128,128]{1,0:T(8,128)S(1)} %shard_map.175.refs_2_, f32[1024,128]{1,0:T(8,128)S(1)} %get-tuple-element.53.refs_3_, ...), custom_call_target="tpu_custom_call" | custom-call | tf_op jit(solution)/shard_map/pallas_call | solution.py:47
  (1 shorter events, 0.0 us)
Async XLA Ops:
  0.6 25.2 %copy-start.4 = (bf16[256,128]{1,0:T(8,128)(2,1)S(1)}, bf16[256,128]{1,0:T(8,128)(2,1)}, u32[]{:S(2)}) copy-start(bf16[256,128]{1,0:T(8,128)(2,1)} %refs_1_.1) | copy-start | bytes 196612
  0.6 25.2 %copy-start = (bf16[256,1024]{1,0:T(8,128)(2,1)S(1)}, bf16[256,1024]{1,0:T(8,128)(2,1)}, u32[]{:S(2)}) copy-start(bf16[256,1024]{1,0:T(8,128)(2,1)} %refs_0_.1) | copy-start | bytes 1572868
  2.2 9.8 %collective-permute-start = (f32[128,128]{1,0:T(8,128)S(1)}, f32[128,128]{1,0:T(8,128)S(1)}, u32[]{:S(2)}, u32[]{:S(2)}) collective-permute-start(f32[128,128]{1,0:T(8,128)S(1)} %get-tuple-element.30), channel_id=1, source_target_pairs={{0,1},{1,0},{2,3},{3,2},{4,5},{5,4},{6,7},{7,6},{8,9},{9,8},{10,11... | collective-permute-start | bytes 196616 | tf_op jit(solution)/shard_map/ppermute | solution.py:39
  12.0 40.9 %copy-start.8 = (s32[32]{0:T(128)S(1)}, s32[32]{0:T(128)}, u32[]{:S(2)}) copy-start(s32[32]{0:T(128)} %param.29) | copy-start | bytes 388
  12.1 41.1 %copy-start.7 = (bf16[32,4,1024]{2,1,0:T(4,128)(2,1)S(1)}, bf16[32,4,1024]{2,1,0:T(4,128)(2,1)}, u32[]{:S(2)}) copy-start(bf16[32,4,1024]{2,1,0:T(4,128)(2,1)} %param.26) | copy-start | bytes 786436
  12.7 8.2 %all-to-all-start = ((bf16[4,128,128]{2,1,0:T(8,128)(2,1)}), bf16[4,128,128]{2,1,0:T(8,128)(2,1)S(1)}, u32[]{:S(2)}, u32[]{:S(2)}) async-start(bf16[4,128,128]{2,1,0:T(8,128)(2,1)} %shard_map.167), calls=%async_computation | async-start | bytes 262144 | tf_op jit(solution)/shard_map/all_to_all | solution.py:35
  16.1 37.2 %copy-start.2 = (bf16[32,32,128]{2,1,0:T(8,128)(2,1)S(1)}, bf16[32,32,128]{2,1,0:T(8,128)(2,1)}, u32[]{:S(2)}) copy-start(bf16[32,32,128]{2,1,0:T(8,128)(2,1)} %param.27) | copy-start | bytes 786436
  16.1 37.2 %copy-start.3 = (bf16[32,32,128]{2,1,0:T(8,128)(2,1)S(1)}, bf16[32,32,128]{2,1,0:T(8,128)(2,1)}, u32[]{:S(2)}) copy-start(bf16[32,32,128]{2,1,0:T(8,128)(2,1)} %param.28) | copy-start | bytes 786436
  16.1 37.2 %copy-start.6 = (bf16[32,4,128]{2,1,0:T(4,128)(2,1)S(1)}, bf16[32,4,128]{2,1,0:T(4,128)(2,1)}, u32[]{:S(2)}) copy-start(bf16[32,4,128]{2,1,0:T(4,128)(2,1)} %param.25) | copy-start | bytes 98308
  16.1 21.0 %collective-permute-start.2 = (bf16[1,128,1024]{2,1,0:T(8,128)(2,1)S(1)}, bf16[1,128,1024]{2,1,0:T(8,128)(2,1)S(1)}, u32[]{:S(2)}, u32[]{:S(2)}) collective-permute-start(bf16[1,128,1024]{2,1,0:T(8,128)(2,1)S(1)} %bitcast.9), channel_id=1, source_target_pairs={{0,4},{2,6},{4,0},{6,2},{1,5},{3,7},{5,1},{7,3},{8,12},{10,14},{12... | collective-permute-start | bytes 786440 | tf_op jit(solution)/shard_map/ppermute | solution.py:43
  21.0 4.9 %collective-permute-start.1 = (bf16[128,128]{1,0:T(8,128)(2,1)S(1)}, bf16[128,128]{1,0:T(8,128)(2,1)S(1)}, u32[]{:S(2)}, u32[]{:S(2)}) collective-permute-start(bf16[128,128]{1,0:T(8,128)(2,1)S(1)} %reduce_sum.12.refs_2_), channel_id=1, source_target_pairs={{0,1},{1,0},{2,3},{3,2},{4,5},{5,4},{6,7},{7,6},{8,9},{9,8},{10,11... | collective-permute-start | bytes 98312 | tf_op jit(solution)/shard_map/ppermute | solution.py:39
  26.8 49.8 %copy-start.1 = (f32[1024,64]{0,1:T(8,128)S(1)}, f32[1024,64]{0,1:T(8,128)}, u32[]{:S(2)}) copy-start(f32[1024,64]{0,1:T(8,128)} %param.17) | copy-start | bytes 786436
  26.8 17.3 %all-to-all-start.1 = ((bf16[16,48,128]{2,1,0:T(8,128)(2,1)}), bf16[16,48,128]{2,1,0:T(8,128)(2,1)S(1)}, u32[]{:S(2)}, u32[]{:S(2)}) async-start(bf16[16,48,128]{2,1,0:T(8,128)(2,1)} %shard_map.169), calls=%async_computation.1 | async-start | bytes 393216 | tf_op jit(solution)/shard_map/all_to_all | solution.py:35
  37.2 47.4 %copy-start.5 = (f32[64,128]{1,0:T(8,128)S(1)}, f32[64,128]{1,0:T(8,128)}, u32[]{:S(2)}) copy-start(f32[64,128]{1,0:T(8,128)} %b_ref.3) | copy-start | bytes 98308
  37.2 32.5 %collective-permute-start.3 = (bf16[2,128,1024]{2,1,0:T(8,128)(2,1)S(1)}, bf16[2,128,1024]{2,1,0:T(8,128)(2,1)S(1)}, u32[]{:S(2)}, u32[]{:S(2)}) collective-permute-start(bf16[2,128,1024]{2,1,0:T(8,128)(2,1)S(1)} %pad_maximum_fusion.refs_0_), channel_id=1, source_target_pairs={{0,2},{2,0},{4,6},{6,4},{1,3},{3,1},{5,7},{7,5},{8,10},{10,8},{12,... | collective-permute-start | bytes 1572872 | tf_op jit(solution)/shard_map/ppermute | solution.py:43
  44.8 20.6 %all-to-all-start.2 = ((f32[4,48,128]{2,1,0:T(8,128)}), f32[4,48,128]{2,1,0:T(8,128)S(1)}, u32[]{:S(2)}, u32[]{:S(2)}) async-start(f32[4,48,128]{2,1,0:T(8,128)} %shard_map.170), calls=%async_computation.2 | async-start | bytes 196608 | tf_op jit(solution)/shard_map/all_to_all | solution.py:35
  66.1 10.5 %all-to-all-start.3 = ((bf16[16,48,128]{2,1,0:T(8,128)(2,1)}), bf16[16,48,128]{2,1,0:T(8,128)(2,1)S(1)}, u32[]{:S(2)}, u32[]{:S(2)}) async-start(bf16[16,48,128]{2,1,0:T(8,128)(2,1)} %shard_map.172), calls=%async_computation.3 | async-start | bytes 393216 | tf_op jit(solution)/shard_map/all_to_all | solution.py:35
  69.7 15.6 %collective-permute-start.4 = (bf16[2,128,1024]{2,1,0:T(8,128)(2,1)S(1)}, bf16[2,128,1024]{2,1,0:T(8,128)(2,1)S(1)}, u32[]{:S(2)}, u32[]{:S(2)}) collective-permute-start(bf16[2,128,1024]{2,1,0:T(8,128)(2,1)S(1)} %pad_maximum_fusion.refs_0_), channel_id=1, source_target_pairs={{0,1},{1,0},{2,3},{3,2},{4,5},{5,4},{6,7},{7,6},{8,9},{9,8},{10,11... | collective-permute-start | bytes 1572872 | tf_op jit(solution)/shard_map/ppermute | solution.py:39
  74.3 11.0 %collective-permute-start.5 = (bf16[2,128,1024]{2,1,0:T(8,128)(2,1)S(1)}, bf16[2,128,1024]{2,1,0:T(8,128)(2,1)}, u32[]{:S(2)}, u32[]{:S(2)}) collective-permute-start(bf16[2,128,1024]{2,1,0:T(8,128)(2,1)S(1)} %collective-permute-done.3.refs_1_), channel_id=1, source_target_pairs={{0,1},{1,0},{2,3},{3,2},{4,5},{5,4},{6,7},{7,6},{8,9},{9,8},{10,11... | collective-permute-start | bytes 1572872 | tf_op jit(solution)/shard_map/ppermute | solution.py:39
  77.5 12.9 %all-to-all-start.4 = ((bf16[8,64,128]{2,1,0:T(8,128)(2,1)}), bf16[8,64,128]{2,1,0:T(8,128)(2,1)S(1)}, u32[]{:S(2)}, u32[]{:S(2)}) async-start(bf16[8,64,128]{2,1,0:T(8,128)(2,1)} %shard_map.174), calls=%async_computation.4 | async-start | bytes 262144 | tf_op jit(solution)/shard_map/all_to_all | solution.py:35

commit v8 on v7

--- a/solution.py
+++ b/solution.py
@@ -286,13 +286,13 @@
     flat = lax.optimization_barrier(decode_states.reshape(count, width))
     a_turned = adapter_a.T
 
+    second_chip = reach(decode_states, 2)
+
     half = shape((tokens // 2, two), F32)
     starts = (trainer_token_input, cotangent, a_turned, adapter_b)
     mine, theirs = call(low_body, (half, half), *map(far, starts))
     pair = call(pair_body, shape((pairs, tokens // 2, two), BF), mine, swap(theirs))
 
-    pair, send = lax.optimization_barrier((pair, flat))
-    second_chip = reach(send[None], 2)
     mine = jnp.sum(trade(pair, "zl").astype(F32), axis=0).astype(BF)
     mine, moments = lax.optimization_barrier((mine, (moment_a.T, second_a.T, moment_b, second_b)))
     theirs = swap(mine)
@@ -313,7 +313,7 @@
     )
 
     shard = trade(block, PLANE)
-    near = jnp.concatenate([send[None], second_chip], axis=0)
+    near = jnp.stack([flat, second_chip.reshape(count, width)])
     distant = reach(near, 1)
     shard = call(sum_body, shape((lax.axis_size("zh"), deep, kv), F32), shard)
     shard, query = lax.optimization_barrier((shard, queries))
@@ -334,15 +334,9 @@
     )
     shard, old, weights = lax.optimization_barrier((shard, old, weights))
     step = call(adam_body, shape((plane, deep, kv), BF), shard, *moments)
-    distant_sent, near_sent, _ = lax.optimization_barrier((distant, near, step))
-    distant_other, near_other = swap(distant_sent), swap(near_sent)
+    distant_other, near_other = swap(distant), swap(near)
     step = trade(step, PLANE)
 
-    inner = call(inner_body, shape((tensor, rank, count), BF), step, a_turned, flat)
-    inner = trade(inner, TENSOR)
-    step_a, step_b, new_b = call(
-        step_body, (shape((rank, width), F32), shape((rank, kv), F32), shape((rank, kv), BF)), step, adapter_b
-    )
     base = call(
         base_body,
         shape((count, kv), F32),
@@ -359,6 +353,14 @@
             pltpu.VMEM((pairs, 2, width, kv), BF),
             pltpu.SemaphoreType.DMA((pairs, 2, 2)),
         ],
+    )
+
+    step, base = lax.optimization_barrier((step, base))
+
+    inner = call(inner_body, shape((tensor, rank, count), BF), step, a_turned, flat)
+    inner = trade(inner, TENSOR)
+    step_a, step_b, new_b = call(
+        step_body, (shape((rank, width), F32), shape((rank, kv), F32), shape((rank, kv), BF)), step, adapter_b
     )
 
     attended = call(

time: 92.4 us -> 98.4 us (1.065)
  local copies, waits for them, and re-layouts: 1.37 us -> 4.97 us
  waiting for transfers between devices: 17.5 us -> 19.4 us
    ppermute x4, starting transfers between devices: 19.1 us -> 13.3 us  [swap(): return lax.ppermute(value, 'core', [(0, 1), (1, 0)])]
    unnamed x18 -> x22, local copies, waits for them, and re-layouts: 0.05 us -> 3.59 us
    all_to_all x5, starting transfers between devices: 32.4 us -> 35.7 us  [trade(): return lax.all_to_all(parts, axes, 0, 0, tiled=True)]
    ppermute x2, starting transfers between devices: 6.25 us -> 9.1 us  [reach(): lax.ppermute(value, 'zl', [(i, i ^ hop) for i in range(lax.axis_size('zl'...]
    all_to_all x5, waiting for transfers between devices: 17.5 us -> 19.4 us  [trade(): return lax.all_to_all(parts, axes, 0, 0, tiled=True)]
  transfers between devices with their start and end apart: 11 -> 11, of which waited for: 5 -> 5; matrix products, arithmetic and copies ran while one was open for 2% -> 1% of each run, Pallas kernels for 12% -> 12%
where the time goes in v8:
time: 98.4 us; the launch traced here: 97.4 us
  starting transfers between devices  58.1 us (59%)
  waiting for transfers between devices  19.4 us (20%)
  Pallas kernels  14 us (14%)
  local copies, waits for them, and re-layouts  4.97 us (5%)
    all_to_all x5, starting transfers between devices, trade(): return lax.all_to_all(parts, axes, 0, 0, tiled=True)  35.7 us
    all_to_all x5, waiting for transfers between devices, trade(): return lax.all_to_all(parts, axes, 0, 0, tiled=True)  19.4 us
    pallas_call x11, Pallas kernels, call(): pl.pallas_call(body, out_shape=out, cost_estimate=pl.CostEstimate(flops=f...  14 us
    ppermute x4, starting transfers between devices, swap(): return lax.ppermute(value, 'core', [(0, 1), (1, 0)])  13.3 us
    ppermute x2, starting transfers between devices, reach(): lax.ppermute(value, 'zl', [(i, i ^ hop) for i in range(lax.axis_size('zl'...  9.1 us
    unnamed x22, local copies, waits for them, and re-layouts  3.59 us
  transfers between devices with their start and end apart: 11, of which 5 were waited for; matrix products, arithmetic and copies ran while one was open for 1% of the time, Pallas kernels for 12%

profile of v8, /device:TPU:1, one launch (start us, length us, event | category | flops | bytes accessed | tf_op | source)
XLA Modules:
  0.0 97.4 jit_solution(11983782433668960219)
XLA Ops:
  0.6 5.7 %collective-permute-start.2 = (bf16[32,4,1024]{2,1,0:T(4,128)(2,1)}, bf16[32,4,1024]{2,1,0:T(4,128)(2,1)S(1)}, u32[]{:S(2)}, u32[]{:S(2)}) collective-permute-start(bf16[32,4,1024]{2,1,0:T(4,128)(2,1)} %param.24), channel_id=1, source_target_pairs={{0,4},{2,6},{4,0},{6,2},{1,5},{3,7},{5,1},{7,3},{8,12},{10,14},{12... | collective-permute-start | bytes 786440 | tf_op jit(solution)/shard_map/ppermute | solution.py:43
  6.4 0.0 copy-start
  6.4 0.0 copy-start.6
  6.4 1.6 %shard_map.166 = (f32[128,128]{1,0:T(8,128)S(1)}, f32[128,128]{1,0:T(8,128)S(1)}) custom-call(bf16[256,1024]{1,0:T(8,128)(2,1)} %refs_0_.1, bf16[256,128]{1,0:T(8,128)(2,1)} %refs_1_.1, f32[64,1024]{1,0:T(8,128)} %bitcast.10, f32[64,128]{1,0:T(8,128)} %b_ref.3), custom_call_target="tpu_custom_call" | custom-call | tf_op jit(solution)/shard_map/pallas_call | solution.py:47
  8.0 5.0 %collective-permute-start = (f32[128,128]{1,0:T(8,128)S(1)}, f32[128,128]{1,0:T(8,128)S(1)}, u32[]{:S(2)}, u32[]{:S(2)}) collective-permute-start(f32[128,128]{1,0:T(8,128)S(1)} %get-tuple-element.28), channel_id=1, source_target_pairs={{0,1},{1,0},{2,3},{3,2},{4,5},{5,4},{6,7},{7,6},{8,9},{9,8},{10,11... | collective-permute-start | bytes 196616 | tf_op jit(solution)/shard_map/ppermute | solution.py:39
  13.0 1.0 %reshape.31.flat_ref = bf16[128,1024]{1,0:T(8,128)(2,1)S(1)} reshape(bf16[32,4,1024]{2,1,0:T(4,128)(2,1)} %param.24) | data formatting | bytes 524288 | tf_op jit(solution)/shard_map/reshape | solution.py:286
  14.0 0.0 collective-permute-done.theirs_ref
  14.0 0.7 shard_map.167
  14.7 3.9 %all-to-all-start = ((bf16[4,128,128]{2,1,0:T(8,128)(2,1)}), bf16[4,128,128]{2,1,0:T(8,128)(2,1)S(1)}, u32[]{:S(2)}, u32[]{:S(2)}) async-start(bf16[4,128,128]{2,1,0:T(8,128)(2,1)} %shard_map.167), calls=%async_computation | async-start | bytes 262144 | tf_op jit(solution)/shard_map/all_to_all | solution.py:35
  18.6 0.0 copy-start.10
  18.6 0.0 copy-start.9
  18.6 0.0 collective-permute-done.2
  18.6 0.1 stack_reshape.3
  18.6 0.0 copy-start.8
  18.6 0.1 pad_maximum_fusion.refs_0_
  18.7 3.4 %collective-permute-start.3 = (bf16[2,128,1024]{2,1,0:T(8,128)(2,1)S(1)}, bf16[2,128,1024]{2,1,0:T(8,128)(2,1)S(1)}, u32[]{:S(2)}, u32[]{:S(2)}) collective-permute-start(bf16[2,128,1024]{2,1,0:T(8,128)(2,1)S(1)} %pad_maximum_fusion.refs_0_), channel_id=1, source_target_pairs={{0,2},{2,0},{4,6},{6,4},{1,3},{3,1},{5,7},{7,5},{8,10},{10,8},{12,... | collective-permute-start | bytes 1572872 | tf_op jit(solution)/shard_map/ppermute | solution.py:43
  22.1 1.3 %all-to-all-done = bf16[4,128,128]{2,1,0:T(8,128)(2,1)S(1)} async-done(((bf16[4,128,128]{2,1,0:T(8,128)(2,1)}), bf16[4,128,128]{2,1,0:T(8,128)(2,1)S(1)}, u32[]{:S(2)}, u32[]{:S(2)}) %all-to-all-start) | async-done | bytes 131104 | tf_op jit(solution)/shard_map/all_to_all | solution.py:35
  23.4 4.0 %collective-permute-start.1 = (bf16[128,128]{1,0:T(8,128)(2,1)S(1)}, bf16[128,128]{1,0:T(8,128)(2,1)S(1)}, u32[]{:S(2)}, u32[]{:S(2)}) collective-permute-start(bf16[128,128]{1,0:T(8,128)(2,1)S(1)} %reduce_sum.12.refs_2_), channel_id=1, source_target_pairs={{0,1},{1,0},{2,3},{3,2},{4,5},{5,4},{6,7},{7,6},{8,9},{9,8},{10,11... | collective-permute-start | bytes 98312 | tf_op jit(solution)/shard_map/ppermute | solution.py:39
  27.4 1.0 %shard_map.168 = (f32[48,128]{1,0:T(8,128)S(1)}, f32[48,128]{1,0:T(8,128)S(1)}) custom-call(f32[64,1024]{1,0:T(8,128)} %bitcast.16, f32[64,1024]{1,0:T(8,128)} %bitcast.17, f32[64,128]{1,0:T(8,128)} %moment_b_ref, f32[64,128]{1,0:T(8,128)} %second_b_ref), custom_call_target="tpu_custom_call" | custom-call | tf_op jit(solution)/shard_map/pallas_call | solution.py:47
  28.5 0.0 collective-permute-done.1.refs_3_
  28.5 0.0 copy-done
  28.5 0.0 copy-done.6
  28.5 1.0 shard_map.169
  29.5 5.1 %all-to-all-start.1 = ((bf16[16,48,128]{2,1,0:T(8,128)(2,1)}), bf16[16,48,128]{2,1,0:T(8,128)(2,1)S(1)}, u32[]{:S(2)}, u32[]{:S(2)}) async-start(bf16[16,48,128]{2,1,0:T(8,128)(2,1)} %shard_map.169), calls=%async_computation.1 | async-start | bytes 393216 | tf_op jit(solution)/shard_map/all_to_all | solution.py:35
  34.6 2.3 %collective-permute-start.4 = (bf16[2,128,1024]{2,1,0:T(8,128)(2,1)S(1)}, bf16[2,128,1024]{2,1,0:T(8,128)(2,1)S(1)}, u32[]{:S(2)}, u32[]{:S(2)}) collective-permute-start(bf16[2,128,1024]{2,1,0:T(8,128)(2,1)S(1)} %pad_maximum_fusion.refs_0_), channel_id=1, source_target_pairs={{0,1},{1,0},{2,3},{3,2},{4,5},{5,4},{6,7},{7,6},{8,9},{9,8},{10,11... | collective-permute-start | bytes 1572872 | tf_op jit(solution)/shard_map/ppermute | solution.py:39
  36.9 0.0 collective-permute-done.3.refs_1_
  36.9 2.1 %collective-permute-start.5 = (bf16[2,128,1024]{2,1,0:T(8,128)(2,1)S(1)}, bf16[2,128,1024]{2,1,0:T(8,128)(2,1)S(1)}, u32[]{:S(2)}, u32[]{:S(2)}) collective-permute-start(bf16[2,128,1024]{2,1,0:T(8,128)(2,1)S(1)} %collective-permute-done.3.refs_1_), channel_id=1, source_target_pairs={{0,1},{1,0},{2,3},{3,2},{4,5},{5,4},{6,7},{7,6},{8,9},{9,8},{10,11... | collective-permute-start | bytes 1572872 | tf_op jit(solution)/shard_map/ppermute | solution.py:39
  39.0 2.6 %all-to-all-done.1.in_ref = bf16[16,48,128]{2,1,0:T(8,128)(2,1)S(1)} async-done(((bf16[16,48,128]{2,1,0:T(8,128)(2,1)}), bf16[16,48,128]{2,1,0:T(8,128)(2,1)S(1)}, u32[]{:S(2)}, u32[]{:S(2)}) %all-to-all-start.1) | async-done | bytes 196640 | tf_op jit(solution)/shard_map/all_to_all | solution.py:35
  41.6 0.7 shard_map.170
  42.3 13.0 %all-to-all-start.2 = ((f32[4,48,128]{2,1,0:T(8,128)}), f32[4,48,128]{2,1,0:T(8,128)S(1)}, u32[]{:S(2)}, u32[]{:S(2)}) async-start(f32[4,48,128]{2,1,0:T(8,128)} %shard_map.170), calls=%async_computation.2 | async-start | bytes 196608 | tf_op jit(solution)/shard_map/all_to_all | solution.py:35
  55.3 0.0 copy-done.10
  55.3 0.1 broadcast_in_dim.7
  55.4 0.1 broadcast_in_dim.8
  55.5 0.1 broadcast_in_dim.9.refs_4_
  55.5 0.0 copy-done.9
  55.6 0.1 reshape.26.refs_0_
  55.6 0.0 copy-done.8
  55.6 0.0 copy-start.2
  55.7 0.9 copy-done.2
  56.6 0.0 copy-start.3
  56.6 0.9 copy-done.3
  57.5 2.8 %shard_map.171 = (f32[1024,128]{1,0:T(8,128)S(1)}, bf16[1024,128]{1,0:T(8,128)(2,1)S(1)}) custom-call(bf16[128,1024]{1,0:T(8,128)(2,1)S(1)} %reshape.26.refs_0_, bf16[1024,128]{1,0:T(8,128)(2,1)S(1)} %bitcast.12, bf16[1024,128]{1,0:T(8,128)(2,1)S(1)} %bitcast.13, bf16[128,128]{1,0:T(8,128)(2,1)S(1)} %bitcast.14, s32[8,128]{1,0:T(8,128)S(1)} %broadcast_in_dim.9.refs_4_), custom_call_target="tpu_custom_call" | custom-call | flops 100663296 | bytes 8388608 | tf_op jit(solution)/shard_map/pallas_call | solution.py:47
  60.3 0.0 copy-start.4
  60.3 0.7 copy-done.4
  61.0 6.4 %all-to-all-done.2.in_ref = f32[4,48,128]{2,1,0:T(8,128)S(1)} async-done(((f32[4,48,128]{2,1,0:T(8,128)}), f32[4,48,128]{2,1,0:T(8,128)S(1)}, u32[]{:S(2)}, u32[]{:S(2)}) %all-to-all-start.2) | async-done | bytes 98336 | tf_op jit(solution)/shard_map/all_to_all | solution.py:35
  67.4 0.7 shard_map.172
  68.1 4.2 %all-to-all-start.3 = ((bf16[16,48,128]{2,1,0:T(8,128)(2,1)}), bf16[16,48,128]{2,1,0:T(8,128)(2,1)S(1)}, u32[]{:S(2)}, u32[]{:S(2)}) async-start(bf16[16,48,128]{2,1,0:T(8,128)(2,1)} %shard_map.172), calls=%async_computation.3 | async-start | bytes 393216 | tf_op jit(solution)/shard_map/all_to_all | solution.py:35
  72.3 0.0 collective-permute-done.4.refs_2_
  72.3 0.0 collective-permute-done.5.refs_3_
  72.3 0.0 copy-start.1
  72.3 0.0 copy-start.7
  72.3 2.9 %shard_map.173.refs_2_ = f32[128,128]{1,0:T(8,128)S(1)} custom-call(bf16[4,2,1024,128]{3,2,1,0:T(8,128)(2,1)} %bitcast.15, bf16[2,128,1024]{2,1,0:T(8,128)(2,1)S(1)} %pad_maximum_fusion.refs_0_, bf16[2,128,1024]{2,1,0:T(8,128)(2,1)S(1)} %collective-permute-done.3.refs_1_, bf16[2,128,1024]{2,1,0:T(8,128)(2,1)S(1)} %collective-permute-done.4.refs_2_, ...), custom_call_target="tpu_custom_call" | custom-call | flops 268435456 | bytes 4194304 | tf_op jit(solution)/shard_map/pallas_call | solution.py:47
  75.2 4.0 %all-to-all-done.3.step_ref = bf16[16,48,128]{2,1,0:T(8,128)(2,1)S(1)} async-done(((bf16[16,48,128]{2,1,0:T(8,128)(2,1)}), bf16[16,48,128]{2,1,0:T(8,128)(2,1)S(1)}, u32[]{:S(2)}, u32[]{:S(2)}) %all-to-all-start.3) | async-done | bytes 196640 | tf_op jit(solution)/shard_map/all_to_all | solution.py:35
  79.2 0.0 copy-done.1
  79.2 0.9 shard_map.175
  80.1 9.4 %all-to-all-start.4 = ((bf16[8,64,128]{2,1,0:T(8,128)(2,1)}), bf16[8,64,128]{2,1,0:T(8,128)(2,1)S(1)}, u32[]{:S(2)}, u32[]{:S(2)}) async-start(bf16[8,64,128]{2,1,0:T(8,128)(2,1)} %shard_map.175), calls=%async_computation.4 | async-start | bytes 262144 | tf_op jit(solution)/shard_map/all_to_all | solution.py:35
  89.5 0.0 copy-done.7
  89.5 0.7 shard_map.174
  90.3 5.1 %all-to-all-done.4.refs_0_ = bf16[8,64,128]{2,1,0:T(8,128)(2,1)S(1)} async-done(((bf16[8,64,128]{2,1,0:T(8,128)(2,1)}), bf16[8,64,128]{2,1,0:T(8,128)(2,1)S(1)}, u32[]{:S(2)}, u32[]{:S(2)}) %all-to-all-start.4) | async-done | bytes 131104 | tf_op jit(solution)/shard_map/all_to_all | solution.py:35
  95.4 0.0 copy-start.5
  95.4 0.9 copy-done.5
  96.3 1.1 %shard_map.176 = bf16[32,4,1024]{2,1,0:T(4,128)(2,1)} custom-call(bf16[8,64,128]{2,1,0:T(8,128)(2,1)S(1)} %all-to-all-done.4.refs_0_, bf16[64,128]{1,0:T(8,128)(2,1)S(1)} %get-tuple-element.47.refs_1_, f32[128,128]{1,0:T(8,128)S(1)} %shard_map.173.refs_2_, f32[1024,128]{1,0:T(8,128)S(1)} %get-tuple-element.49.refs_3_, bf16[1024,128]{1,0:T(8,128)(2,1)S(1)} %copy-done.5), custom_call_target="tpu_custom_call" | custom-call | tf_op jit(solution)/shard_map/pallas_call | solution.py:47
  (1 shorter events, 0.0 us)
Async XLA Ops:
  0.6 17.9 %collective-permute-start.2 = (bf16[32,4,1024]{2,1,0:T(4,128)(2,1)}, bf16[32,4,1024]{2,1,0:T(4,128)(2,1)S(1)}, u32[]{:S(2)}, u32[]{:S(2)}) collective-permute-start(bf16[32,4,1024]{2,1,0:T(4,128)(2,1)} %param.24), channel_id=1, source_target_pairs={{0,4},{2,6},{4,0},{6,2},{1,5},{3,7},{5,1},{7,3},{8,12},{10,14},{12... | collective-permute-start | bytes 786440 | tf_op jit(solution)/shard_map/ppermute | solution.py:43
  6.4 22.1 %copy-start = (bf16[256,1024]{1,0:T(8,128)(2,1)S(1)}, bf16[256,1024]{1,0:T(8,128)(2,1)}, u32[]{:S(2)}) copy-start(bf16[256,1024]{1,0:T(8,128)(2,1)} %refs_0_.1) | copy-start | bytes 1572868
  6.4 22.1 %copy-start.6 = (bf16[256,128]{1,0:T(8,128)(2,1)S(1)}, bf16[256,128]{1,0:T(8,128)(2,1)}, u32[]{:S(2)}) copy-start(bf16[256,128]{1,0:T(8,128)(2,1)} %refs_1_.1) | copy-start | bytes 196612
  8.0 6.0 %collective-permute-start = (f32[128,128]{1,0:T(8,128)S(1)}, f32[128,128]{1,0:T(8,128)S(1)}, u32[]{:S(2)}, u32[]{:S(2)}) collective-permute-start(f32[128,128]{1,0:T(8,128)S(1)} %get-tuple-element.28), channel_id=1, source_target_pairs={{0,1},{1,0},{2,3},{3,2},{4,5},{5,4},{6,7},{7,6},{8,9},{9,8},{10,11... | collective-permute-start | bytes 196616 | tf_op jit(solution)/shard_map/ppermute | solution.py:39
  14.7 8.7 %all-to-all-start = ((bf16[4,128,128]{2,1,0:T(8,128)(2,1)}), bf16[4,128,128]{2,1,0:T(8,128)(2,1)S(1)}, u32[]{:S(2)}, u32[]{:S(2)}) async-start(bf16[4,128,128]{2,1,0:T(8,128)(2,1)} %shard_map.167), calls=%async_computation | async-start | bytes 262144 | tf_op jit(solution)/shard_map/all_to_all | solution.py:35
  18.6 36.8 %copy-start.10 = (s32[32]{0:T(128)S(1)}, s32[32]{0:T(128)}, u32[]{:S(2)}) copy-start(s32[32]{0:T(128)} %param.29) | copy-start | bytes 388
  18.6 37.0 %copy-start.9 = (bf16[32,4,1024]{2,1,0:T(4,128)(2,1)S(1)}, bf16[32,4,1024]{2,1,0:T(4,128)(2,1)}, u32[]{:S(2)}) copy-start(bf16[32,4,1024]{2,1,0:T(4,128)(2,1)} %param.26) | copy-start | bytes 786436
  18.6 37.0 %copy-start.8 = (bf16[32,4,128]{2,1,0:T(4,128)(2,1)S(1)}, bf16[32,4,128]{2,1,0:T(4,128)(2,1)}, u32[]{:S(2)}) copy-start(bf16[32,4,128]{2,1,0:T(4,128)(2,1)} %param.25) | copy-start | bytes 98308
  18.7 18.2 %collective-permute-start.3 = (bf16[2,128,1024]{2,1,0:T(8,128)(2,1)S(1)}, bf16[2,128,1024]{2,1,0:T(8,128)(2,1)S(1)}, u32[]{:S(2)}, u32[]{:S(2)}) collective-permute-start(bf16[2,128,1024]{2,1,0:T(8,128)(2,1)S(1)} %pad_maximum_fusion.refs_0_), channel_id=1, source_target_pairs={{0,2},{2,0},{4,6},{6,4},{1,3},{3,1},{5,7},{7,5},{8,10},{10,8},{12,... | collective-permute-start | bytes 1572872 | tf_op jit(solution)/shard_map/ppermute | solution.py:43
  23.4 5.1 %collective-permute-start.1 = (bf16[128,128]{1,0:T(8,128)(2,1)S(1)}, bf16[128,128]{1,0:T(8,128)(2,1)S(1)}, u32[]{:S(2)}, u32[]{:S(2)}) collective-permute-start(bf16[128,128]{1,0:T(8,128)(2,1)S(1)} %reduce_sum.12.refs_2_), channel_id=1, source_target_pairs={{0,1},{1,0},{2,3},{3,2},{4,5},{5,4},{6,7},{7,6},{8,9},{9,8},{10,11... | collective-permute-start | bytes 98312 | tf_op jit(solution)/shard_map/ppermute | solution.py:39
  29.5 12.1 %all-to-all-start.1 = ((bf16[16,48,128]{2,1,0:T(8,128)(2,1)}), bf16[16,48,128]{2,1,0:T(8,128)(2,1)S(1)}, u32[]{:S(2)}, u32[]{:S(2)}) async-start(bf16[16,48,128]{2,1,0:T(8,128)(2,1)} %shard_map.169), calls=%async_computation.1 | async-start | bytes 393216 | tf_op jit(solution)/shard_map/all_to_all | solution.py:35
  34.6 37.7 %collective-permute-start.4 = (bf16[2,128,1024]{2,1,0:T(8,128)(2,1)S(1)}, bf16[2,128,1024]{2,1,0:T(8,128)(2,1)S(1)}, u32[]{:S(2)}, u32[]{:S(2)}) collective-permute-start(bf16[2,128,1024]{2,1,0:T(8,128)(2,1)S(1)} %pad_maximum_fusion.refs_0_), channel_id=1, source_target_pairs={{0,1},{1,0},{2,3},{3,2},{4,5},{5,4},{6,7},{7,6},{8,9},{9,8},{10,11... | collective-permute-start | bytes 1572872 | tf_op jit(solution)/shard_map/ppermute | solution.py:39
  36.9 35.4 %collective-permute-start.5 = (bf16[2,128,1024]{2,1,0:T(8,128)(2,1)S(1)}, bf16[2,128,1024]{2,1,0:T(8,128)(2,1)S(1)}, u32[]{:S(2)}, u32[]{:S(2)}) collective-permute-start(bf16[2,128,1024]{2,1,0:T(8,128)(2,1)S(1)} %collective-permute-done.3.refs_1_), channel_id=1, source_target_pairs={{0,1},{1,0},{2,3},{3,2},{4,5},{5,4},{6,7},{7,6},{8,9},{9,8},{10,11... | collective-permute-start | bytes 1572872 | tf_op jit(solution)/shard_map/ppermute | solution.py:39
  42.3 25.1 %all-to-all-start.2 = ((f32[4,48,128]{2,1,0:T(8,128)}), f32[4,48,128]{2,1,0:T(8,128)S(1)}, u32[]{:S(2)}, u32[]{:S(2)}) async-start(f32[4,48,128]{2,1,0:T(8,128)} %shard_map.170), calls=%async_computation.2 | async-start | bytes 196608 | tf_op jit(solution)/shard_map/all_to_all | solution.py:35
  55.6 1.0 copy-start.2
  56.6 0.9 copy-start.3
  60.3 0.7 copy-start.4
  68.1 11.1 %all-to-all-start.3 = ((bf16[16,48,128]{2,1,0:T(8,128)(2,1)}), bf16[16,48,128]{2,1,0:T(8,128)(2,1)S(1)}, u32[]{:S(2)}, u32[]{:S(2)}) async-start(bf16[16,48,128]{2,1,0:T(8,128)(2,1)} %shard_map.172), calls=%async_computation.3 | async-start | bytes 393216 | tf_op jit(solution)/shard_map/all_to_all | solution.py:35
  72.3 6.9 %copy-start.1 = (f32[1024,64]{0,1:T(8,128)S(1)}, f32[1024,64]{0,1:T(8,128)}, u32[]{:S(2)}) copy-start(f32[1024,64]{0,1:T(8,128)} %param.17) | copy-start | bytes 786436
  72.3 17.2 %copy-start.7 = (f32[64,128]{1,0:T(8,128)S(1)}, f32[64,128]{1,0:T(8,128)}, u32[]{:S(2)}) copy-start(f32[64,128]{1,0:T(8,128)} %b_ref.3) | copy-start | bytes 98308
  80.1 15.2 %all-to-all-start.4 = ((bf16[8,64,128]{2,1,0:T(8,128)(2,1)}), bf16[8,64,128]{2,1,0:T(8,128)(2,1)S(1)}, u32[]{:S(2)}, u32[]{:S(2)}) async-start(bf16[8,64,128]{2,1,0:T(8,128)(2,1)} %shard_map.175), calls=%async_computation.4 | async-start | bytes 262144 | tf_op jit(solution)/shard_map/all_to_all | solution.py:35
  95.4 1.0 copy-start.5

commit v9 on v7

--- a/solution.py
+++ b/solution.py
@@ -117,7 +117,7 @@
 
 
 def sum_body(in_ref, out_ref):
-    total = total_of(in_ref)
+    total = total_of(in_ref).astype(BF)
     for i in range(out_ref.shape[0]):
         out_ref[i] = total
 
@@ -297,7 +297,7 @@
     mine, moments = lax.optimization_barrier((mine, (moment_a.T, second_a.T, moment_b, second_b)))
     theirs = swap(mine)
     rows_a, rows_b = rank * width // kv // plane, rank // plane
-    deep = rows_a + rows_b + -(rows_a + rows_b) % 16
+    deep = rows_a + rows_b + -(rows_a + rows_b) % 8
     piece = shape((deep, kv), F32)
     moments = call(shard_body, (piece, piece), *map(far, moments))
     theirs, moments = lax.optimization_barrier((theirs, moments))
@@ -312,12 +312,8 @@
         theirs,
     )
 
+    block, query = lax.optimization_barrier((block, queries))
     shard = trade(block, PLANE)
-    near = jnp.concatenate([send[None], second_chip], axis=0)
-    distant = reach(near, 1)
-    shard = call(sum_body, shape((lax.axis_size("zh"), deep, kv), F32), shard)
-    shard, query = lax.optimization_barrier((shard, queries))
-    shard = trade(shard, "zh")
 
     groups = rows * slots // HD
     heads = queries.shape[2] // HD
@@ -333,7 +329,13 @@
         moved=8 * 2**20,
     )
     shard, old, weights = lax.optimization_barrier((shard, old, weights))
-    step = call(adam_body, shape((plane, deep, kv), BF), shard, *moments)
+    near = jnp.concatenate([send[None], second_chip], axis=0)
+    distant = reach(near, 1)
+    shard = call(sum_body, shape((lax.axis_size("zh"), deep, kv), BF), shard)
+    shard = trade(shard, "zh")
+
+    step = adam_step(jnp.sum(shard.astype(F32), axis=0), *moments).astype(BF)
+    step = jnp.broadcast_to(step[None], (plane, deep, kv))
     distant_sent, near_sent, _ = lax.optimization_barrier((distant, near, step))
     distant_other, near_other = swap(distant_sent), swap(near_sent)
     step = trade(step, PLANE)

time: 92.4 us -> 91.8 us (level)
  waiting for transfers between devices: 17.5 us -> 16.5 us
    all_to_all x5, waiting for transfers between devices: 17.5 us -> 16.4 us  [trade(): return lax.all_to_all(parts, axes, 0, 0, tiled=True)]
    pallas_call x11 -> x10, Pallas kernels: 13.9 us -> 13.2 us  [call(): pl.pallas_call(body, out_shape=out, cost_estimate=pl.CostEstimate(flops=f...]
  transfers between devices with their start and end apart: 11 -> 11, of which waited for: 5 -> 4; matrix products, arithmetic and copies ran while one was open for 2% -> 2% of each run, Pallas kernels for 12% -> 11%
where the time goes in v9:
time: 91.8 us; the launch traced here: 91 us
  starting transfers between devices  58.2 us (63%)
  waiting for transfers between devices  16.5 us (18%)
  Pallas kernels  13.2 us (14%)
  local copies, waits for them, and re-layouts  2.05 us (2%)
  between operations  0.93 us (1%)
    all_to_all x5, starting transfers between devices, trade(): return lax.all_to_all(parts, axes, 0, 0, tiled=True)  32.5 us
    ppermute x4, starting transfers between devices, swap(): return lax.ppermute(value, 'core', [(0, 1), (1, 0)])  19.6 us
    all_to_all x5, waiting for transfers between devices, trade(): return lax.all_to_all(parts, axes, 0, 0, tiled=True)  16.4 us
    pallas_call x10, Pallas kernels, call(): pl.pallas_call(body, out_shape=out, cost_estimate=pl.CostEstimate(flops=f...  13.2 us
    ppermute x2, starting transfers between devices, reach(): lax.ppermute(value, 'zl', [(i, i ^ hop) for i in range(lax.axis_size('zl'...  6.14 us
  transfers between devices with their start and end apart: 11, of which 4 were waited for; matrix products, arithmetic and copies ran while one was open for 2% of the time, Pallas kernels for 11%

profile of v9, /device:TPU:1, one launch (start us, length us, event | category | flops | bytes accessed | tf_op | source)
XLA Modules:
  0.0 91.0 jit_solution(12530734895994271829)
XLA Ops:
  0.6 0.0 copy-start
  0.6 0.0 copy-start.6
  0.7 0.0 copy-start.9
  0.7 0.0 copy-start.10
  0.7 0.0 copy-start.2
  0.7 0.0 copy-start.3
  0.7 0.0 copy-start.8
  0.7 1.6 %shard_map.166 = (f32[128,128]{1,0:T(8,128)S(1)}, f32[128,128]{1,0:T(8,128)S(1)}) custom-call(bf16[256,1024]{1,0:T(8,128)(2,1)} %refs_0_.1, bf16[256,128]{1,0:T(8,128)(2,1)} %refs_1_.1, f32[64,1024]{1,0:T(8,128)} %bitcast.11, f32[64,128]{1,0:T(8,128)} %b_ref.3), custom_call_target="tpu_custom_call" | custom-call | tf_op jit(solution)/shard_map/pallas_call | solution.py:47
  2.3 8.8 %collective-permute-start = (f32[128,128]{1,0:T(8,128)S(1)}, f32[128,128]{1,0:T(8,128)S(1)}, u32[]{:S(2)}, u32[]{:S(2)}) collective-permute-start(f32[128,128]{1,0:T(8,128)S(1)} %get-tuple-element.30), channel_id=1, source_target_pairs={{0,1},{1,0},{2,3},{3,2},{4,5},{5,4},{6,7},{7,6},{8,9},{9,8},{10,11... | collective-permute-start | bytes 196616 | tf_op jit(solution)/shard_map/ppermute | solution.py:39
  11.1 1.0 %reshape.27.flat_ref = bf16[128,1024]{1,0:T(8,128)(2,1)S(1)} reshape(bf16[32,4,1024]{2,1,0:T(4,128)(2,1)} %param.24) | data formatting | bytes 524288 | tf_op jit(solution)/shard_map/reshape | solution.py:286
  12.1 0.0 collective-permute-done.theirs_ref
  12.1 0.7 shard_map.167
  12.8 3.3 %all-to-all-start = ((bf16[4,128,128]{2,1,0:T(8,128)(2,1)}), bf16[4,128,128]{2,1,0:T(8,128)(2,1)S(1)}, u32[]{:S(2)}, u32[]{:S(2)}) async-start(bf16[4,128,128]{2,1,0:T(8,128)(2,1)} %shard_map.167), calls=%async_computation | async-start | bytes 262144 | tf_op jit(solution)/shard_map/all_to_all | solution.py:35
  16.1 4.2 %collective-permute-start.2 = (bf16[1,128,1024]{2,1,0:T(8,128)(2,1)S(1)}, bf16[1,128,1024]{2,1,0:T(8,128)(2,1)S(1)}, u32[]{:S(2)}, u32[]{:S(2)}) collective-permute-start(bf16[1,128,1024]{2,1,0:T(8,128)(2,1)S(1)} %bitcast.9), channel_id=1, source_target_pairs={{0,4},{2,6},{4,0},{6,2},{1,5},{3,7},{5,1},{7,3},{8,12},{10,14},{12... | collective-permute-start | bytes 786440 | tf_op jit(solution)/shard_map/ppermute | solution.py:43
  20.4 0.6 all-to-all-done
  21.0 3.8 %collective-permute-start.1 = (bf16[128,128]{1,0:T(8,128)(2,1)S(1)}, bf16[128,128]{1,0:T(8,128)(2,1)S(1)}, u32[]{:S(2)}, u32[]{:S(2)}) collective-permute-start(bf16[128,128]{1,0:T(8,128)(2,1)S(1)} %reduce_sum.21.refs_2_), channel_id=1, source_target_pairs={{0,1},{1,0},{2,3},{3,2},{4,5},{5,4},{6,7},{7,6},{8,9},{9,8},{10,11... | collective-permute-start | bytes 98312 | tf_op jit(solution)/shard_map/ppermute | solution.py:39
  24.9 1.0 %shard_map.168 = (f32[40,128]{1,0:T(8,128)S(1)}, f32[40,128]{1,0:T(8,128)S(1)}) custom-call(f32[64,1024]{1,0:T(8,128)} %bitcast.17, f32[64,1024]{1,0:T(8,128)} %bitcast.18, f32[64,128]{1,0:T(8,128)} %moment_b_ref, f32[64,128]{1,0:T(8,128)} %second_b_ref), custom_call_target="tpu_custom_call" | custom-call | tf_op jit(solution)/shard_map/pallas_call | solution.py:47
  25.9 0.0 collective-permute-done.1.refs_3_
  25.9 0.0 copy-done
  25.9 0.0 copy-done.6
  25.9 0.0 copy-start.1
  25.9 1.0 %shard_map.169 = bf16[16,40,128]{2,1,0:T(8,128)(2,1)} custom-call(bf16[256,1024]{1,0:T(8,128)(2,1)S(1)} %copy-done, bf16[256,128]{1,0:T(8,128)(2,1)S(1)} %copy-done.6, bf16[128,128]{1,0:T(8,128)(2,1)S(1)} %reduce_sum.21.refs_2_, bf16[128,128]{1,0:T(8,128)(2,1)S(1)} %collective-permute-done.1.refs_3_), custom_call_target="tpu_custom_call" | custom-call | tf_op jit(solution)/shard_map/pallas_call | solution.py:47
  26.9 10.1 %all-to-all-start.1 = ((bf16[16,40,128]{2,1,0:T(8,128)(2,1)}), bf16[16,40,128]{2,1,0:T(8,128)(2,1)S(1)}, u32[]{:S(2)}, u32[]{:S(2)}) async-start(bf16[16,40,128]{2,1,0:T(8,128)(2,1)} %shard_map.169), calls=%async_computation.1 | async-start | bytes 327680 | tf_op jit(solution)/shard_map/all_to_all | solution.py:35
  37.0 0.0 copy-done.10
  37.1 0.1 broadcast_in_dim.17
  37.1 0.1 broadcast_in_dim.18
  37.2 0.1 broadcast_in_dim.19.refs_4_
  37.3 0.0 copy-done.9
  37.3 0.0 copy-start.7
  37.3 0.1 reshape.28.refs_0_
  37.4 0.0 copy-done.2
  37.4 0.0 copy-done.3
  37.4 0.0 copy-done.8
  37.4 2.8 %shard_map.170 = (f32[1024,128]{1,0:T(8,128)S(1)}, bf16[1024,128]{1,0:T(8,128)(2,1)S(1)}) custom-call(bf16[128,1024]{1,0:T(8,128)(2,1)S(1)} %reshape.28.refs_0_, bf16[1024,128]{1,0:T(8,128)(2,1)S(1)} %bitcast.13, bf16[1024,128]{1,0:T(8,128)(2,1)S(1)} %bitcast.14, bf16[128,128]{1,0:T(8,128)(2,1)S(1)} %bitcast.15, s32[8,128]{1,0:T(8,128)S(1)} %broadcast_in_dim.19.refs_4_), custom_call_target="tpu_custom_call" | custom-call | flops 100663296 | bytes 8388608 | tf_op jit(solution)/shard_map/pallas_call | solution.py:47
  40.2 0.0 copy-start.4
  40.2 3.7 %all-to-all-done.1.in_ref = bf16[16,40,128]{2,1,0:T(8,128)(2,1)S(1)} async-done(((bf16[16,40,128]{2,1,0:T(8,128)(2,1)}), bf16[16,40,128]{2,1,0:T(8,128)(2,1)S(1)}, u32[]{:S(2)}, u32[]{:S(2)}) %all-to-all-start.1) | async-done | bytes 163872 | tf_op jit(solution)/shard_map/all_to_all | solution.py:35
  43.9 0.6 shard_map.171
  44.5 8.2 %all-to-all-start.2 = ((bf16[4,40,128]{2,1,0:T(8,128)(2,1)}), bf16[4,40,128]{2,1,0:T(8,128)(2,1)S(1)}, u32[]{:S(2)}, u32[]{:S(2)}) async-start(bf16[4,40,128]{2,1,0:T(8,128)(2,1)} %shard_map.171), calls=%async_computation.2 | async-start | bytes 81920 | tf_op jit(solution)/shard_map/all_to_all | solution.py:35
  52.7 0.0 copy-done.4
  52.7 0.0 collective-permute-done.2
  52.7 0.1 pad_maximum_fusion.refs_0_
  52.8 1.9 %collective-permute-start.3 = (bf16[2,128,1024]{2,1,0:T(8,128)(2,1)S(1)}, bf16[2,128,1024]{2,1,0:T(8,128)(2,1)S(1)}, u32[]{:S(2)}, u32[]{:S(2)}) collective-permute-start(bf16[2,128,1024]{2,1,0:T(8,128)(2,1)S(1)} %pad_maximum_fusion.refs_0_), channel_id=1, source_target_pairs={{0,2},{2,0},{4,6},{6,4},{1,3},{3,1},{5,7},{7,5},{8,10},{10,8},{12,... | collective-permute-start | bytes 1572872 | tf_op jit(solution)/shard_map/ppermute | solution.py:43
  54.7 9.9 %all-to-all-done.2 = bf16[4,40,128]{2,1,0:T(8,128)(2,1)S(1)} async-done(((bf16[4,40,128]{2,1,0:T(8,128)(2,1)}), bf16[4,40,128]{2,1,0:T(8,128)(2,1)S(1)}, u32[]{:S(2)}, u32[]{:S(2)}) %all-to-all-start.2) | async-done | bytes 40992 | tf_op jit(solution)/shard_map/all_to_all | solution.py:35
  64.6 0.7 broadcast_in_dim.20
  65.3 3.5 %all-to-all-start.3 = ((bf16[16,40,128]{2,1,0:T(8,128)(2,1)}), bf16[16,40,128]{2,1,0:T(8,128)(2,1)S(1)}, u32[]{:S(2)}, u32[]{:S(2)}) async-start(bf16[16,40,128]{2,1,0:T(8,128)(2,1)} %broadcast_in_dim.20), calls=%async_computation.3 | async-start | bytes 327680 | tf_op jit(solution)/shard_map/all_to_all | solution.py:35
  68.9 0.0 collective-permute-done.3.refs_1_
  68.9 5.0 %collective-permute-start.4 = (bf16[2,128,1024]{2,1,0:T(8,128)(2,1)S(1)}, bf16[2,128,1024]{2,1,0:T(8,128)(2,1)S(1)}, u32[]{:S(2)}, u32[]{:S(2)}) collective-permute-start(bf16[2,128,1024]{2,1,0:T(8,128)(2,1)S(1)} %pad_maximum_fusion.refs_0_), channel_id=1, source_target_pairs={{0,1},{1,0},{2,3},{3,2},{4,5},{5,4},{6,7},{7,6},{8,9},{9,8},{10,11... | collective-permute-start | bytes 1572872 | tf_op jit(solution)/shard_map/ppermute | solution.py:39
  73.9 1.9 %collective-permute-start.5 = (bf16[2,128,1024]{2,1,0:T(8,128)(2,1)S(1)}, bf16[2,128,1024]{2,1,0:T(8,128)(2,1)S(1)}, u32[]{:S(2)}, u32[]{:S(2)}) collective-permute-start(bf16[2,128,1024]{2,1,0:T(8,128)(2,1)S(1)} %collective-permute-done.3.refs_1_), channel_id=1, source_target_pairs={{0,1},{1,0},{2,3},{3,2},{4,5},{5,4},{6,7},{7,6},{8,9},{9,8},{10,11... | collective-permute-start | bytes 1572872 | tf_op jit(solution)/shard_map/ppermute | solution.py:39
  75.8 0.0 all-to-all-done.3.step_ref
  75.8 0.0 copy-done.1
  75.8 0.9 shard_map.173
  76.7 7.3 %all-to-all-start.4 = ((bf16[8,64,128]{2,1,0:T(8,128)(2,1)}), bf16[8,64,128]{2,1,0:T(8,128)(2,1)S(1)}, u32[]{:S(2)}, u32[]{:S(2)}) async-start(bf16[8,64,128]{2,1,0:T(8,128)(2,1)} %shard_map.173), calls=%async_computation.4 | async-start | bytes 262144 | tf_op jit(solution)/shard_map/all_to_all | solution.py:35
  84.0 0.0 copy-done.7
  84.0 0.7 shard_map.172
  84.8 0.0 collective-permute-done.4.refs_2_
  84.8 0.0 collective-permute-done.5.refs_3_
  84.8 0.0 copy-start.5
  84.8 2.9 %shard_map.174.refs_2_ = f32[128,128]{1,0:T(8,128)S(1)} custom-call(bf16[4,2,1024,128]{3,2,1,0:T(8,128)(2,1)} %bitcast.16, bf16[2,128,1024]{2,1,0:T(8,128)(2,1)S(1)} %pad_maximum_fusion.refs_0_, bf16[2,128,1024]{2,1,0:T(8,128)(2,1)S(1)} %collective-permute-done.3.refs_1_, bf16[2,128,1024]{2,1,0:T(8,128)(2,1)S(1)} %collective-permute-done.4.refs_2_, ...), custom_call_target="tpu_custom_call" | custom-call | flops 268435456 | bytes 4194304 | tf_op jit(solution)/shard_map/pallas_call | solution.py:47
  87.6 2.2 %all-to-all-done.4.refs_0_ = bf16[8,64,128]{2,1,0:T(8,128)(2,1)S(1)} async-done(((bf16[8,64,128]{2,1,0:T(8,128)(2,1)}), bf16[8,64,128]{2,1,0:T(8,128)(2,1)S(1)}, u32[]{:S(2)}, u32[]{:S(2)}) %all-to-all-start.4) | async-done | bytes 131104 | tf_op jit(solution)/shard_map/all_to_all | solution.py:35
  89.9 0.0 copy-done.5
  89.9 1.1 %shard_map.175 = bf16[32,4,1024]{2,1,0:T(4,128)(2,1)} custom-call(bf16[8,64,128]{2,1,0:T(8,128)(2,1)S(1)} %all-to-all-done.4.refs_0_, bf16[64,128]{1,0:T(8,128)(2,1)S(1)} %get-tuple-element.49.refs_1_, f32[128,128]{1,0:T(8,128)S(1)} %shard_map.174.refs_2_, f32[1024,128]{1,0:T(8,128)S(1)} %get-tuple-element.53.refs_3_, bf16[1024,128]{1,0:T(8,128)(2,1)S(1)} %copy-done.5), custom_call_target="tpu_custom_call" | custom-call | tf_op jit(solution)/shard_map/pallas_call | solution.py:47
  (3 shorter events, 0.1 us)
Async XLA Ops:
  0.6 25.3 %copy-start = (bf16[256,1024]{1,0:T(8,128)(2,1)S(1)}, bf16[256,1024]{1,0:T(8,128)(2,1)}, u32[]{:S(2)}) copy-start(bf16[256,1024]{1,0:T(8,128)(2,1)} %refs_0_.1) | copy-start | bytes 1572868
  0.6 25.3 %copy-start.6 = (bf16[256,128]{1,0:T(8,128)(2,1)S(1)}, bf16[256,128]{1,0:T(8,128)(2,1)}, u32[]{:S(2)}) copy-start(bf16[256,128]{1,0:T(8,128)(2,1)} %refs_1_.1) | copy-start | bytes 196612
  0.7 36.6 %copy-start.9 = (bf16[32,4,1024]{2,1,0:T(4,128)(2,1)S(1)}, bf16[32,4,1024]{2,1,0:T(4,128)(2,1)}, u32[]{:S(2)}) copy-start(bf16[32,4,1024]{2,1,0:T(4,128)(2,1)} %param.26) | copy-start | bytes 786436
  0.7 36.4 %copy-start.10 = (s32[32]{0:T(128)S(1)}, s32[32]{0:T(128)}, u32[]{:S(2)}) copy-start(s32[32]{0:T(128)} %param.29) | copy-start | bytes 388
  0.7 36.7 %copy-start.2 = (bf16[32,32,128]{2,1,0:T(8,128)(2,1)S(1)}, bf16[32,32,128]{2,1,0:T(8,128)(2,1)}, u32[]{:S(2)}) copy-start(bf16[32,32,128]{2,1,0:T(8,128)(2,1)} %param.27) | copy-start | bytes 786436
  0.7 36.7 %copy-start.3 = (bf16[32,32,128]{2,1,0:T(8,128)(2,1)S(1)}, bf16[32,32,128]{2,1,0:T(8,128)(2,1)}, u32[]{:S(2)}) copy-start(bf16[32,32,128]{2,1,0:T(8,128)(2,1)} %param.28) | copy-start | bytes 786436
  0.7 36.7 %copy-start.8 = (bf16[32,4,128]{2,1,0:T(4,128)(2,1)S(1)}, bf16[32,4,128]{2,1,0:T(4,128)(2,1)}, u32[]{:S(2)}) copy-start(bf16[32,4,128]{2,1,0:T(4,128)(2,1)} %param.25) | copy-start | bytes 98308
  2.3 9.8 %collective-permute-start = (f32[128,128]{1,0:T(8,128)S(1)}, f32[128,128]{1,0:T(8,128)S(1)}, u32[]{:S(2)}, u32[]{:S(2)}) collective-permute-start(f32[128,128]{1,0:T(8,128)S(1)} %get-tuple-element.30), channel_id=1, source_target_pairs={{0,1},{1,0},{2,3},{3,2},{4,5},{5,4},{6,7},{7,6},{8,9},{9,8},{10,11... | collective-permute-start | bytes 196616 | tf_op jit(solution)/shard_map/ppermute | solution.py:39
  12.8 8.2 %all-to-all-start = ((bf16[4,128,128]{2,1,0:T(8,128)(2,1)}), bf16[4,128,128]{2,1,0:T(8,128)(2,1)S(1)}, u32[]{:S(2)}, u32[]{:S(2)}) async-start(bf16[4,128,128]{2,1,0:T(8,128)(2,1)} %shard_map.167), calls=%async_computation | async-start | bytes 262144 | tf_op jit(solution)/shard_map/all_to_all | solution.py:35
  16.1 36.6 %collective-permute-start.2 = (bf16[1,128,1024]{2,1,0:T(8,128)(2,1)S(1)}, bf16[1,128,1024]{2,1,0:T(8,128)(2,1)S(1)}, u32[]{:S(2)}, u32[]{:S(2)}) collective-permute-start(bf16[1,128,1024]{2,1,0:T(8,128)(2,1)S(1)} %bitcast.9), channel_id=1, source_target_pairs={{0,4},{2,6},{4,0},{6,2},{1,5},{3,7},{5,1},{7,3},{8,12},{10,14},{12... | collective-permute-start | bytes 786440 | tf_op jit(solution)/shard_map/ppermute | solution.py:43
  21.0 4.9 %collective-permute-start.1 = (bf16[128,128]{1,0:T(8,128)(2,1)S(1)}, bf16[128,128]{1,0:T(8,128)(2,1)S(1)}, u32[]{:S(2)}, u32[]{:S(2)}) collective-permute-start(bf16[128,128]{1,0:T(8,128)(2,1)S(1)} %reduce_sum.21.refs_2_), channel_id=1, source_target_pairs={{0,1},{1,0},{2,3},{3,2},{4,5},{5,4},{6,7},{7,6},{8,9},{9,8},{10,11... | collective-permute-start | bytes 98312 | tf_op jit(solution)/shard_map/ppermute | solution.py:39
  25.9 49.9 %copy-start.1 = (f32[1024,64]{0,1:T(8,128)S(1)}, f32[1024,64]{0,1:T(8,128)}, u32[]{:S(2)}) copy-start(f32[1024,64]{0,1:T(8,128)} %param.17) | copy-start | bytes 786436
  26.9 17.0 %all-to-all-start.1 = ((bf16[16,40,128]{2,1,0:T(8,128)(2,1)}), bf16[16,40,128]{2,1,0:T(8,128)(2,1)S(1)}, u32[]{:S(2)}, u32[]{:S(2)}) async-start(bf16[16,40,128]{2,1,0:T(8,128)(2,1)} %shard_map.169), calls=%async_computation.1 | async-start | bytes 327680 | tf_op jit(solution)/shard_map/all_to_all | solution.py:35
  37.3 46.8 %copy-start.7 = (f32[64,128]{1,0:T(8,128)S(1)}, f32[64,128]{1,0:T(8,128)}, u32[]{:S(2)}) copy-start(f32[64,128]{1,0:T(8,128)} %b_ref.3) | copy-start | bytes 98308
  40.2 12.6 %copy-start.4 = (bf16[1024,128]{1,0:T(8,128)(2,1)}, bf16[1024,128]{1,0:T(8,128)(2,1)S(1)}, u32[]{:S(2)}) copy-start(bf16[1024,128]{1,0:T(8,128)(2,1)S(1)} %get-tuple-element.54.refs_4_) | copy-start | bytes 786436
  44.5 20.0 %all-to-all-start.2 = ((bf16[4,40,128]{2,1,0:T(8,128)(2,1)}), bf16[4,40,128]{2,1,0:T(8,128)(2,1)S(1)}, u32[]{:S(2)}, u32[]{:S(2)}) async-start(bf16[4,40,128]{2,1,0:T(8,128)(2,1)} %shard_map.171), calls=%async_computation.2 | async-start | bytes 81920 | tf_op jit(solution)/shard_map/all_to_all | solution.py:35
  52.8 16.1 %collective-permute-start.3 = (bf16[2,128,1024]{2,1,0:T(8,128)(2,1)S(1)}, bf16[2,128,1024]{2,1,0:T(8,128)(2,1)S(1)}, u32[]{:S(2)}, u32[]{:S(2)}) collective-permute-start(bf16[2,128,1024]{2,1,0:T(8,128)(2,1)S(1)} %pad_maximum_fusion.refs_0_), channel_id=1, source_target_pairs={{0,2},{2,0},{4,6},{6,4},{1,3},{3,1},{5,7},{7,5},{8,10},{10,8},{12,... | collective-permute-start | bytes 1572872 | tf_op jit(solution)/shard_map/ppermute | solution.py:43
  65.3 10.5 %all-to-all-start.3 = ((bf16[16,40,128]{2,1,0:T(8,128)(2,1)}), bf16[16,40,128]{2,1,0:T(8,128)(2,1)S(1)}, u32[]{:S(2)}, u32[]{:S(2)}) async-start(bf16[16,40,128]{2,1,0:T(8,128)(2,1)} %broadcast_in_dim.20), calls=%async_computation.3 | async-start | bytes 327680 | tf_op jit(solution)/shard_map/all_to_all | solution.py:35
  68.9 15.9 %collective-permute-start.4 = (bf16[2,128,1024]{2,1,0:T(8,128)(2,1)S(1)}, bf16[2,128,1024]{2,1,0:T(8,128)(2,1)S(1)}, u32[]{:S(2)}, u32[]{:S(2)}) collective-permute-start(bf16[2,128,1024]{2,1,0:T(8,128)(2,1)S(1)} %pad_maximum_fusion.refs_0_), channel_id=1, source_target_pairs={{0,1},{1,0},{2,3},{3,2},{4,5},{5,4},{6,7},{7,6},{8,9},{9,8},{10,11... | collective-permute-start | bytes 1572872 | tf_op jit(solution)/shard_map/ppermute | solution.py:39
  73.9 10.9 %collective-permute-start.5 = (bf16[2,128,1024]{2,1,0:T(8,128)(2,1)S(1)}, bf16[2,128,1024]{2,1,0:T(8,128)(2,1)S(1)}, u32[]{:S(2)}, u32[]{:S(2)}) collective-permute-start(bf16[2,128,1024]{2,1,0:T(8,128)(2,1)S(1)} %collective-permute-done.3.refs_1_), channel_id=1, source_target_pairs={{0,1},{1,0},{2,3},{3,2},{4,5},{5,4},{6,7},{7,6},{8,9},{9,8},{10,11... | collective-permute-start | bytes 1572872 | tf_op jit(solution)/shard_map/ppermute | solution.py:39
  76.7 13.2 %all-to-all-start.4 = ((bf16[8,64,128]{2,1,0:T(8,128)(2,1)}), bf16[8,64,128]{2,1,0:T(8,128)(2,1)S(1)}, u32[]{:S(2)}, u32[]{:S(2)}) async-start(bf16[8,64,128]{2,1,0:T(8,128)(2,1)} %shard_map.173), calls=%async_computation.4 | async-start | bytes 262144 | tf_op jit(solution)/shard_map/all_to_all | solution.py:35
  84.8 5.1 %copy-start.5 = (bf16[1024,128]{1,0:T(8,128)(2,1)S(1)}, bf16[1024,128]{1,0:T(8,128)(2,1)}, u32[]{:S(2)}) copy-start(bf16[1024,128]{1,0:T(8,128)(2,1)} %copy-done.4) | copy-start | bytes 786436

commit v10 on v9

--- a/solution.py
+++ b/solution.py
@@ -331,13 +331,14 @@
     shard, old, weights = lax.optimization_barrier((shard, old, weights))
     near = jnp.concatenate([send[None], second_chip], axis=0)
     distant = reach(near, 1)
+    near_other = swap(near)
     shard = call(sum_body, shape((lax.axis_size("zh"), deep, kv), BF), shard)
     shard = trade(shard, "zh")
 
     step = adam_step(jnp.sum(shard.astype(F32), axis=0), *moments).astype(BF)
     step = jnp.broadcast_to(step[None], (plane, deep, kv))
-    distant_sent, near_sent, _ = lax.optimization_barrier((distant, near, step))
-    distant_other, near_other = swap(distant_sent), swap(near_sent)
+    distant_sent, _ = lax.optimization_barrier((distant, step))
+    distant_other = swap(distant_sent)
     step = trade(step, PLANE)
 
     inner = call(inner_body, shape((tensor, rank, count), BF), step, a_turned, flat)

time: 91.8 us -> 91.8 us (level)
  no operation moved by 1% of the time
where the time goes in v10:
time: 91.8 us; the launch traced here: 91 us
  starting transfers between devices  58.2 us (63%)
  waiting for transfers between devices  16.5 us (18%)
  Pallas kernels  13.2 us (14%)
  local copies, waits for them, and re-layouts  2.05 us (2%)
  between operations  0.93 us (1%)
    all_to_all x5, starting transfers between devices, trade(): return lax.all_to_all(parts, axes, 0, 0, tiled=True)  32.5 us
    ppermute x4, starting transfers between devices, swap(): return lax.ppermute(value, 'core', [(0, 1), (1, 0)])  19.6 us
    all_to_all x5, waiting for transfers between devices, trade(): return lax.all_to_all(parts, axes, 0, 0, tiled=True)  16.4 us
    pallas_call x10, Pallas kernels, call(): pl.pallas_call(body, out_shape=out, cost_estimate=pl.CostEstimate(flops=f...  13.2 us
    ppermute x2, starting transfers between devices, reach(): lax.ppermute(value, 'zl', [(i, i ^ hop) for i in range(lax.axis_size('zl'...  6.14 us
  transfers between devices with their start and end apart: 11, of which 4 were waited for; matrix products, arithmetic and copies ran while one was open for 2% of the time, Pallas kernels for 11%

profile of v10, /device:TPU:1, one launch (start us, length us, event | category | flops | bytes accessed | tf_op | source)
XLA Modules:
  0.0 91.0 jit_solution(7768631284949218306)
XLA Ops:
  0.6 0.0 copy-start
  0.6 0.0 copy-start.6
  0.7 0.0 copy-start.9
  0.7 0.0 copy-start.10
  0.7 0.0 copy-start.2
  0.7 0.0 copy-start.3
  0.7 0.0 copy-start.8
  0.7 1.6 %shard_map.166 = (f32[128,128]{1,0:T(8,128)S(1)}, f32[128,128]{1,0:T(8,128)S(1)}) custom-call(bf16[256,1024]{1,0:T(8,128)(2,1)} %refs_0_.1, bf16[256,128]{1,0:T(8,128)(2,1)} %refs_1_.1, f32[64,1024]{1,0:T(8,128)} %bitcast.11, f32[64,128]{1,0:T(8,128)} %b_ref.3), custom_call_target="tpu_custom_call" | custom-call | tf_op jit(solution)/shard_map/pallas_call | solution.py:47
  2.3 8.8 %collective-permute-start = (f32[128,128]{1,0:T(8,128)S(1)}, f32[128,128]{1,0:T(8,128)S(1)}, u32[]{:S(2)}, u32[]{:S(2)}) collective-permute-start(f32[128,128]{1,0:T(8,128)S(1)} %get-tuple-element.29), channel_id=1, source_target_pairs={{0,1},{1,0},{2,3},{3,2},{4,5},{5,4},{6,7},{7,6},{8,9},{9,8},{10,11... | collective-permute-start | bytes 196616 | tf_op jit(solution)/shard_map/ppermute | solution.py:39
  11.1 1.0 %reshape.27.flat_ref = bf16[128,1024]{1,0:T(8,128)(2,1)S(1)} reshape(bf16[32,4,1024]{2,1,0:T(4,128)(2,1)} %param.24) | data formatting | bytes 524288 | tf_op jit(solution)/shard_map/reshape | solution.py:286
  12.1 0.0 collective-permute-done.theirs_ref
  12.1 0.7 shard_map.167
  12.8 3.3 %all-to-all-start = ((bf16[4,128,128]{2,1,0:T(8,128)(2,1)}), bf16[4,128,128]{2,1,0:T(8,128)(2,1)S(1)}, u32[]{:S(2)}, u32[]{:S(2)}) async-start(bf16[4,128,128]{2,1,0:T(8,128)(2,1)} %shard_map.167), calls=%async_computation | async-start | bytes 262144 | tf_op jit(solution)/shard_map/all_to_all | solution.py:35
  16.1 4.2 %collective-permute-start.2 = (bf16[1,128,1024]{2,1,0:T(8,128)(2,1)S(1)}, bf16[1,128,1024]{2,1,0:T(8,128)(2,1)S(1)}, u32[]{:S(2)}, u32[]{:S(2)}) collective-permute-start(bf16[1,128,1024]{2,1,0:T(8,128)(2,1)S(1)} %bitcast.9), channel_id=1, source_target_pairs={{0,4},{2,6},{4,0},{6,2},{1,5},{3,7},{5,1},{7,3},{8,12},{10,14},{12... | collective-permute-start | bytes 786440 | tf_op jit(solution)/shard_map/ppermute | solution.py:43
  20.4 0.6 all-to-all-done
  21.0 3.8 %collective-permute-start.1 = (bf16[128,128]{1,0:T(8,128)(2,1)S(1)}, bf16[128,128]{1,0:T(8,128)(2,1)S(1)}, u32[]{:S(2)}, u32[]{:S(2)}) collective-permute-start(bf16[128,128]{1,0:T(8,128)(2,1)S(1)} %reduce_sum.21.refs_2_), channel_id=1, source_target_pairs={{0,1},{1,0},{2,3},{3,2},{4,5},{5,4},{6,7},{7,6},{8,9},{9,8},{10,11... | collective-permute-start | bytes 98312 | tf_op jit(solution)/shard_map/ppermute | solution.py:39
  24.9 1.0 %shard_map.168 = (f32[40,128]{1,0:T(8,128)S(1)}, f32[40,128]{1,0:T(8,128)S(1)}) custom-call(f32[64,1024]{1,0:T(8,128)} %bitcast.17, f32[64,1024]{1,0:T(8,128)} %bitcast.18, f32[64,128]{1,0:T(8,128)} %moment_b_ref, f32[64,128]{1,0:T(8,128)} %second_b_ref), custom_call_target="tpu_custom_call" | custom-call | tf_op jit(solution)/shard_map/pallas_call | solution.py:47
  25.9 0.0 collective-permute-done.1.refs_3_
  25.9 0.0 copy-done
  25.9 0.0 copy-done.6
  25.9 0.0 copy-start.1
  25.9 1.0 %shard_map.169 = bf16[16,40,128]{2,1,0:T(8,128)(2,1)} custom-call(bf16[256,1024]{1,0:T(8,128)(2,1)S(1)} %copy-done, bf16[256,128]{1,0:T(8,128)(2,1)S(1)} %copy-done.6, bf16[128,128]{1,0:T(8,128)(2,1)S(1)} %reduce_sum.21.refs_2_, bf16[128,128]{1,0:T(8,128)(2,1)S(1)} %collective-permute-done.1.refs_3_), custom_call_target="tpu_custom_call" | custom-call | tf_op jit(solution)/shard_map/pallas_call | solution.py:47
  26.9 10.1 %all-to-all-start.1 = ((bf16[16,40,128]{2,1,0:T(8,128)(2,1)}), bf16[16,40,128]{2,1,0:T(8,128)(2,1)S(1)}, u32[]{:S(2)}, u32[]{:S(2)}) async-start(bf16[16,40,128]{2,1,0:T(8,128)(2,1)} %shard_map.169), calls=%async_computation.1 | async-start | bytes 327680 | tf_op jit(solution)/shard_map/all_to_all | solution.py:35
  37.0 0.0 copy-done.10
  37.1 0.1 broadcast_in_dim.17
  37.1 0.1 broadcast_in_dim.18
  37.2 0.1 broadcast_in_dim.19.refs_4_
  37.3 0.0 copy-done.9
  37.3 0.0 copy-start.7
  37.3 0.1 reshape.28.refs_0_
  37.4 0.0 copy-done.2
  37.4 0.0 copy-done.3
  37.4 0.0 copy-done.8
  37.4 2.8 %shard_map.170 = (f32[1024,128]{1,0:T(8,128)S(1)}, bf16[1024,128]{1,0:T(8,128)(2,1)S(1)}) custom-call(bf16[128,1024]{1,0:T(8,128)(2,1)S(1)} %reshape.28.refs_0_, bf16[1024,128]{1,0:T(8,128)(2,1)S(1)} %bitcast.13, bf16[1024,128]{1,0:T(8,128)(2,1)S(1)} %bitcast.14, bf16[128,128]{1,0:T(8,128)(2,1)S(1)} %bitcast.15, s32[8,128]{1,0:T(8,128)S(1)} %broadcast_in_dim.19.refs_4_), custom_call_target="tpu_custom_call" | custom-call | flops 100663296 | bytes 8388608 | tf_op jit(solution)/shard_map/pallas_call | solution.py:47
  40.2 0.0 copy-start.4
  40.2 3.7 %all-to-all-done.1.in_ref = bf16[16,40,128]{2,1,0:T(8,128)(2,1)S(1)} async-done(((bf16[16,40,128]{2,1,0:T(8,128)(2,1)}), bf16[16,40,128]{2,1,0:T(8,128)(2,1)S(1)}, u32[]{:S(2)}, u32[]{:S(2)}) %all-to-all-start.1) | async-done | bytes 163872 | tf_op jit(solution)/shard_map/all_to_all | solution.py:35
  43.9 0.6 shard_map.171
  44.5 8.2 %all-to-all-start.2 = ((bf16[4,40,128]{2,1,0:T(8,128)(2,1)}), bf16[4,40,128]{2,1,0:T(8,128)(2,1)S(1)}, u32[]{:S(2)}, u32[]{:S(2)}) async-start(bf16[4,40,128]{2,1,0:T(8,128)(2,1)} %shard_map.171), calls=%async_computation.2 | async-start | bytes 81920 | tf_op jit(solution)/shard_map/all_to_all | solution.py:35
  52.7 0.0 copy-done.4
  52.7 0.0 collective-permute-done.2
  52.7 0.1 pad_maximum_fusion.refs_0_
  52.8 1.9 %collective-permute-start.3 = (bf16[2,128,1024]{2,1,0:T(8,128)(2,1)S(1)}, bf16[2,128,1024]{2,1,0:T(8,128)(2,1)S(1)}, u32[]{:S(2)}, u32[]{:S(2)}) collective-permute-start(bf16[2,128,1024]{2,1,0:T(8,128)(2,1)S(1)} %pad_maximum_fusion.refs_0_), channel_id=1, source_target_pairs={{0,2},{2,0},{4,6},{6,4},{1,3},{3,1},{5,7},{7,5},{8,10},{10,8},{12,... | collective-permute-start | bytes 1572872 | tf_op jit(solution)/shard_map/ppermute | solution.py:43
  54.7 9.9 %all-to-all-done.2 = bf16[4,40,128]{2,1,0:T(8,128)(2,1)S(1)} async-done(((bf16[4,40,128]{2,1,0:T(8,128)(2,1)}), bf16[4,40,128]{2,1,0:T(8,128)(2,1)S(1)}, u32[]{:S(2)}, u32[]{:S(2)}) %all-to-all-start.2) | async-done | bytes 40992 | tf_op jit(solution)/shard_map/all_to_all | solution.py:35
  64.6 0.7 broadcast_in_dim.20
  65.3 3.5 %all-to-all-start.3 = ((bf16[16,40,128]{2,1,0:T(8,128)(2,1)}), bf16[16,40,128]{2,1,0:T(8,128)(2,1)S(1)}, u32[]{:S(2)}, u32[]{:S(2)}) async-start(bf16[16,40,128]{2,1,0:T(8,128)(2,1)} %broadcast_in_dim.20), calls=%async_computation.3 | async-start | bytes 327680 | tf_op jit(solution)/shard_map/all_to_all | solution.py:35
  68.9 5.0 %collective-permute-start.4 = (bf16[2,128,1024]{2,1,0:T(8,128)(2,1)S(1)}, bf16[2,128,1024]{2,1,0:T(8,128)(2,1)S(1)}, u32[]{:S(2)}, u32[]{:S(2)}) collective-permute-start(bf16[2,128,1024]{2,1,0:T(8,128)(2,1)S(1)} %pad_maximum_fusion.refs_0_), channel_id=1, source_target_pairs={{0,1},{1,0},{2,3},{3,2},{4,5},{5,4},{6,7},{7,6},{8,9},{9,8},{10,11... | collective-permute-start | bytes 1572872 | tf_op jit(solution)/shard_map/ppermute | solution.py:39
  73.9 0.0 collective-permute-done.3.refs_1_
  73.9 1.9 %collective-permute-start.5 = (bf16[2,128,1024]{2,1,0:T(8,128)(2,1)S(1)}, bf16[2,128,1024]{2,1,0:T(8,128)(2,1)S(1)}, u32[]{:S(2)}, u32[]{:S(2)}) collective-permute-start(bf16[2,128,1024]{2,1,0:T(8,128)(2,1)S(1)} %collective-permute-done.3.refs_1_), channel_id=1, source_target_pairs={{0,1},{1,0},{2,3},{3,2},{4,5},{5,4},{6,7},{7,6},{8,9},{9,8},{10,11... | collective-permute-start | bytes 1572872 | tf_op jit(solution)/shard_map/ppermute | solution.py:39
  75.8 0.0 all-to-all-done.3.step_ref
  75.8 0.0 copy-done.1
  75.8 0.9 shard_map.173
  76.7 7.3 %all-to-all-start.4 = ((bf16[8,64,128]{2,1,0:T(8,128)(2,1)}), bf16[8,64,128]{2,1,0:T(8,128)(2,1)S(1)}, u32[]{:S(2)}, u32[]{:S(2)}) async-start(bf16[8,64,128]{2,1,0:T(8,128)(2,1)} %shard_map.173), calls=%async_computation.4 | async-start | bytes 262144 | tf_op jit(solution)/shard_map/all_to_all | solution.py:35
  84.0 0.0 copy-done.7
  84.0 0.7 shard_map.172
  84.8 0.0 collective-permute-done.4.refs_2_
  84.8 0.0 collective-permute-done.5.refs_3_
  84.8 0.0 copy-start.5
  84.8 2.9 %shard_map.174.refs_2_ = f32[128,128]{1,0:T(8,128)S(1)} custom-call(bf16[4,2,1024,128]{3,2,1,0:T(8,128)(2,1)} %bitcast.16, bf16[2,128,1024]{2,1,0:T(8,128)(2,1)S(1)} %pad_maximum_fusion.refs_0_, bf16[2,128,1024]{2,1,0:T(8,128)(2,1)S(1)} %collective-permute-done.3.refs_1_, bf16[2,128,1024]{2,1,0:T(8,128)(2,1)S(1)} %collective-permute-done.4.refs_2_, ...), custom_call_target="tpu_custom_call" | custom-call | flops 268435456 | bytes 4194304 | tf_op jit(solution)/shard_map/pallas_call | solution.py:47
  87.6 2.2 %all-to-all-done.4.refs_0_ = bf16[8,64,128]{2,1,0:T(8,128)(2,1)S(1)} async-done(((bf16[8,64,128]{2,1,0:T(8,128)(2,1)}), bf16[8,64,128]{2,1,0:T(8,128)(2,1)S(1)}, u32[]{:S(2)}, u32[]{:S(2)}) %all-to-all-start.4) | async-done | bytes 131104 | tf_op jit(solution)/shard_map/all_to_all | solution.py:35
  89.9 0.0 copy-done.5
  89.9 1.1 %shard_map.175 = bf16[32,4,1024]{2,1,0:T(4,128)(2,1)} custom-call(bf16[8,64,128]{2,1,0:T(8,128)(2,1)S(1)} %all-to-all-done.4.refs_0_, bf16[64,128]{1,0:T(8,128)(2,1)S(1)} %get-tuple-element.48.refs_1_, f32[128,128]{1,0:T(8,128)S(1)} %shard_map.174.refs_2_, f32[1024,128]{1,0:T(8,128)S(1)} %get-tuple-element.51.refs_3_, bf16[1024,128]{1,0:T(8,128)(2,1)S(1)} %copy-done.5), custom_call_target="tpu_custom_call" | custom-call | tf_op jit(solution)/shard_map/pallas_call | solution.py:47
  (3 shorter events, 0.1 us)
Async XLA Ops:
  0.6 25.3 %copy-start = (bf16[256,1024]{1,0:T(8,128)(2,1)S(1)}, bf16[256,1024]{1,0:T(8,128)(2,1)}, u32[]{:S(2)}) copy-start(bf16[256,1024]{1,0:T(8,128)(2,1)} %refs_0_.1) | copy-start | bytes 1572868
  0.6 25.3 %copy-start.6 = (bf16[256,128]{1,0:T(8,128)(2,1)S(1)}, bf16[256,128]{1,0:T(8,128)(2,1)}, u32[]{:S(2)}) copy-start(bf16[256,128]{1,0:T(8,128)(2,1)} %refs_1_.1) | copy-start | bytes 196612
  0.7 36.6 %copy-start.9 = (bf16[32,4,1024]{2,1,0:T(4,128)(2,1)S(1)}, bf16[32,4,1024]{2,1,0:T(4,128)(2,1)}, u32[]{:S(2)}) copy-start(bf16[32,4,1024]{2,1,0:T(4,128)(2,1)} %param.26) | copy-start | bytes 786436
  0.7 36.4 %copy-start.10 = (s32[32]{0:T(128)S(1)}, s32[32]{0:T(128)}, u32[]{:S(2)}) copy-start(s32[32]{0:T(128)} %param.29) | copy-start | bytes 388
  0.7 36.7 %copy-start.2 = (bf16[32,32,128]{2,1,0:T(8,128)(2,1)S(1)}, bf16[32,32,128]{2,1,0:T(8,128)(2,1)}, u32[]{:S(2)}) copy-start(bf16[32,32,128]{2,1,0:T(8,128)(2,1)} %param.27) | copy-start | bytes 786436
  0.7 36.7 %copy-start.3 = (bf16[32,32,128]{2,1,0:T(8,128)(2,1)S(1)}, bf16[32,32,128]{2,1,0:T(8,128)(2,1)}, u32[]{:S(2)}) copy-start(bf16[32,32,128]{2,1,0:T(8,128)(2,1)} %param.28) | copy-start | bytes 786436
  0.7 36.7 %copy-start.8 = (bf16[32,4,128]{2,1,0:T(4,128)(2,1)S(1)}, bf16[32,4,128]{2,1,0:T(4,128)(2,1)}, u32[]{:S(2)}) copy-start(bf16[32,4,128]{2,1,0:T(4,128)(2,1)} %param.25) | copy-start | bytes 98308
  2.3 9.8 %collective-permute-start = (f32[128,128]{1,0:T(8,128)S(1)}, f32[128,128]{1,0:T(8,128)S(1)}, u32[]{:S(2)}, u32[]{:S(2)}) collective-permute-start(f32[128,128]{1,0:T(8,128)S(1)} %get-tuple-element.29), channel_id=1, source_target_pairs={{0,1},{1,0},{2,3},{3,2},{4,5},{5,4},{6,7},{7,6},{8,9},{9,8},{10,11... | collective-permute-start | bytes 196616 | tf_op jit(solution)/shard_map/ppermute | solution.py:39
  12.8 8.2 %all-to-all-start = ((bf16[4,128,128]{2,1,0:T(8,128)(2,1)}), bf16[4,128,128]{2,1,0:T(8,128)(2,1)S(1)}, u32[]{:S(2)}, u32[]{:S(2)}) async-start(bf16[4,128,128]{2,1,0:T(8,128)(2,1)} %shard_map.167), calls=%async_computation | async-start | bytes 262144 | tf_op jit(solution)/shard_map/all_to_all | solution.py:35
  16.1 36.6 %collective-permute-start.2 = (bf16[1,128,1024]{2,1,0:T(8,128)(2,1)S(1)}, bf16[1,128,1024]{2,1,0:T(8,128)(2,1)S(1)}, u32[]{:S(2)}, u32[]{:S(2)}) collective-permute-start(bf16[1,128,1024]{2,1,0:T(8,128)(2,1)S(1)} %bitcast.9), channel_id=1, source_target_pairs={{0,4},{2,6},{4,0},{6,2},{1,5},{3,7},{5,1},{7,3},{8,12},{10,14},{12... | collective-permute-start | bytes 786440 | tf_op jit(solution)/shard_map/ppermute | solution.py:43
  21.0 4.9 %collective-permute-start.1 = (bf16[128,128]{1,0:T(8,128)(2,1)S(1)}, bf16[128,128]{1,0:T(8,128)(2,1)S(1)}, u32[]{:S(2)}, u32[]{:S(2)}) collective-permute-start(bf16[128,128]{1,0:T(8,128)(2,1)S(1)} %reduce_sum.21.refs_2_), channel_id=1, source_target_pairs={{0,1},{1,0},{2,3},{3,2},{4,5},{5,4},{6,7},{7,6},{8,9},{9,8},{10,11... | collective-permute-start | bytes 98312 | tf_op jit(solution)/shard_map/ppermute | solution.py:39
  25.9 49.9 %copy-start.1 = (f32[1024,64]{0,1:T(8,128)S(1)}, f32[1024,64]{0,1:T(8,128)}, u32[]{:S(2)}) copy-start(f32[1024,64]{0,1:T(8,128)} %param.17) | copy-start | bytes 786436
  26.9 17.0 %all-to-all-start.1 = ((bf16[16,40,128]{2,1,0:T(8,128)(2,1)}), bf16[16,40,128]{2,1,0:T(8,128)(2,1)S(1)}, u32[]{:S(2)}, u32[]{:S(2)}) async-start(bf16[16,40,128]{2,1,0:T(8,128)(2,1)} %shard_map.169), calls=%async_computation.1 | async-start | bytes 327680 | tf_op jit(solution)/shard_map/all_to_all | solution.py:35
  37.3 46.8 %copy-start.7 = (f32[64,128]{1,0:T(8,128)S(1)}, f32[64,128]{1,0:T(8,128)}, u32[]{:S(2)}) copy-start(f32[64,128]{1,0:T(8,128)} %b_ref.3) | copy-start | bytes 98308
  40.2 12.6 %copy-start.4 = (bf16[1024,128]{1,0:T(8,128)(2,1)}, bf16[1024,128]{1,0:T(8,128)(2,1)S(1)}, u32[]{:S(2)}) copy-start(bf16[1024,128]{1,0:T(8,128)(2,1)S(1)} %get-tuple-element.52.refs_4_) | copy-start | bytes 786436
  44.5 20.0 %all-to-all-start.2 = ((bf16[4,40,128]{2,1,0:T(8,128)(2,1)}), bf16[4,40,128]{2,1,0:T(8,128)(2,1)S(1)}, u32[]{:S(2)}, u32[]{:S(2)}) async-start(bf16[4,40,128]{2,1,0:T(8,128)(2,1)} %shard_map.171), calls=%async_computation.2 | async-start | bytes 81920 | tf_op jit(solution)/shard_map/all_to_all | solution.py:35
  52.8 21.1 %collective-permute-start.3 = (bf16[2,128,1024]{2,1,0:T(8,128)(2,1)S(1)}, bf16[2,128,1024]{2,1,0:T(8,128)(2,1)S(1)}, u32[]{:S(2)}, u32[]{:S(2)}) collective-permute-start(bf16[2,128,1024]{2,1,0:T(8,128)(2,1)S(1)} %pad_maximum_fusion.refs_0_), channel_id=1, source_target_pairs={{0,2},{2,0},{4,6},{6,4},{1,3},{3,1},{5,7},{7,5},{8,10},{10,8},{12,... | collective-permute-start | bytes 1572872 | tf_op jit(solution)/shard_map/ppermute | solution.py:43
  65.3 10.5 %all-to-all-start.3 = ((bf16[16,40,128]{2,1,0:T(8,128)(2,1)}), bf16[16,40,128]{2,1,0:T(8,128)(2,1)S(1)}, u32[]{:S(2)}, u32[]{:S(2)}) async-start(bf16[16,40,128]{2,1,0:T(8,128)(2,1)} %broadcast_in_dim.20), calls=%async_computation.3 | async-start | bytes 327680 | tf_op jit(solution)/shard_map/all_to_all | solution.py:35
  68.9 15.9 %collective-permute-start.4 = (bf16[2,128,1024]{2,1,0:T(8,128)(2,1)S(1)}, bf16[2,128,1024]{2,1,0:T(8,128)(2,1)S(1)}, u32[]{:S(2)}, u32[]{:S(2)}) collective-permute-start(bf16[2,128,1024]{2,1,0:T(8,128)(2,1)S(1)} %pad_maximum_fusion.refs_0_), channel_id=1, source_target_pairs={{0,1},{1,0},{2,3},{3,2},{4,5},{5,4},{6,7},{7,6},{8,9},{9,8},{10,11... | collective-permute-start | bytes 1572872 | tf_op jit(solution)/shard_map/ppermute | solution.py:39
  73.9 10.9 %collective-permute-start.5 = (bf16[2,128,1024]{2,1,0:T(8,128)(2,1)S(1)}, bf16[2,128,1024]{2,1,0:T(8,128)(2,1)S(1)}, u32[]{:S(2)}, u32[]{:S(2)}) collective-permute-start(bf16[2,128,1024]{2,1,0:T(8,128)(2,1)S(1)} %collective-permute-done.3.refs_1_), channel_id=1, source_target_pairs={{0,1},{1,0},{2,3},{3,2},{4,5},{5,4},{6,7},{7,6},{8,9},{9,8},{10,11... | collective-permute-start | bytes 1572872 | tf_op jit(solution)/shard_map/ppermute | solution.py:39
  76.7 13.2 %all-to-all-start.4 = ((bf16[8,64,128]{2,1,0:T(8,128)(2,1)}), bf16[8,64,128]{2,1,0:T(8,128)(2,1)S(1)}, u32[]{:S(2)}, u32[]{:S(2)}) async-start(bf16[8,64,128]{2,1,0:T(8,128)(2,1)} %shard_map.173), calls=%async_computation.4 | async-start | bytes 262144 | tf_op jit(solution)/shard_map/all_to_all | solution.py:35
  84.8 5.1 %copy-start.5 = (bf16[1024,128]{1,0:T(8,128)(2,1)S(1)}, bf16[1024,128]{1,0:T(8,128)(2,1)}, u32[]{:S(2)}) copy-start(bf16[1024,128]{1,0:T(8,128)(2,1)} %copy-done.4) | copy-start | bytes 786436
